TPU v7x, 32 devices: a whole 2x2x4 slice. The times are simulated.
32 devices in a mesh: dp: 8 (over y, x, core), seq: 4 (over z).
Axes of the slice: x: 2, y: 2, z: 4, core: 2. Of those that a mesh axis runs over, the one named last changes fastest.
Arguments:
- section_input: bfloat16 [8, 512, 768], P('dp', 'seq'), may hold values from -6 to 6
- conv_kernel: bfloat16 [5, 768, 768], P(None, None, 'seq'), may hold values from -0.09375 to 0.09375
- qkv_weight: bfloat16 [1536, 4608], P(None, 'seq'), may hold values from -0.15625 to 0.15625
- gain_in: float32 [768], replicated, may hold values from 0.1 to 1.9
- gain_mid: float32 [1536], replicated, may hold values from 0.1 to 1.9
- qkv_cotangent: bfloat16 [8, 256, 4608], P('dp', None, 'seq'), may hold values from -6 to 6
Outputs:
- qkv: bfloat16 [8, 256, 4608], P('dp', None, 'seq')
- input_grad: bfloat16 [8, 512, 768], P('dp', 'seq')
- kernel_grad: bfloat16 [5, 768, 768], P(None, None, 'seq')
- gain_in_grad: float32 [768], replicated
- gain_mid_grad: float32 [1536], replicated
- weight_grad: bfloat16 [1536, 4608], P(None, 'seq')
All inputs are finite; a program needn't handle non-finite values.
Results may differ from a plain program's by a relative error of at most 0.02.
Values may be sent and summed in bfloat16 or wider, within the bound.
No kernel may reach another device: no remote copies, remote signals or barrier semaphores. Data moves between devices by JAX's collectives and lax.ppermute only.
A program may use at most 64 MiB of HBM per device.

v0:
```python
import math

import jax
import jax.numpy as jnp
from jax import lax
from jax.sharding import PartitionSpec as P

EPS = 1e-06


def extended(cells, sides, width):
    for axis, dim in sides:
        count = lax.axis_size(axis)
        ends = count - 1
        head = lax.slice_in_dim(cells, 0, width, axis=dim)
        tail = lax.slice_in_dim(cells, cells.shape[dim] - width, cells.shape[dim], axis=dim)
        cells = jnp.concatenate(
            [
                lax.ppermute(tail, axis, [(i, (i + 1) % count) for i in range(ends)]),
                cells,
                lax.ppermute(head, axis, [((i + 1) % count, i) for i in range(ends)]),
            ],
            axis=dim,
        )
    return cells


def inverse_rms(values):
    return lax.rsqrt(jnp.mean(values * values, axis=-1, keepdims=True) + EPS)


def forward_taps(rows, kernel, length):
    total = jnp.dot(rows[0:length], kernel[0], preferred_element_type=jnp.float32)
    for k in range(1, 5):
        total = total + jnp.dot(rows[k : k + length], kernel[k], preferred_element_type=jnp.float32)
    return total


def backward_taps(total, rows, kernel, length):
    for k in range(5):
        total = total + lax.dot_general(
            rows[4 - k : 4 - k + length],
            kernel[k],
            (((1,), (1,)), ((), ())),
            preferred_element_type=jnp.float32,
        )
    return total


def body(section_input, conv_kernel, qkv_weight, gain_in, gain_mid, qkv_cotangent):
    seq_rows = section_input[0]
    length, chans = seq_rows.shape
    half = length // 2
    width = 2 * chans
    shards = lax.axis_size("seq")
    scale = 1.0 / math.sqrt(lax.axis_size("dp") * shards * half)
    xfull = seq_rows.astype(jnp.float32)
    rone = inverse_rms(xfull)
    aone = xfull * rone
    normed_in = (aone * gain_in).astype(jnp.bfloat16)
    all_in = lax.all_gather(normed_in, "seq", axis=0, tiled=True)
    total_len = all_in.shape[0]
    padded_all = jnp.pad(all_in, ((2, 2), (0, 0)))
    full_kernel = lax.all_gather(conv_kernel, "seq", axis=2, tiled=True)
    own_rows = lax.dynamic_slice_in_dim(padded_all, lax.axis_index("seq") * length, length + 4, 0)
    conv_out = forward_taps(own_rows, full_kernel, length)
    sig = jax.nn.sigmoid(conv_out)
    pooled = (xfull + conv_out * sig).reshape(half, width)
    rtwo = inverse_rms(pooled)
    atwo = pooled * rtwo
    normed_mid = (atwo * gain_mid).astype(jnp.bfloat16)
    grads_out = qkv_cotangent[0]
    all_normed = lax.all_gather(normed_mid, "seq", axis=0, tiled=True)
    qkv_out = jnp.dot(all_normed, qkv_weight, preferred_element_type=jnp.float32).astype(
        jnp.bfloat16
    )
    mid_grad = lax.psum_scatter(
        lax.dot_general(
            grads_out, qkv_weight, (((1,), (1,)), ((), ())), preferred_element_type=jnp.float32
        ).astype(jnp.bfloat16),
        "seq",
        scatter_dimension=0,
        tiled=True,
    ).astype(jnp.float32)
    proj_grad = lax.dot_general(
        all_normed, grads_out, (((0,), (0,)), ((), ())), preferred_element_type=jnp.float32
    )
    gain_mid_term = jnp.sum(mid_grad * atwo, axis=0)
    gmid = gain_mid * mid_grad
    pooled_grad = rtwo * (gmid - atwo * jnp.mean(gmid * atwo, axis=-1, keepdims=True))
    section_grad = pooled_grad.reshape(length, chans)
    conv_grad = (section_grad * sig * (1.0 + conv_out * (1.0 - sig))).astype(jnp.bfloat16)
    grad_pad = extended(conv_grad, (("seq", 0),), 2)
    empty = jnp.zeros((length, chans), jnp.float32)
    normed_grad = backward_taps(empty, grad_pad, full_kernel, length)
    grad_cols = lax.all_to_all(conv_grad, "seq", split_axis=1, concat_axis=0, tiled=True)
    kernel_term = jnp.stack(
        [
            lax.dot_general(
                padded_all[k : k + total_len],
                grad_cols,
                (((0,), (0,)), ((), ())),
                preferred_element_type=jnp.float32,
            )
            for k in range(5)
        ]
    )
    gain_in_term = jnp.sum(normed_grad * aone, axis=0)
    hin = gain_in * normed_grad
    input_grad = (
        section_grad + rone * (hin - aone * jnp.mean(hin * aone, axis=-1, keepdims=True))
    ).astype(jnp.bfloat16)
    kernel_total, proj_total = lax.psum((kernel_term, proj_grad), "dp")
    gain_in_total, gain_mid_total = lax.psum((gain_in_term, gain_mid_term), ("dp", "seq"))
    return (
        qkv_out[None],
        input_grad[None],
        (kernel_total * scale).astype(jnp.bfloat16),
        gain_in_total * scale,
        gain_mid_total * scale,
        (proj_total * scale).astype(jnp.bfloat16),
    )


def solution(mesh):
    placed = (
        P("dp", "seq", None),
        P(None, None, "seq"),
        P(None, "seq"),
        P(),
        P(),
        P("dp", None, "seq"),
    )
    return jax.shard_map(
        body,
        mesh=mesh,
        in_specs=placed,
        out_specs=(
            P("dp", None, "seq"),
            P("dp", "seq", None),
            P(None, None, "seq"),
            P(),
            P(),
            P(None, "seq"),
        ),
        check_vma=False,
    )
```

profile of v0, /device:TPU:9, one launch (start us, length us, event | category | flops | bytes accessed | tf_op | source)
XLA Modules:
  0.0 365.7 jit_solution(14119079020681952466)
XLA Ops:
  9.2 3.2 convolution_convert_fusion.1
  14.5 25.9 %all_gather.9 = bf16[512,768]{1,0:T(8,128)(2,1)} all-gather(bf16[128,768]{1,0:T(8,128)(2,1)S(1)} %fusion.28), channel_id=1, replica_groups=mesh['dp'=8,'seq'=4] {'seq'}, dimensions={0}, use_global_device_ids=true | all-gather | bytes 983040 | tf_op jit(solution)/shard_map/all_gather | solution.py:61
  40.4 87.6 %all-gather.2.cloned.1.call-done = bf16[5,768,768]{1,2,0:T(8,128)(2,1)} async-done(((bf16[5,768,192]{1,2,0:T(8,128)(2,1)}), bf16[5,768,768]{1,2,0:T(8,128)(2,1)}) %all-gather.2.cloned.1.call-update) | async-done | bytes 5898256 | tf_op jit(solution)/shard_map/all_gather | solution.py:64
  128.0 2.0 fusion.8
  130.0 2.0 convolution_add_fusion.5
  132.0 1.9 convolution_add_fusion.4
  133.9 1.8 convolution_add_fusion.3
  135.7 2.7 multiply_reduce_fusion
  139.2 1.9 reshape.50
  142.4 9.4 %reduce-scatter.2.cloned.1.call-done = bf16[64,1536]{1,0:T(8,128)(2,1)} async-done(((bf16[256,1536]{1,0:T(8,128)(2,1)}), bf16[64,1536]{1,0:T(8,128)(2,1)}) %reduce-scatter.2.cloned.1.call-update) | async-done | bytes 196624 | tf_op jit(solution)/shard_map/reduce_scatter | solution.py:77
  153.1 2.0 fusion.26
  155.2 1.8 reshape.51
  157.0 1.9 multiply_convert_fusion.2
  158.9 1.7 copy.12
  160.7 4.9 %all-to-all-start = ((bf16[128,4,192]{0,2,1:T(8,128)(2,1)}), bf16[128,4,192]{0,2,1:T(8,128)(2,1)}, u32[]{:S(2)}, u32[]{:S(2)}) async-start(bf16[128,4,192]{0,2,1:T(8,128)(2,1)} %bitcast.97), calls=%async_computation.1 | async-start | bytes 393216 | tf_op jit(solution)/shard_map/all_to_all | solution.py:96
  165.5 17.7 %all_gather.11 = bf16[256,1536]{1,0:T(8,128)(2,1)S(1)} all-gather(bf16[64,1536]{1,0:T(8,128)(2,1)} %get-tuple-element.17), channel_id=1, replica_groups=mesh['dp'=8,'seq'=4] {'seq'}, dimensions={0}, use_global_device_ids=true | all-gather | bytes 983040 | tf_op jit(solution)/shard_map/all_gather | solution.py:73
  184.1 5.2 %fusion.20 = f32[1536,1152]{1,0:T(8,128)} fusion(bf16[256,1536]{1,0:T(8,128)(2,1)S(1)} %all_gather.11, bf16[1,256,1152]{2,1,0:T(8,128)(2,1)} %param.11), kind=kOutput, calls=%fused_computation.43 | convolution fusion | flops 905969664 | bytes 8454144 | tf_op jit(solution)/shard_map/dot_general | solution.py:85
  189.3 2.5 fusion.5
  191.8 2.4 fusion.4
  194.3 2.1 fusion.3
  196.4 2.1 fusion.2
  198.5 2.1 fusion.1
  201.4 2.0 collective-permute-start
  203.4 3.4 collective-permute-start.1
  206.8 3.1 fusion
  210.0 2.0 fusion.10
  216.9 2.9 fusion.34
  219.8 43.8 %all-reduce.1 = (f32[768]{0:T(1024)}, f32[1536]{0:T(1024)}) all-reduce(f32[768]{0:T(1024)S(1)} %get-tuple-element.8, f32[1536]{0:T(1024)S(1)} %get-tuple-element.6), channel_id=1, replica_groups=mesh['dp'=8,'seq'=4] {'dp','seq'}, use_global_device_ids=true, to_apply=%region_8.9 | all-reduce | flops 2304 | bytes 18432 | tf_op jit(solution)/shard_map/psum | solution.py:114
  266.8 2.1 fusion.40
  268.9 81.6 %all-reduce.5.cloned.1.call-done = (f32[5,768,192]{1,2,0:T(8,128)}, f32[1536,1152]{1,0:T(8,128)}) async-done(((f32[5,768,192]{1,2,0:T(8,128)}, f32[1536,1152]{1,0:T(8,128)}), (f32[5,768,192]{1,2,0:T(8,128)}, f32[1536,1152]{1,0:T(8,128)})) %all-reduce.5.cloned.1.call-update) | async-done | bytes 10027024 | tf_op jit(solution)/shard_map/psum | solution.py:113
  350.5 3.2 multiply_convert_fusion.1
  353.7 5.5 %multiply_convert_fusion = bf16[1536,1152]{1,0:T(8,128)(2,1)} fusion(f32[1536,1152]{1,0:T(8,128)} %get-tuple-element.13), kind=kLoop, calls=%fused_computation | loop fusion | flops 3538944 | bytes 10616832 | tf_op jit(solution)/shard_map/convert_element_type | solution.py:121
  (48 shorter events, 17.3 us)
Async XLA Ops:
  7.2 2.0 copy-start
  7.2 120.8 %all-gather.2.cloned.1.call-start = ((), (), s32[]{:S(2)}) async-start(), calls=%async_computation.2 | async-start | bytes 7372800 | tf_op jit(solution)/shard_map/all_gather | solution.py:64
  7.9 5.5 %copy-start.8 = (f32[768]{0:T(1024)S(1)}, f32[768]{0:T(1024)}, u32[]{:S(2)}) copy-start(f32[768]{0:T(1024)} %param.9) | copy-start | bytes 9220
  7.9 143.9 %reduce-scatter.2.cloned.1.call-start = ((), (), s32[]{:S(2)}) async-start(), calls=%async_computation.3 | async-start | bytes 983040 | tf_op jit(solution)/shard_map/reduce_scatter | solution.py:77
  13.4 1.1 copy-start.10
  128.0 4.0 %copy-start.1 = (bf16[512,768]{1,0:T(8,128)(2,1)S(1)}, bf16[512,768]{1,0:T(8,128)(2,1)}, u32[]{:S(2)}) copy-start(bf16[512,768]{1,0:T(8,128)(2,1)} %all_gather.9) | copy-start | bytes 2359300
  132.0 3.7 %copy-start.5 = (bf16[1,128,768]{2,1,0:T(8,128)(2,1)S(1)}, bf16[1,128,768]{2,1,0:T(8,128)(2,1)}, u32[]{:S(2)}) copy-start(bf16[1,128,768]{2,1,0:T(8,128)(2,1)} %param.6) | copy-start | bytes 589828
  135.7 16.1 %copy-start.7 = (f32[1536]{0:T(1024)S(1)}, f32[1536]{0:T(1024)}, u32[]{:S(2)}) copy-start(f32[1536]{0:T(1024)} %param.10) | copy-start | bytes 18436
  160.7 28.7 %all-to-all-start = ((bf16[128,4,192]{0,2,1:T(8,128)(2,1)}), bf16[128,4,192]{0,2,1:T(8,128)(2,1)}, u32[]{:S(2)}, u32[]{:S(2)}) async-start(bf16[128,4,192]{0,2,1:T(8,128)(2,1)} %bitcast.97), calls=%async_computation.1 | async-start | bytes 393216 | tf_op jit(solution)/shard_map/all_to_all | solution.py:96
  165.5 184.9 %all-reduce.5.cloned.1.call-start = ((), (), s32[]{:S(2)}) async-start(), calls=%async_computation.4 | async-start | bytes 20054016 | tf_op jit(solution)/shard_map/psum | solution.py:113
  183.2 0.9 copy-start.3
  189.3 5.0 %copy-start.2 = (bf16[512,768]{1,0:T(8,128)(2,1)S(1)}, bf16[512,768]{1,0:T(8,128)(2,1)}, u32[]{:S(2)}) copy-start(bf16[512,768]{1,0:T(8,128)(2,1)} %all_gather.9) | copy-start | bytes 2359300
  201.4 12.3 %collective-permute-start = (bf16[2,768]{1,0:T(2,128)(2,1)S(1)}, bf16[2,768]{1,0:T(2,128)(2,1)S(1)}, u32[]{:S(2)}, u32[]{:S(2)}) collective-permute-start(bf16[2,768]{1,0:T(2,128)(2,1)S(1)} %get-tuple-element.18), channel_id=1, source_target_pairs={{1,0},{2,1},{3,2},{5,4},{6,5},{7,6},{9,8},{10,9},{11,10},{13,12},{... | collective-permute-start | bytes 9224 | tf_op jit(solution)/shard_map/ppermute | solution.py:21
  203.4 6.6 %copy-start.4 = (bf16[128,768]{1,0:T(8,128)(2,1)S(1)}, bf16[128,768]{1,0:T(8,128)(2,1)}, u32[]{:S(2)}) copy-start(bf16[128,768]{1,0:T(8,128)(2,1)} %multiply_convert_fusion.2) | copy-start | bytes 589828
  203.4 8.5 %collective-permute-start.1 = (bf16[2,768]{1,0:T(2,128)(2,1)S(1)}, bf16[2,768]{1,0:T(2,128)(2,1)S(1)}, u32[]{:S(2)}, u32[]{:S(2)}) collective-permute-start(bf16[2,768]{1,0:T(2,128)(2,1)S(1)} %get-tuple-element.19), channel_id=1, source_target_pairs={{0,1},{1,2},{2,3},{4,5},{5,6},{6,7},{8,9},{9,10},{10,11},{12,13},{... | collective-permute-start | bytes 9224 | tf_op jit(solution)/shard_map/ppermute | solution.py:19
  211.9 4.9 %copy-start.6 = (bf16[1,128,768]{2,1,0:T(8,128)(2,1)S(1)}, bf16[1,128,768]{2,1,0:T(8,128)(2,1)}, u32[]{:S(2)}) copy-start(bf16[1,128,768]{2,1,0:T(8,128)(2,1)} %param.6) | copy-start | bytes 589828
  211.9 4.9 %copy-start.9 = (f32[768]{0:T(1024)S(1)}, f32[768]{0:T(1024)}, u32[]{:S(2)}) copy-start(f32[768]{0:T(1024)} %param.9) | copy-start | bytes 9220
  211.9 4.9 %copy-start.11 = (f32[128]{0:T(128)S(1)}, f32[128]{0:T(128)}, u32[]{:S(2)}) copy-start(f32[128]{0:T(128)} %copy-done.10) | copy-start | bytes 1540
Sparse Core Ops, SparseCore 0:
  9.6 118.3 all-gather.1
  130.9 20.8 reduce-scatter.1
  200.8 149.6 all-reduce.4
where the time goes:
time: 369 us; the launch traced here: 366 us
  waiting for transfers between devices  179 us (49%)
  blocking collectives  87.4 us (24%)
  matrix products  42.8 us (12%)
  other arithmetic  22.8 us (6%)
  between operations  14 us (4%)
  starting transfers between devices  10.4 us (3%)
  local copies, waits for them, and re-layouts  9.06 us (2%)
    all_gather x1, waiting for transfers between devices, body(): full_kernel = lax.all_gather(conv_kernel, 'seq', axis=2, tiled=True)  87.6 us
    psum x1, waiting for transfers between devices, body(): kernel_total, proj_total = lax.psum((kernel_term, proj_grad), 'dp')  81.6 us
    psum x1, blocking collectives, body(): lax.psum((gain_in_term, gain_mid_term), ('dp', 'seq'))  43.8 us
    all_gather x1, blocking collectives, body(): all_in = lax.all_gather(normed_in, 'seq', axis=0, tiled=True)  25.9 us
    all_gather x1, blocking collectives, body(): all_normed = lax.all_gather(normed_mid, 'seq', axis=0, tiled=True)  17.7 us
    dot_general x5, matrix products, body(): lax.dot_general(padded_all[k:k + total_len], grad_cols, (((0,), (0,)), ((...  11.3 us
    dot_general x5, matrix products, backward_taps(): lax.dot_general(rows[4 - k:4 - k + length], kernel[k], (((1,), (1,)), (()...  9.7 us
    reduce_scatter x1, waiting for transfers between devices, body(): lax.psum_scatter(lax.dot_general(grads_out, qkv_weight, (((1,), (1,)), ((...  9.38 us
  transfers between devices with their start and end apart: 6, of which 3 were waited for; matrix products, arithmetic and copies ran while one was open for 12% of the time, Pallas kernels for 0%

commit v1 on v0

v1 whole, which is shorter than its diff:
```python
import functools
import math

import jax
import jax.numpy as jnp
from jax import lax
from jax.experimental import pallas as pl
from jax.experimental.pallas import tpu as pltpu
from jax.sharding import PartitionSpec as P

EPS = 1e-06
F32 = jnp.float32
BF16 = jnp.bfloat16
VMEM = pl.BlockSpec(memory_space=pltpu.VMEM)
SMEM = pl.BlockSpec(memory_space=pltpu.SMEM)


def call(kernel, outs, args, scratch=(), flops=0, name=None):
    specs = [SMEM if a.dtype == jnp.int32 else VMEM for a in args]
    size = lambda a: a.size * a.dtype.itemsize
    moved = sum(map(size, args)) + sum(map(size, outs))
    return pl.pallas_call(
        kernel,
        out_shape=tuple(outs),
        in_specs=specs,
        out_specs=tuple(VMEM for _ in outs),
        scratch_shapes=list(scratch),
        compiler_params=pltpu.CompilerParams(vmem_limit_bytes=56 << 20),
        cost_estimate=pl.CostEstimate(flops=flops, bytes_accessed=moved, transcendentals=0),
        name=name,
    )(*args)


def shaped(shape, dtype):
    return jax.ShapeDtypeStruct(shape, dtype)


def dot(a, b):
    return jnp.dot(a, b, preferred_element_type=F32)


def dot_nt(a, b):
    return lax.dot_general(a, b, (((1,), (1,)), ((), ())), preferred_element_type=F32)


def dot_tn(a, b):
    return lax.dot_general(a, b, (((0,), (0,)), ((), ())), preferred_element_type=F32)


def later(v):
    row = lax.broadcasted_iota(jnp.int32, v.shape, 0)
    return jnp.where(row == 0, 0.0, pltpu.roll(v, 1, 0))


def sooner(v):
    rows = v.shape[0]
    row = lax.broadcasted_iota(jnp.int32, v.shape, 0)
    return jnp.where(row == rows - 1, 0.0, pltpu.roll(v, rows - 1, 0))


def inv_rms(v):
    return lax.rsqrt(jnp.mean(v * v, axis=-1, keepdims=True) + EPS)


def mid_kernel(n, c, chans, cot, w, out):
    g = cot[...]
    for b in range(n):
        cols = jnp.concatenate(
            [w[b * c : (b + 1) * c, :], w[chans + b * c : chans + (b + 1) * c, :]], axis=0
        )
        out[b] = dot_nt(g, cols).astype(BF16)


def conv_kernel_fwd(n, c, chans, *refs):
    me = refs[0][0]
    blocks = refs[1 : 1 + n]
    taps, gain, pooled_msg, pooled, conv_out, nin, xs = refs[1 + n :]
    rows = blocks[0].shape[0]
    gains = gain[...]
    for k in range(n):
        at = pl.multiple_of(lax.rem(me - k + n, n) * rows, rows)
        v = blocks[k][...]
        xs[pl.ds(at, rows), :] = v
        for h in range(2):
            f = v[:, h * chans : (h + 1) * chans].astype(F32)
            nin[pl.ds(at, rows), h * chans : (h + 1) * chans] = (f * inv_rms(f) * gains).astype(BF16)
    xe, xo = nin[:, :chans], nin[:, chans:]
    k0, k1, k2, k3, k4 = (taps[k] for k in range(5))
    even = dot(xe, k2) + dot(xo, k3) + later(dot(xe, k0) + dot(xo, k1)) + sooner(dot(xe, k4))
    odd = dot(xe, k1) + dot(xo, k2) + later(dot(xo, k0)) + sooner(dot(xe, k3) + dot(xo, k4))
    conv = jnp.concatenate([even, odd], axis=1)
    row = lax.broadcasted_iota(jnp.int32, (chans, c), 0)
    col = lax.broadcasted_iota(jnp.int32, (chans, c), 1)
    pick = jnp.where(row == col + me * c, 1.0, 0.0).astype(BF16)
    own = jnp.concatenate([dot(xs[:, :chans], pick), dot(xs[:, chans:], pick)], axis=1)
    total = own + conv * jax.nn.sigmoid(conv)
    conv_out[...] = conv
    pooled[...] = total
    pooled_msg[...] = total.astype(BF16)


def norm_kernel(n, c, chans, *refs):
    me = refs[0][0]
    blocks = refs[1 : 1 + n]
    gains, nmt, rtwo = refs[1 + n :]
    squares = 0.0
    for k in range(n):
        v = blocks[k][...].astype(F32)
        squares = squares + jnp.sum(v * v, axis=1, keepdims=True)
    r = lax.rsqrt(squares * (1.0 / (2 * chans)) + EPS)
    rtwo[...] = r
    for k in range(n):
        b = lax.rem(me - k + n, n)
        v = blocks[k][...].astype(F32) * r * gains[pl.ds(b, 1), :]
        t = v.T.astype(BF16)
        for h in range(2):
            at = pl.multiple_of(h * chans + b * c, c & -c)
            nmt[pl.ds(at, c), :] = t[h * c : (h + 1) * c, :]


def qkv_kernel(nmt, w, cot, qkv, part):
    q = dot_tn(nmt[...], w[...])
    qkv[...] = q.astype(BF16)
    row = jnp.sum(q * cot[...].astype(F32), axis=1, keepdims=True)
    part[...] = jnp.broadcast_to(row, (row.shape[0], 128)).T[:8, :]


def weight_kernel(m, scale, *refs):
    me = refs[0][0]
    nms = refs[1]
    cots = refs[2 : 2 + m]
    out = refs[2 + m]
    total = dot(nms[me], cots[0][...])
    for k in range(1, m):
        total = total + dot(nms[me ^ k], cots[k][...])
    out[...] = (total * scale).astype(BF16)


def back_kernel(n, c, chans, m, *refs):
    seq_at, dp_at = refs[0][0], refs[0][1]
    parts = refs[1 : 1 + n]
    (mids, pooled, rtwo, conv_out, gmid, gin, nin, taps, keep, send, msg, sums, kg) = refs[1 + n :]
    width = 2 * chans
    mid = mids[0].astype(F32)
    for b in range(1, n):
        mid = mid + mids[b].astype(F32)
    r = rtwo[...]
    atwo = pooled[...] * r
    rowsum = parts[0][...]
    for k in range(1, n):
        rowsum = rowsum + parts[k][...]
    half = atwo.shape[0]
    mean = jnp.concatenate([rowsum] * 16, axis=0).T[:, :1] * (1.0 / width)
    mid_sum = jnp.sum(mid * atwo, axis=0, keepdims=True)
    section = r * (gmid[pl.ds(seq_at, 1), :] * mid - atwo * mean)
    conv = conv_out[...]
    sig = jax.nn.sigmoid(conv)
    cg = section * sig * (1.0 + conv * (1.0 - sig))
    cg = cg.astype(BF16).astype(F32)
    ge, go = cg[:, :c], cg[:, c:]
    bf = lambda v: v.astype(BF16)
    g0, gp, gm = bf(ge), bf(sooner(ge)), bf(later(ge))
    o0, op, om = bf(go), bf(sooner(go)), bf(later(go))
    es, os_ = (gp, o0, g0, om, gm), (op, gp, o0, g0, om)
    xe, xo = nin[:, :chans], nin[:, chans:]
    kg[...] = dot_tn(xe, jnp.concatenate(es, axis=1)) + dot_tn(xo, jnp.concatenate(os_, axis=1))
    rows = chans // m
    core = lax.rem(dp_at, 2)
    for q in range(m // 2):
        keep[q] = kg[pl.ds(pl.multiple_of((2 * q + core) * rows, rows & -rows), rows), :]
        send[q] = kg[pl.ds(pl.multiple_of((2 * q + 1 - core) * rows, rows & -rows), rows), :].astype(BF16)
    gains = gin[...]
    acc = 0.0
    block = half // n
    for h, terms in ((0, es), (1, os_)):
        ng = dot_nt(terms[0], taps[0])
        for k in range(1, 5):
            ng = ng + dot_nt(terms[k], taps[k])
        acc = acc + jnp.sum(ng * (nin[:, h * chans : (h + 1) * chans].astype(F32)), axis=0, keepdims=True)
        for b in range(n):
            msg[b, :, h * chans : (h + 1) * chans] = ng[b * block : (b + 1) * block, :].astype(BF16)
    line = lax.broadcasted_iota(jnp.int32, sums.shape, 0)
    wide = jnp.concatenate([mid_sum, jnp.zeros((1, chans - 2 * c), F32)], axis=1)
    sums[...] = jnp.where(line == 0, acc / gains, jnp.where(line == 1 + seq_at, wide, 0.0))
    for b in range(n):
        msg[b, :, width:] = section[b * block : (b + 1) * block, :].astype(BF16)


def split_kernel(q, at, keep, recv, *outs):
    me = at[1] // 2
    for k in range(q):
        v = keep[me ^ k] + recv[me ^ k].astype(F32)
        outs[k][...] = v.astype(outs[k].dtype)


def finish_kernel(scale, *refs):
    total = refs[0][...]
    for r in refs[1:-1]:
        total = total + r[...].astype(F32)
    refs[-1][...] = (total * scale).astype(BF16)


def place_taps_kernel(m, c, *refs):
    me = refs[0][1]
    shares = refs[1 : 1 + m]
    out = refs[1 + m]
    rows = shares[0].shape[0]
    for k in range(m):
        at = pl.multiple_of((me ^ k) * rows, rows & -rows)
        v = shares[k][...]
        for t in range(5):
            out[t, pl.ds(at, rows), :] = v[:, t * c : (t + 1) * c].astype(out.dtype)


def place_rows_kernel(m, *refs):
    me = refs[0][1]
    shares = refs[1 : 1 + m]
    out = refs[1 + m]
    rows = shares[0].shape[0]
    for k in range(m):
        at = pl.multiple_of((me ^ k) * rows, rows & -rows)
        out[pl.ds(at, rows), :] = shares[k][...]


def input_kernel(n, c, chans, got, own, gin, out):
    total = got[0, :, : 2 * chans].astype(F32)
    for b in range(1, n):
        total = total + got[b, :, : 2 * chans].astype(F32)
    gains = gin[...]
    for h in range(2):
        x = own[:, h * chans : (h + 1) * chans].astype(F32)
        r = inv_rms(x)
        a = x * r
        g = gains * total[:, h * chans : (h + 1) * chans]
        sect = jnp.concatenate(
            [got[b, :, 2 * chans + h * c : 2 * chans + (h + 1) * c] for b in range(n)], axis=1
        ).astype(F32)
        v = sect + r * (g - a * jnp.mean(g * a, axis=-1, keepdims=True))
        out[:, h * chans : (h + 1) * chans] = v.astype(BF16)


def body(section_input, conv_kernel, qkv_weight, gain_in, gain_mid, qkv_cotangent):
    x = section_input[0]
    cot = qkv_cotangent[0]
    length, chans = x.shape
    c = conv_kernel.shape[2]
    width, cols = qkv_weight.shape
    n, m = lax.axis_size("seq"), lax.axis_size("dp")
    half = length // 2 * n
    scale = 1.0 / math.sqrt(m * half)
    seq_at, dp_at = lax.axis_index("seq"), lax.axis_index("dp")
    at = jnp.stack([seq_at, dp_at]).astype(jnp.int32)
    from_ring = lambda v: [v] + [
        lax.ppermute(v, "seq", [(i, (i + k) % n) for i in range(n)]) for k in range(1, n)
    ]
    across = lambda v, k: lax.ppermute(v, "dp", [(i, i ^ k) for i in range(m)])

    def to_all(v):
        firsts = [v] + [across(v, k) for k in range(2, m, 2)]
        both = []
        for f in firsts:
            both += [f, across(f, 1)]
        return both

    own = x.reshape(length // 2, 2 * chans)
    xs = from_ring(own)
    gin = gain_in.reshape(1, chans)
    gmid = gain_mid.reshape(2, n, c).transpose(1, 0, 2).reshape(n, 2 * c)
    cots = to_all(cot)
    (mid_msg,) = call(
        functools.partial(mid_kernel, n, c, chans),
        [shaped((n, half, 2 * c), BF16)],
        [cot, qkv_weight],
        flops=2 * half * width * cols,
        name="mid_parts",
    )
    pooled_msg, pooled, conv_out, nin = call(
        functools.partial(conv_kernel_fwd, n, c, chans),
        [
            shaped((half, 2 * c), BF16),
            shaped((half, 2 * c), F32),
            shaped((half, 2 * c), F32),
            shaped((half, width), BF16),
        ],
        [at, *xs, conv_kernel, gin],
        scratch=[pltpu.VMEM((half, width), BF16)],
        flops=20 * half * chans * c,
        name="conv_forward",
    )
    blocks = from_ring(pooled_msg)
    nmt, rtwo = call(
        functools.partial(norm_kernel, n, c, chans),
        [shaped((width, half), BF16), shaped((half, 1), F32)],
        [at, *blocks, gmid],
        name="norm_mid",
    )
    mids = lax.all_to_all(mid_msg, "seq", 0, 0, tiled=True)
    nms = lax.all_to_all(nmt.reshape(m, width // m, half), "dp", 0, 0, tiled=True)
    qkv, part = call(
        qkv_kernel,
        [shaped((half, cols), BF16), shaped((8, half), F32)],
        [nmt, qkv_weight, cot],
        flops=2 * half * width * cols,
        name="qkv",
    )
    parts = from_ring(part)
    (wshare,) = call(
        functools.partial(weight_kernel, m, scale),
        [shaped((width // m, cols), BF16)],
        [at[1:], nms, *cots],
        flops=2 * half * width * cols,
        name="weight_share",
    )
    wshares = to_all(wshare)
    rows = chans // m
    keep, send, msg, sums = call(
        functools.partial(back_kernel, n, c, chans, m),
        [
            shaped((m // 2, rows, 5 * c), F32),
            shaped((m // 2, rows, 5 * c), BF16),
            shaped((n, half // n, width + 2 * c), BF16),
            shaped((-(-(1 + n) // 8) * 8, chans), F32),
        ],
        [at, *parts, mids, pooled, rtwo, conv_out, gmid, gin, nin, conv_kernel],
        scratch=[pltpu.VMEM((chans, 5 * c), F32)],
        flops=40 * half * chans * c,
        name="conv_backward",
    )
    got = lax.all_to_all(msg, "seq", 0, 0, tiled=True)
    split = call(
        functools.partial(split_kernel, m // 2),
        [shaped((rows, 5 * c), F32)] + [shaped((rows, 5 * c), BF16)] * (m // 2 - 1),
        [at, keep, across(send, 1)],
        name="core_sum",
    )
    (kshare,) = call(
        functools.partial(finish_kernel, scale),
        [shaped((rows, 5 * c), BF16)],
        [split[0]] + [across(split[k], 2 * k) for k in range(1, m // 2)],
        name="chip_sum",
    )
    kshares = to_all(kshare)
    k = 1
    while k < m:
        sums = sums + across(sums, k)
        k *= 2
    totals = from_ring(sums)
    total = totals[0]
    for v in totals[1:]:
        total = total + v
    total = total * scale
    (input_grad,) = call(
        functools.partial(input_kernel, n, c, chans),
        [shaped((length // 2, 2 * chans), BF16)],
        [got, own, gin],
        name="input_grad",
    )
    (kernel_grad,) = call(
        functools.partial(place_taps_kernel, m, c),
        [shaped((5, chans, c), BF16 if rows % 16 == 0 else F32)],
        [at, *kshares],
        name="place_kernel_grad",
    )
    (weight_grad,) = call(
        functools.partial(place_rows_kernel, m),
        [shaped((width, cols), BF16)],
        [at, *wshares],
        name="place_weight_grad",
    )
    gain_mid_grad = total[1 : 1 + n, : 2 * c].reshape(n, 2, c).transpose(1, 0, 2).reshape(width)
    return (
        qkv[None],
        input_grad.reshape(1, length, chans),
        kernel_grad.astype(BF16),
        total[0],
        gain_mid_grad,
        weight_grad,
    )


def solution(mesh):
    placed = (
        P("dp", "seq", None),
        P(None, None, "seq"),
        P(None, "seq"),
        P(),
        P(),
        P("dp", None, "seq"),
    )
    return jax.shard_map(
        body,
        mesh=mesh,
        in_specs=placed,
        out_specs=(
            P("dp", None, "seq"),
            P("dp", "seq", None),
            P(None, None, "seq"),
            P(),
            P(),
            P(None, "seq"),
        ),
        check_vma=False,
    )
```

time: 369 us -> 202 us (0.55)
  waiting for transfers between devices: 179 us -> 71.3 us
  blocking collectives: 87.4 us -> 0 us
  starting transfers between devices: 10.4 us -> 69.8 us
  matrix products: 42.8 us -> 0 us
  Pallas kernels: 0 us -> 41.8 us
  other arithmetic: 22.8 us -> 0.67 us
  between operations: 14 us -> 0.83 us
  local copies, waits for them, and re-layouts: 9.06 us -> 14.5 us
    all_gather x1 -> x0, waiting for transfers between devices: 87.6 us -> none  [body(): full_kernel = lax.all_gather(conv_kernel, 'seq', axis=2, tiled=True)]
    psum x1 -> x0, waiting for transfers between devices: 81.6 us -> none  [body(): kernel_total, proj_total = lax.psum((kernel_term, proj_grad), 'dp')]
    ppermute x2 -> x40, waiting for transfers between devices: 0.01 us -> 71.3 us  [the longest x12 43.9 us: body(): lax.ppermute(v, 'seq', [(i, (i + k) % n) for i in range(n)])]
    ppermute x2 -> x40, starting transfers between devices: 5.41 us -> 51.1 us  [the longest x28 37 us: body(): across = lambda v, k: lax.ppermute(v, 'dp', [(i, i ^ k) for i in range(m)])]
    psum x1 -> x0, blocking collectives: 43.8 us -> none  [body(): lax.psum((gain_in_term, gain_mid_term), ('dp', 'seq'))]
    all_gather x2 -> x0, blocking collectives: 43.6 us -> none  [the longest x1 25.9 us: body(): all_in = lax.all_gather(normed_in, 'seq', axis=0, tiled=True)]
    dot_general x18 -> x0, matrix products: 42.8 us -> none  [the longest x5 11.3 us: body(): lax.dot_general(padded_all[k:k + total_len], grad_cols, (((0,), (0,)), ((...]
    pallas_call x0 -> x11, Pallas kernels: none -> 41.8 us  [call(): pl.pallas_call(kernel, out_shape=tuple(outs), in_specs=specs, out_specs=t...]
  transfers between devices with their start and end apart: 6 -> 43, of which waited for: 3 -> 14; matrix products, arithmetic and copies ran while one was open for 12% -> 5% of each run, Pallas kernels for 0% -> 17%
where the time goes in v1:
time: 202 us; the launch traced here: 199 us
  waiting for transfers between devices  71.3 us (35%)
  starting transfers between devices  69.8 us (35%)
  Pallas kernels  41.8 us (21%)
  local copies, waits for them, and re-layouts  14.5 us (7%)
    ppermute x12, waiting for transfers between devices, body(): lax.ppermute(v, 'seq', [(i, (i + k) % n) for i in range(n)])  43.9 us
    pallas_call x11, Pallas kernels, call(): pl.pallas_call(kernel, out_shape=tuple(outs), in_specs=specs, out_specs=t...  41.8 us
    ppermute x28, starting transfers between devices, body(): across = lambda v, k: lax.ppermute(v, 'dp', [(i, i ^ k) for i in range(m)])  37 us
    ppermute x28, waiting for transfers between devices, body(): across = lambda v, k: lax.ppermute(v, 'dp', [(i, i ^ k) for i in range(m)])  27.4 us
    ppermute x12, starting transfers between devices, body(): lax.ppermute(v, 'seq', [(i, (i + k) % n) for i in range(n)])  14.1 us
    unnamed x64, local copies, waits for them, and re-layouts  10 us
    all_to_all x1, starting transfers between devices, body(): lax.all_to_all(nmt.reshape(m, width // m, half), 'dp', 0, 0, tiled=True)  8.44 us
    all_to_all x1, starting transfers between devices, body(): got = lax.all_to_all(msg, 'seq', 0, 0, tiled=True)  5.42 us
  transfers between devices with their start and end apart: 43, of which 14 were waited for; matrix products, arithmetic and copies ran while one was open for 5% of the time, Pallas kernels for 17%

profile of v1, /device:TPU:9, one launch (start us, length us, event | category | flops | bytes accessed | tf_op | source)
XLA Modules:
  0.0 199.0 jit_solution(3494140804405619563)
XLA Ops:
  0.7 4.8 %mid_parts.1 = bf16[4,256,384]{2,1,0:T(8,128)(2,1)} custom-call(bf16[256,1152]{1,0:T(8,128)(2,1)} %bitcast.9, bf16[1536,1152]{1,0:T(8,128)(2,1)} %w.3), custom_call_target="tpu_custom_call" | custom-call | flops 905969664 | bytes 4915200 | tf_op jit(solution)/shard_map/mid_parts/pallas_call | solution.py:22
  5.4 4.9 %all-to-all-start = ((bf16[4,256,384]{2,1,0:T(8,128)(2,1)}), bf16[4,256,384]{2,1,0:T(8,128)(2,1)S(1)}, u32[]{:S(2)}, u32[]{:S(2)}) async-start(bf16[4,256,384]{2,1,0:T(8,128)(2,1)} %mid_parts.1), calls=%async_computation | async-start | bytes 1572864 | tf_op jit(solution)/shard_map/all_to_all | solution.py:297
  16.4 2.2 %copy.15.refs_5_.refs_12_ = bf16[5,768,192]{2,1,0:T(8,128)(2,1)} copy(bf16[5,768,192]{1,2,0:T(8,128)(2,1)S(1)} %copy-done.4) | data formatting | bytes 2949120 | tf_op args[1]
  19.9 19.1 %collective-permute-done.refs_2_ = bf16[64,1536]{1,0:T(8,128)(2,1)S(1)} collective-permute-done((bf16[64,1536]{1,0:T(8,128)(2,1)S(1)}, bf16[64,1536]{1,0:T(8,128)(2,1)S(1)}, u32[]{:S(2)}, u32[]{:S(2)}) %collective-permute-start) | collective-permute-done | bytes 196640 | tf_op jit(solution)/shard_map/ppermute | solution.py:254
  39.0 2.2 %collective-permute-start.31 = (bf16[256,1152]{1,0:T(8,128)(2,1)S(1)}, bf16[256,1152]{1,0:T(8,128)(2,1)}, u32[]{:S(2)}, u32[]{:S(2)}) collective-permute-start(bf16[256,1152]{1,0:T(8,128)(2,1)S(1)} %bitcast.14), channel_id=1, source_target_pairs={{0,24},{4,28},{8,16},{12,20},{16,8},{20,12},{24,0},{28,4},{1,25},{... | collective-permute-start | bytes 1769480 | tf_op jit(solution)/shard_map/ppermute | solution.py:256
  43.3 2.4 %collective-permute-done.2.refs_4_ = bf16[64,1536]{1,0:T(8,128)(2,1)} collective-permute-done((bf16[64,1536]{1,0:T(8,128)(2,1)S(1)}, bf16[64,1536]{1,0:T(8,128)(2,1)}, u32[]{:S(2)}, u32[]{:S(2)}) %collective-permute-start.2) | collective-permute-done | bytes 196640 | tf_op jit(solution)/shard_map/ppermute | solution.py:254
  45.7 4.7 %conv_forward.1 = (bf16[256,384]{1,0:T(8,128)(2,1)}, f32[256,384]{1,0:T(8,128)}, f32[256,384]{1,0:T(8,128)}, bf16[256,1536]{1,0:T(8,128)(2,1)}) custom-call(s32[2]{0:T(128)} %pad_add_fusion.refs_0_.at, bf16[64,1536]{1,0:T(8,128)(2,1)} %copy-done.6, bf16[64,1536]{1,0:T(8,128)(2,1)} %copy-done.26, bf16[64,1536]{1,0:T(8,128)(2,1)} %copy-done.27, ...), custom_call_target="tpu_custom_call" | custom-call | flops 754974720 | bytes 4033544 | tf_op jit(solution)/shard_map/conv_forward/pallas_call | solution.py:22
  51.8 3.8 %collective-permute-done.3.refs_2_ = bf16[256,384]{1,0:T(8,128)(2,1)S(1)} collective-permute-done((bf16[256,384]{1,0:T(8,128)(2,1)}, bf16[256,384]{1,0:T(8,128)(2,1)S(1)}, u32[]{:S(2)}, u32[]{:S(2)}) %collective-permute-start.3) | collective-permute-done | bytes 196640 | tf_op jit(solution)/shard_map/ppermute | solution.py:254
  57.0 8.4 %collective-permute-done.4.refs_3_ = bf16[256,384]{1,0:T(8,128)(2,1)S(1)} collective-permute-done((bf16[256,384]{1,0:T(8,128)(2,1)}, bf16[256,384]{1,0:T(8,128)(2,1)S(1)}, u32[]{:S(2)}, u32[]{:S(2)}) %collective-permute-start.4) | collective-permute-done | bytes 196640 | tf_op jit(solution)/shard_map/ppermute | solution.py:254
  65.4 2.2 %collective-permute-done.5.refs_4_ = bf16[256,384]{1,0:T(8,128)(2,1)S(1)} collective-permute-done((bf16[256,384]{1,0:T(8,128)(2,1)}, bf16[256,384]{1,0:T(8,128)(2,1)S(1)}, u32[]{:S(2)}, u32[]{:S(2)}) %collective-permute-start.5) | collective-permute-done | bytes 196640 | tf_op jit(solution)/shard_map/ppermute | solution.py:254
  68.3 2.6 %norm_mid.1 = (bf16[1536,256]{1,0:T(8,128)(2,1)}, f32[256,1]{1,0:T(8,128)}) custom-call(s32[2]{0:T(128)} %pad_add_fusion.refs_0_.at, bf16[256,384]{1,0:T(8,128)(2,1)} %get-tuple-element.22.refs_1_, bf16[256,384]{1,0:T(8,128)(2,1)} %copy-done.19, bf16[256,384]{1,0:T(8,128)(2,1)} %copy-done.20, bf16[256,384]{1,0:T(8,128)(2,1)} %copy-done.21, ...), custom_call_target="tpu_custom_call" | custom-call | bytes 1580040 | tf_op jit(solution)/shard_map/norm_mid/pallas_call | solution.py:22
  71.0 8.4 %all-to-all-start.2 = ((bf16[8,192,256]{2,1,0:T(8,128)(2,1)}), bf16[8,192,256]{2,1,0:T(8,128)(2,1)S(1)}, u32[]{:S(2)}, u32[]{:S(2)}) async-start(bf16[8,192,256]{2,1,0:T(8,128)(2,1)} %bitcast.16), calls=%async_computation.2 | async-start | bytes 1572864 | tf_op jit(solution)/shard_map/all_to_all | solution.py:298
  80.4 4.4 %qkv.1 = (bf16[256,1152]{1,0:T(8,128)(2,1)}, f32[8,256]{1,0:T(8,128)}) custom-call(bf16[1536,256]{1,0:T(8,128)(2,1)} %get-tuple-element.23.nmt, bf16[1536,1152]{1,0:T(8,128)(2,1)} %w.3, bf16[256,1152]{1,0:T(8,128)(2,1)} %bitcast.10), custom_call_target="tpu_custom_call" | custom-call | flops 905969664 | bytes 5513216 | tf_op jit(solution)/shard_map/qkv/pallas_call | solution.py:22
  89.3 2.3 %collective-permute-done.7.refs_3_ = f32[8,256]{1,0:T(8,128)S(1)} collective-permute-done((f32[8,256]{1,0:T(8,128)}, f32[8,256]{1,0:T(8,128)S(1)}, u32[]{:S(2)}, u32[]{:S(2)}) %collective-permute-start.7) | collective-permute-done | bytes 8224 | tf_op jit(solution)/shard_map/ppermute | solution.py:254
  92.3 2.3 %collective-permute-done.8.refs_4_ = f32[8,256]{1,0:T(8,128)S(1)} collective-permute-done((f32[8,256]{1,0:T(8,128)}, f32[8,256]{1,0:T(8,128)S(1)}, u32[]{:S(2)}, u32[]{:S(2)}) %collective-permute-start.8) | collective-permute-done | bytes 8224 | tf_op jit(solution)/shard_map/ppermute | solution.py:254
  95.2 6.8 %conv_backward.1 = (f32[4,96,960]{2,1,0:T(8,128)}, bf16[4,96,960]{2,1,0:T(8,128)(2,1)}, bf16[4,64,1920]{2,1,0:T(8,128)(2,1)}, f32[8,768]{1,0:T(8,128)}) custom-call(s32[2]{0:T(128)} %pad_add_fusion.refs_0_.at, f32[8,256]{1,0:T(8,128)} %get-tuple-element.25.refs_1_, f32[8,256]{1,0:T(8,128)} %copy-done.28, f32[8,256]{1,0:T(8,128)} %copy-done.29, ...), custom_call_target="tpu_custom_call" | custom-call | flops 1509949440 | bytes 7096328 | tf_op jit(solution)/shard_map/conv_backward/pallas_call | solution.py:22
  102.0 2.9 %collective-permute-start.9 = (bf16[4,96,960]{2,1,0:T(8,128)(2,1)}, bf16[4,96,960]{2,1,0:T(8,128)(2,1)S(1)}, u32[]{:S(2)}, u32[]{:S(2)}) collective-permute-start(bf16[4,96,960]{2,1,0:T(8,128)(2,1)} %get-tuple-element.32), channel_id=1, source_target_pairs={{0,4},{4,0},{8,12},{12,8},{16,20},{20,16},{24,28},{28,24},{1,5},{5... | collective-permute-start | bytes 2211848 | tf_op jit(solution)/shard_map/ppermute | solution.py:256
  104.9 5.4 %all-to-all-start.1 = ((bf16[4,64,1920]{2,1,0:T(8,128)(2,1)}), bf16[4,64,1920]{2,1,0:T(8,128)(2,1)S(1)}, u32[]{:S(2)}, u32[]{:S(2)}) async-start(bf16[4,64,1920]{2,1,0:T(8,128)(2,1)} %get-tuple-element.30), calls=%async_computation.1 | async-start | bytes 1966080 | tf_op jit(solution)/shard_map/all_to_all | solution.py:329
  110.3 4.5 %weight_share.1.refs_1_ = bf16[192,1152]{1,0:T(8,128)(2,1)} custom-call(s32[1]{0:T(128)} %bitcast.1.refs_0_, bf16[8,192,256]{2,1,0:T(8,128)(2,1)} %copy-done.2, bf16[256,1152]{1,0:T(8,128)(2,1)} %bitcast.11, bf16[256,1152]{1,0:T(8,128)(2,1)} %collective-permute-done.26.refs_3_, bf16[256,1152]{1,0:T(8,128)(2,1)} %collective-permute-done.27.refs_4_, ...), custom_call_target="tpu_custom_call" | custom-call | flops 905969664 | bytes 5947396 | tf_op jit(solution)/shard_map/weight_share/pallas_call | solution.py:22
  119.9 7.1 %collective-permute-done.21 = f32[8,768]{1,0:T(8,128)S(1)} collective-permute-done((f32[8,768]{1,0:T(8,128)S(1)}, f32[8,768]{1,0:T(8,128)S(1)}, u32[]{:S(2)}, u32[]{:S(2)}) %collective-permute-start.21) | collective-permute-done | bytes 24608 | tf_op jit(solution)/shard_map/ppermute | solution.py:256
  133.0 2.7 %core_sum.1 = (f32[96,960]{1,0:T(8,128)}, bf16[96,960]{1,0:T(8,128)(2,1)}, bf16[96,960]{1,0:T(8,128)(2,1)}, bf16[96,960]{1,0:T(8,128)(2,1)}) custom-call(s32[2]{0:T(128)} %pad_add_fusion.refs_0_.at, f32[4,96,960]{2,1,0:T(8,128)} %get-tuple-element.31.keep, bf16[4,96,960]{2,1,0:T(8,128)(2,1)} %copy-done.5), custom_call_target="tpu_custom_call" | custom-call | bytes 3133448 | tf_op jit(solution)/shard_map/core_sum/pallas_call | solution.py:22
  136.9 3.4 %collective-permute-start.33 = (bf16[192,1152]{1,0:T(8,128)(2,1)S(1)}, bf16[192,1152]{1,0:T(8,128)(2,1)S(1)}, u32[]{:S(2)}, u32[]{:S(2)}) collective-permute-start(bf16[192,1152]{1,0:T(8,128)(2,1)S(1)} %copy-done.3), channel_id=1, source_target_pairs={{0,4},{4,0},{8,12},{12,8},{16,20},{20,16},{24,28},{28,24},{1,5},{5... | collective-permute-start | bytes 1327112 | tf_op jit(solution)/shard_map/ppermute | solution.py:256
  142.2 2.9 %collective-permute-start.37 = (bf16[192,1152]{1,0:T(8,128)(2,1)S(1)}, bf16[192,1152]{1,0:T(8,128)(2,1)S(1)}, u32[]{:S(2)}, u32[]{:S(2)}) collective-permute-start(bf16[192,1152]{1,0:T(8,128)(2,1)S(1)} %collective-permute-done.36.refs_5_), channel_id=1, source_target_pairs={{0,4},{4,0},{8,12},{12,8},{16,20},{20,16},{24,28},{28,24},{1,5},{5... | collective-permute-start | bytes 1327112 | tf_op jit(solution)/shard_map/ppermute | solution.py:256
  145.1 12.4 %collective-permute-done.11.refs_2_ = bf16[96,960]{1,0:T(8,128)(2,1)S(1)} collective-permute-done((bf16[96,960]{1,0:T(8,128)(2,1)}, bf16[96,960]{1,0:T(8,128)(2,1)S(1)}, u32[]{:S(2)}, u32[]{:S(2)}) %collective-permute-start.11) | collective-permute-done | bytes 184352 | tf_op jit(solution)/shard_map/ppermute | solution.py:256
  158.7 5.6 %collective-permute-done.12.refs_3_ = bf16[96,960]{1,0:T(8,128)(2,1)S(1)} collective-permute-done((bf16[96,960]{1,0:T(8,128)(2,1)}, bf16[96,960]{1,0:T(8,128)(2,1)S(1)}, u32[]{:S(2)}, u32[]{:S(2)}) %collective-permute-start.12) | collective-permute-done | bytes 184352 | tf_op jit(solution)/shard_map/ppermute | solution.py:256
  171.0 2.8 %collective-permute-start.39 = (bf16[192,1152]{1,0:T(8,128)(2,1)S(1)}, bf16[192,1152]{1,0:T(8,128)(2,1)S(1)}, u32[]{:S(2)}, u32[]{:S(2)}) collective-permute-start(bf16[192,1152]{1,0:T(8,128)(2,1)S(1)} %collective-permute-done.38.refs_7_), channel_id=1, source_target_pairs={{0,4},{4,0},{8,12},{12,8},{16,20},{20,16},{24,28},{28,24},{1,5},{5... | collective-permute-start | bytes 1327112 | tf_op jit(solution)/shard_map/ppermute | solution.py:256
  174.6 3.4 %collective-permute-start.15 = (bf16[96,960]{1,0:T(8,128)(2,1)S(1)}, bf16[96,960]{1,0:T(8,128)(2,1)}, u32[]{:S(2)}, u32[]{:S(2)}) collective-permute-start(bf16[96,960]{1,0:T(8,128)(2,1)S(1)} %collective-permute-done.14.refs_3_), channel_id=1, source_target_pairs={{0,4},{4,0},{8,12},{12,8},{16,20},{20,16},{24,28},{28,24},{1,5},{5... | collective-permute-start | bytes 552968 | tf_op jit(solution)/shard_map/ppermute | solution.py:256
  178.0 2.9 %collective-permute-start.17 = (bf16[96,960]{1,0:T(8,128)(2,1)}, bf16[96,960]{1,0:T(8,128)(2,1)}, u32[]{:S(2)}, u32[]{:S(2)}) collective-permute-start(bf16[96,960]{1,0:T(8,128)(2,1)} %collective-permute-done.16.refs_5_), channel_id=1, source_target_pairs={{0,4},{4,0},{8,12},{12,8},{16,20},{20,16},{24,28},{28,24},{1,5},{5... | collective-permute-start | bytes 552968 | tf_op jit(solution)/shard_map/ppermute | solution.py:256
  183.1 4.0 %place_weight_grad.1 = bf16[1536,1152]{1,0:T(8,128)(2,1)} custom-call(s32[2]{0:T(128)} %pad_add_fusion.refs_0_.at, bf16[192,1152]{1,0:T(8,128)(2,1)} %weight_share.1.refs_1_, bf16[192,1152]{1,0:T(8,128)(2,1)} %copy-done.10, bf16[192,1152]{1,0:T(8,128)(2,1)} %copy-done.8, bf16[192,1152]{1,0:T(8,128)(2,1)} %copy-done.12, bf16[192,1152]{1,0:T(8,128)(2,1)} %copy-done.9, ...), custom_call_target="tpu_custom_call" | custom-call | bytes 7077896 | tf_op jit(solution)/shard_map/place_weight_grad/pallas_call | solution.py:22
  187.1 3.1 %place_kernel_grad.1 = bf16[5,768,192]{2,1,0:T(8,128)(2,1)} custom-call(s32[2]{0:T(128)} %pad_add_fusion.refs_0_.at, bf16[96,960]{1,0:T(8,128)(2,1)} %chip_sum.1.refs_1_, bf16[96,960]{1,0:T(8,128)(2,1)} %collective-permute-done.13.refs_2_, bf16[96,960]{1,0:T(8,128)(2,1)} %copy-done.22, bf16[96,960]{1,0:T(8,128)(2,1)} %collective-permute-done.15.refs_4_, ...), custom_call_target="tpu_custom_call" | custom-call | bytes 2949128 | tf_op jit(solution)/shard_map/place_kernel_grad/pallas_call | solution.py:22
  190.3 3.8 %copy.19 = bf16[5,768,192]{1,2,0:T(8,128)(2,1)} copy(bf16[5,768,192]{2,1,0:T(8,128)(2,1)} %place_kernel_grad.1) | data formatting | bytes 2949120
  195.0 2.3 %input_grad.1 = bf16[64,1536]{1,0:T(8,128)(2,1)} custom-call(bf16[4,64,1920]{2,1,0:T(8,128)(2,1)} %copy-done.1, bf16[64,1536]{1,0:T(8,128)(2,1)} %copy-done.6, f32[1,768]{1,0:T(1,128)} %reshape.33.refs_6_.refs_10_.gin), custom_call_target="tpu_custom_call" | custom-call | bytes 1379328 | tf_op jit(solution)/shard_map/input_grad/pallas_call | solution.py:22
  (145 shorter events, 47.5 us)
Async XLA Ops:
  5.4 65.5 %all-to-all-start = ((bf16[4,256,384]{2,1,0:T(8,128)(2,1)}), bf16[4,256,384]{2,1,0:T(8,128)(2,1)S(1)}, u32[]{:S(2)}, u32[]{:S(2)}) async-start(bf16[4,256,384]{2,1,0:T(8,128)(2,1)} %mid_parts.1), calls=%async_computation | async-start | bytes 1572864 | tf_op jit(solution)/shard_map/all_to_all | solution.py:297
  10.4 28.7 %collective-permute-start = (bf16[64,1536]{1,0:T(8,128)(2,1)S(1)}, bf16[64,1536]{1,0:T(8,128)(2,1)S(1)}, u32[]{:S(2)}, u32[]{:S(2)}) collective-permute-start(bf16[64,1536]{1,0:T(8,128)(2,1)S(1)} %reshape_squeeze.3.refs_1_.own), channel_id=1, source_target_pairs={{0,1},{1,2},{2,3},{3,0},{4,5},{5,6},{6,7},{7,4},{8,9},{9,10},{10,1... | collective-permute-start | bytes 589832 | tf_op jit(solution)/shard_map/ppermute | solution.py:254
  11.6 31.6 %collective-permute-start.1 = (bf16[64,1536]{1,0:T(8,128)(2,1)S(1)}, bf16[64,1536]{1,0:T(8,128)(2,1)S(1)}, u32[]{:S(2)}, u32[]{:S(2)}) collective-permute-start(bf16[64,1536]{1,0:T(8,128)(2,1)S(1)} %reshape_squeeze.3.refs_1_.own), channel_id=1, source_target_pairs={{0,2},{1,3},{2,0},{3,1},{4,6},{5,7},{6,4},{7,5},{8,10},{9,11},{10,... | collective-permute-start | bytes 589832 | tf_op jit(solution)/shard_map/ppermute | solution.py:254
  12.6 33.1 %collective-permute-start.2 = (bf16[64,1536]{1,0:T(8,128)(2,1)S(1)}, bf16[64,1536]{1,0:T(8,128)(2,1)}, u32[]{:S(2)}, u32[]{:S(2)}) collective-permute-start(bf16[64,1536]{1,0:T(8,128)(2,1)S(1)} %reshape_squeeze.3.refs_1_.own), channel_id=1, source_target_pairs={{0,3},{1,0},{2,1},{3,2},{4,7},{5,4},{6,5},{7,6},{8,11},{9,8},{10,9... | collective-permute-start | bytes 589832 | tf_op jit(solution)/shard_map/ppermute | solution.py:254
  14.0 65.6 %collective-permute-start.27 = (bf16[256,1152]{1,0:T(8,128)(2,1)S(1)}, bf16[256,1152]{1,0:T(8,128)(2,1)}, u32[]{:S(2)}, u32[]{:S(2)}) collective-permute-start(bf16[256,1152]{1,0:T(8,128)(2,1)S(1)} %bitcast.12), channel_id=1, source_target_pairs={{0,8},{4,12},{8,0},{12,4},{16,24},{20,28},{24,16},{28,20},{1,9},{5... | collective-permute-start | bytes 1769480 | tf_op jit(solution)/shard_map/ppermute | solution.py:256
  15.2 64.7 %collective-permute-start.29 = (bf16[256,1152]{1,0:T(8,128)(2,1)S(1)}, bf16[256,1152]{1,0:T(8,128)(2,1)}, u32[]{:S(2)}, u32[]{:S(2)}) collective-permute-start(bf16[256,1152]{1,0:T(8,128)(2,1)S(1)} %bitcast.13), channel_id=1, source_target_pairs={{0,16},{4,20},{8,24},{12,28},{16,0},{20,4},{24,8},{28,12},{1,17},{... | collective-permute-start | bytes 1769480 | tf_op jit(solution)/shard_map/ppermute | solution.py:256
  39.0 41.0 %collective-permute-start.31 = (bf16[256,1152]{1,0:T(8,128)(2,1)S(1)}, bf16[256,1152]{1,0:T(8,128)(2,1)}, u32[]{:S(2)}, u32[]{:S(2)}) collective-permute-start(bf16[256,1152]{1,0:T(8,128)(2,1)S(1)} %bitcast.14), channel_id=1, source_target_pairs={{0,24},{4,28},{8,16},{12,20},{16,8},{20,12},{24,0},{28,4},{1,25},{... | collective-permute-start | bytes 1769480 | tf_op jit(solution)/shard_map/ppermute | solution.py:256
  50.4 15.0 %collective-permute-start.4 = (bf16[256,384]{1,0:T(8,128)(2,1)}, bf16[256,384]{1,0:T(8,128)(2,1)S(1)}, u32[]{:S(2)}, u32[]{:S(2)}) collective-permute-start(bf16[256,384]{1,0:T(8,128)(2,1)} %get-tuple-element.22.refs_1_), channel_id=1, source_target_pairs={{0,2},{1,3},{2,0},{3,1},{4,6},{5,7},{6,4},{7,5},{8,10},{9,11},{10,... | collective-permute-start | bytes 589832 | tf_op jit(solution)/shard_map/ppermute | solution.py:254
  55.6 12.1 %collective-permute-start.5 = (bf16[256,384]{1,0:T(8,128)(2,1)}, bf16[256,384]{1,0:T(8,128)(2,1)S(1)}, u32[]{:S(2)}, u32[]{:S(2)}) collective-permute-start(bf16[256,384]{1,0:T(8,128)(2,1)} %get-tuple-element.22.refs_1_), channel_id=1, source_target_pairs={{0,3},{1,0},{2,1},{3,2},{4,7},{5,4},{6,5},{7,6},{8,11},{9,8},{10,9... | collective-permute-start | bytes 589832 | tf_op jit(solution)/shard_map/ppermute | solution.py:254
  71.0 33.9 %all-to-all-start.2 = ((bf16[8,192,256]{2,1,0:T(8,128)(2,1)}), bf16[8,192,256]{2,1,0:T(8,128)(2,1)S(1)}, u32[]{:S(2)}, u32[]{:S(2)}) async-start(bf16[8,192,256]{2,1,0:T(8,128)(2,1)} %bitcast.16), calls=%async_computation.2 | async-start | bytes 1572864 | tf_op jit(solution)/shard_map/all_to_all | solution.py:298
  79.4 30.9 %collective-permute-start.26 = (bf16[256,1152]{1,0:T(8,128)(2,1)S(1)}, bf16[256,1152]{1,0:T(8,128)(2,1)}, u32[]{:S(2)}, u32[]{:S(2)}) collective-permute-start(bf16[256,1152]{1,0:T(8,128)(2,1)S(1)} %bitcast.15), channel_id=1, source_target_pairs={{0,4},{4,0},{8,12},{12,8},{16,20},{20,16},{24,28},{28,24},{1,5},{5... | collective-permute-start | bytes 1769480 | tf_op jit(solution)/shard_map/ppermute | solution.py:256
  79.6 30.7 %collective-permute-start.28 = (bf16[256,1152]{1,0:T(8,128)(2,1)}, bf16[256,1152]{1,0:T(8,128)(2,1)}, u32[]{:S(2)}, u32[]{:S(2)}) collective-permute-start(bf16[256,1152]{1,0:T(8,128)(2,1)} %collective-permute-done.27.refs_4_), channel_id=1, source_target_pairs={{0,4},{4,0},{8,12},{12,8},{16,20},{20,16},{24,28},{28,24},{1,5},{5... | collective-permute-start | bytes 1769480 | tf_op jit(solution)/shard_map/ppermute | solution.py:256
  79.9 30.4 %collective-permute-start.30 = (bf16[256,1152]{1,0:T(8,128)(2,1)}, bf16[256,1152]{1,0:T(8,128)(2,1)}, u32[]{:S(2)}, u32[]{:S(2)}) collective-permute-start(bf16[256,1152]{1,0:T(8,128)(2,1)} %collective-permute-done.29.refs_6_), channel_id=1, source_target_pairs={{0,4},{4,0},{8,12},{12,8},{16,20},{20,16},{24,28},{28,24},{1,5},{5... | collective-permute-start | bytes 1769480 | tf_op jit(solution)/shard_map/ppermute | solution.py:256
  80.1 30.2 %collective-permute-start.32 = (bf16[256,1152]{1,0:T(8,128)(2,1)}, bf16[256,1152]{1,0:T(8,128)(2,1)}, u32[]{:S(2)}, u32[]{:S(2)}) collective-permute-start(bf16[256,1152]{1,0:T(8,128)(2,1)} %collective-permute-done.31.refs_8_), channel_id=1, source_target_pairs={{0,4},{4,0},{8,12},{12,8},{16,20},{20,16},{24,28},{28,24},{1,5},{5... | collective-permute-start | bytes 1769480 | tf_op jit(solution)/shard_map/ppermute | solution.py:256
  102.0 30.2 %collective-permute-start.9 = (bf16[4,96,960]{2,1,0:T(8,128)(2,1)}, bf16[4,96,960]{2,1,0:T(8,128)(2,1)S(1)}, u32[]{:S(2)}, u32[]{:S(2)}) collective-permute-start(bf16[4,96,960]{2,1,0:T(8,128)(2,1)} %get-tuple-element.32), channel_id=1, source_target_pairs={{0,4},{4,0},{8,12},{12,8},{16,20},{20,16},{24,28},{28,24},{1,5},{5... | collective-permute-start | bytes 2211848 | tf_op jit(solution)/shard_map/ppermute | solution.py:256
  104.9 89.2 %all-to-all-start.1 = ((bf16[4,64,1920]{2,1,0:T(8,128)(2,1)}), bf16[4,64,1920]{2,1,0:T(8,128)(2,1)S(1)}, u32[]{:S(2)}, u32[]{:S(2)}) async-start(bf16[4,64,1920]{2,1,0:T(8,128)(2,1)} %get-tuple-element.30), calls=%async_computation.1 | async-start | bytes 1966080 | tf_op jit(solution)/shard_map/all_to_all | solution.py:329
  114.9 26.7 %collective-permute-start.34 = (bf16[192,1152]{1,0:T(8,128)(2,1)}, bf16[192,1152]{1,0:T(8,128)(2,1)S(1)}, u32[]{:S(2)}, u32[]{:S(2)}) collective-permute-start(bf16[192,1152]{1,0:T(8,128)(2,1)} %weight_share.1.refs_1_), channel_id=1, source_target_pairs={{0,8},{4,12},{8,0},{12,4},{16,24},{20,28},{24,16},{28,20},{1,9},{5... | collective-permute-start | bytes 1327112 | tf_op jit(solution)/shard_map/ppermute | solution.py:256
  116.4 25.2 %collective-permute-start.36 = (bf16[192,1152]{1,0:T(8,128)(2,1)}, bf16[192,1152]{1,0:T(8,128)(2,1)S(1)}, u32[]{:S(2)}, u32[]{:S(2)}) collective-permute-start(bf16[192,1152]{1,0:T(8,128)(2,1)} %weight_share.1.refs_1_), channel_id=1, source_target_pairs={{0,16},{4,20},{8,24},{12,28},{16,0},{20,4},{24,8},{28,12},{1,17},{... | collective-permute-start | bytes 1327112 | tf_op jit(solution)/shard_map/ppermute | solution.py:256
  119.6 7.4 %collective-permute-start.21 = (f32[8,768]{1,0:T(8,128)S(1)}, f32[8,768]{1,0:T(8,128)S(1)}, u32[]{:S(2)}, u32[]{:S(2)}) collective-permute-start(f32[8,768]{1,0:T(8,128)S(1)} %add.18), channel_id=1, source_target_pairs={{0,8},{4,12},{8,0},{12,4},{16,24},{20,28},{24,16},{28,20},{1,9},{5... | collective-permute-start | bytes 73736 | tf_op jit(solution)/shard_map/ppermute | solution.py:256
  129.7 7.2 %collective-permute-start.25 = (f32[8,768]{1,0:T(8,128)S(1)}, f32[8,768]{1,0:T(8,128)S(1)}, u32[]{:S(2)}, u32[]{:S(2)}) collective-permute-start(f32[8,768]{1,0:T(8,128)S(1)} %add.20), channel_id=1, source_target_pairs={{0,3},{1,0},{2,1},{3,2},{4,7},{5,4},{6,5},{7,6},{8,11},{9,8},{10,9... | collective-permute-start | bytes 73736 | tf_op jit(solution)/shard_map/ppermute | solution.py:254
  130.3 10.0 %collective-permute-start.24 = (f32[8,768]{1,0:T(8,128)S(1)}, f32[8,768]{1,0:T(8,128)S(1)}, u32[]{:S(2)}, u32[]{:S(2)}) collective-permute-start(f32[8,768]{1,0:T(8,128)S(1)} %add.20), channel_id=1, source_target_pairs={{0,2},{1,3},{2,0},{3,1},{4,6},{5,7},{6,4},{7,5},{8,10},{9,11},{10,... | collective-permute-start | bytes 73736 | tf_op jit(solution)/shard_map/ppermute | solution.py:254
  136.9 31.9 %collective-permute-start.33 = (bf16[192,1152]{1,0:T(8,128)(2,1)S(1)}, bf16[192,1152]{1,0:T(8,128)(2,1)S(1)}, u32[]{:S(2)}, u32[]{:S(2)}) collective-permute-start(bf16[192,1152]{1,0:T(8,128)(2,1)S(1)} %copy-done.3), channel_id=1, source_target_pairs={{0,4},{4,0},{8,12},{12,8},{16,20},{20,16},{24,28},{28,24},{1,5},{5... | collective-permute-start | bytes 1327112 | tf_op jit(solution)/shard_map/ppermute | solution.py:256
  140.3 29.5 %collective-permute-start.38 = (bf16[192,1152]{1,0:T(8,128)(2,1)S(1)}, bf16[192,1152]{1,0:T(8,128)(2,1)S(1)}, u32[]{:S(2)}, u32[]{:S(2)}) collective-permute-start(bf16[192,1152]{1,0:T(8,128)(2,1)S(1)} %copy-done.3), channel_id=1, source_target_pairs={{0,24},{4,28},{8,16},{12,20},{16,8},{20,12},{24,0},{28,4},{1,25},{... | collective-permute-start | bytes 1327112 | tf_op jit(solution)/shard_map/ppermute | solution.py:256
  141.5 16.0 %collective-permute-start.11 = (bf16[96,960]{1,0:T(8,128)(2,1)}, bf16[96,960]{1,0:T(8,128)(2,1)S(1)}, u32[]{:S(2)}, u32[]{:S(2)}) collective-permute-start(bf16[96,960]{1,0:T(8,128)(2,1)} %get-tuple-element.35), channel_id=1, source_target_pairs={{0,16},{4,20},{8,24},{12,28},{16,0},{20,4},{24,8},{28,12},{1,17},{... | collective-permute-start | bytes 552968 | tf_op jit(solution)/shard_map/ppermute | solution.py:256
  141.6 29.4 %collective-permute-start.35 = (bf16[192,1152]{1,0:T(8,128)(2,1)S(1)}, bf16[192,1152]{1,0:T(8,128)(2,1)S(1)}, u32[]{:S(2)}, u32[]{:S(2)}) collective-permute-start(bf16[192,1152]{1,0:T(8,128)(2,1)S(1)} %collective-permute-done.34.refs_3_), channel_id=1, source_target_pairs={{0,4},{4,0},{8,12},{12,8},{16,20},{20,16},{24,28},{28,24},{1,5},{5... | collective-permute-start | bytes 1327112 | tf_op jit(solution)/shard_map/ppermute | solution.py:256
  142.2 31.6 %collective-permute-start.37 = (bf16[192,1152]{1,0:T(8,128)(2,1)S(1)}, bf16[192,1152]{1,0:T(8,128)(2,1)S(1)}, u32[]{:S(2)}, u32[]{:S(2)}) collective-permute-start(bf16[192,1152]{1,0:T(8,128)(2,1)S(1)} %collective-permute-done.36.refs_5_), channel_id=1, source_target_pairs={{0,4},{4,0},{8,12},{12,8},{16,20},{20,16},{24,28},{28,24},{1,5},{5... | collective-permute-start | bytes 1327112 | tf_op jit(solution)/shard_map/ppermute | solution.py:256
  168.8 9.2 %collective-permute-start.16 = (bf16[96,960]{1,0:T(8,128)(2,1)}, bf16[96,960]{1,0:T(8,128)(2,1)}, u32[]{:S(2)}, u32[]{:S(2)}) collective-permute-start(bf16[96,960]{1,0:T(8,128)(2,1)} %chip_sum.1.refs_1_), channel_id=1, source_target_pairs={{0,16},{4,20},{8,24},{12,28},{16,0},{20,4},{24,8},{28,12},{1,17},{... | collective-permute-start | bytes 552968 | tf_op jit(solution)/shard_map/ppermute | solution.py:256
  169.8 11.0 %collective-permute-start.18 = (bf16[96,960]{1,0:T(8,128)(2,1)}, bf16[96,960]{1,0:T(8,128)(2,1)}, u32[]{:S(2)}, u32[]{:S(2)}) collective-permute-start(bf16[96,960]{1,0:T(8,128)(2,1)} %chip_sum.1.refs_1_), channel_id=1, source_target_pairs={{0,24},{4,28},{8,16},{12,20},{16,8},{20,12},{24,0},{28,4},{1,25},{... | collective-permute-start | bytes 552968 | tf_op jit(solution)/shard_map/ppermute | solution.py:256
  171.0 11.3 %collective-permute-start.39 = (bf16[192,1152]{1,0:T(8,128)(2,1)S(1)}, bf16[192,1152]{1,0:T(8,128)(2,1)S(1)}, u32[]{:S(2)}, u32[]{:S(2)}) collective-permute-start(bf16[192,1152]{1,0:T(8,128)(2,1)S(1)} %collective-permute-done.38.refs_7_), channel_id=1, source_target_pairs={{0,4},{4,0},{8,12},{12,8},{16,20},{20,16},{24,28},{28,24},{1,5},{5... | collective-permute-start | bytes 1327112 | tf_op jit(solution)/shard_map/ppermute | solution.py:256
  173.8 13.3 %collective-permute-start.13 = (bf16[96,960]{1,0:T(8,128)(2,1)}, bf16[96,960]{1,0:T(8,128)(2,1)}, u32[]{:S(2)}, u32[]{:S(2)}) collective-permute-start(bf16[96,960]{1,0:T(8,128)(2,1)} %chip_sum.1.refs_1_), channel_id=1, source_target_pairs={{0,4},{4,0},{8,12},{12,8},{16,20},{20,16},{24,28},{28,24},{1,5},{5... | collective-permute-start | bytes 552968 | tf_op jit(solution)/shard_map/ppermute | solution.py:256
  174.6 12.5 %collective-permute-start.15 = (bf16[96,960]{1,0:T(8,128)(2,1)S(1)}, bf16[96,960]{1,0:T(8,128)(2,1)}, u32[]{:S(2)}, u32[]{:S(2)}) collective-permute-start(bf16[96,960]{1,0:T(8,128)(2,1)S(1)} %collective-permute-done.14.refs_3_), channel_id=1, source_target_pairs={{0,4},{4,0},{8,12},{12,8},{16,20},{20,16},{24,28},{28,24},{1,5},{5... | collective-permute-start | bytes 552968 | tf_op jit(solution)/shard_map/ppermute | solution.py:256
  178.0 9.1 %collective-permute-start.17 = (bf16[96,960]{1,0:T(8,128)(2,1)}, bf16[96,960]{1,0:T(8,128)(2,1)}, u32[]{:S(2)}, u32[]{:S(2)}) collective-permute-start(bf16[96,960]{1,0:T(8,128)(2,1)} %collective-permute-done.16.refs_5_), channel_id=1, source_target_pairs={{0,4},{4,0},{8,12},{12,8},{16,20},{20,16},{24,28},{28,24},{1,5},{5... | collective-permute-start | bytes 552968 | tf_op jit(solution)/shard_map/ppermute | solution.py:256
  (42 other events, 409.2 us)

commit v2 on v1

v2 whole, which is shorter than its diff:
```python
import functools
import math

import jax
import jax.numpy as jnp
from jax import lax
from jax.experimental import pallas as pl
from jax.experimental.pallas import tpu as pltpu
from jax.sharding import PartitionSpec as P

EPS = 1e-06
SPARE = 12
F32 = jnp.float32
BF16 = jnp.bfloat16
VMEM = pl.BlockSpec(memory_space=pltpu.VMEM)
ANY = pl.BlockSpec(memory_space=pl.ANY)


def call(kernel, outs, args, held=(), scratch=(), name=None):
    lanes = lambda v: math.prod(v.shape[:-1]) * -(-v.shape[-1] // 128) * 128 * v.dtype.itemsize
    need = sum(map(lanes, [*args, *outs, *scratch]))
    return pl.pallas_call(
        kernel,
        out_shape=tuple(outs) + tuple(shaped(v.shape, v.dtype) for v in held),
        in_specs=[VMEM] * len(args) + [ANY] * len(held),
        out_specs=tuple([VMEM] * len(outs) + [ANY] * len(held)),
        input_output_aliases={len(args) + i: len(outs) + i for i in range(len(held))},
        scratch_shapes=list(scratch),
        compiler_params=pltpu.CompilerParams(vmem_limit_bytes=min(56 << 20, need + (SPARE << 20))),
        cost_estimate=pl.CostEstimate(flops=0, bytes_accessed=0, transcendentals=0),
        name=name,
    )(*args, *held)


def shaped(shape, dtype):
    return jax.ShapeDtypeStruct(shape, dtype)


def dot(a, b):
    return jnp.dot(a, b, preferred_element_type=F32)


def dot_nt(a, b):
    return lax.dot_general(a, b, (((1,), (1,)), ((), ())), preferred_element_type=F32)


def dot_tn(a, b):
    return lax.dot_general(a, b, (((0,), (0,)), ((), ())), preferred_element_type=F32)


def later(v):
    row = lax.broadcasted_iota(jnp.int32, v.shape, 0)
    return jnp.where(row == 0, 0.0, pltpu.roll(v, 1, 0))


def sooner(v):
    rows = v.shape[0]
    row = lax.broadcasted_iota(jnp.int32, v.shape, 0)
    return jnp.where(row == rows - 1, 0.0, pltpu.roll(v, rows - 1, 0))


def inv_rms(v):
    return lax.rsqrt(jnp.mean(v * v, axis=-1, keepdims=True) + EPS)


def mid_kernel(n, c, chans, cot, w, *refs):
    outs = refs[1 : 1 + n]
    me = lax.axis_index("seq")
    g = cot[...]
    for k in range(n):
        at = pl.multiple_of(lax.rem(me + k, n) * c, c & -c)
        rows = jnp.concatenate([w[pl.ds(at, c), :], w[pl.ds(chans + at, c), :]], axis=0)
        outs[k][...] = dot_nt(g, rows).astype(BF16)


def conv_fwd_kernel(n, c, chans, *refs):
    me = lax.axis_index("seq")
    blocks = refs[:n]
    taps, gain, pooled_msg, pooled, conv_out, nin, xs = refs[n:]
    rows = blocks[0].shape[0]
    gains = gain[...]
    for k in range(n):
        at = pl.multiple_of(lax.rem(me - k + n, n) * rows, rows)
        v = blocks[k][...]
        xs[pl.ds(at, rows), :] = v
        for h in range(2):
            f = v[:, h * chans : (h + 1) * chans].astype(F32)
            nin[pl.ds(at, rows), h * chans : (h + 1) * chans] = (f * inv_rms(f) * gains).astype(BF16)
    xe, xo = nin[:, :chans], nin[:, chans:]
    k0, k1, k2, k3, k4 = (taps[k] for k in range(5))
    even = dot_nt(xe, k2) + dot_nt(xo, k3) + later(dot_nt(xe, k0) + dot_nt(xo, k1)) + sooner(dot_nt(xe, k4))
    odd = dot_nt(xe, k1) + dot_nt(xo, k2) + later(dot_nt(xo, k0)) + sooner(dot_nt(xe, k3) + dot_nt(xo, k4))
    conv = jnp.concatenate([even, odd], axis=1)
    row = lax.broadcasted_iota(jnp.int32, (chans, c), 0)
    col = lax.broadcasted_iota(jnp.int32, (chans, c), 1)
    pick = jnp.where(row == col + me * c, 1.0, 0.0).astype(BF16)
    own = jnp.concatenate([dot(xs[:, :chans], pick), dot(xs[:, chans:], pick)], axis=1)
    total = own + conv * jax.nn.sigmoid(conv)
    conv_out[...] = conv
    pooled[...] = total
    pooled_msg[...] = total.astype(BF16)


def norm_kernel(n, c, chans, *refs):
    me = lax.axis_index("seq")
    blocks = refs[:n]
    gains = refs[n]
    nmt, rtwo = refs[2 * n + 1 : 2 * n + 3]
    squares = 0.0
    for k in range(n):
        v = blocks[k][...].astype(F32)
        squares = squares + jnp.sum(v * v, axis=1, keepdims=True)
    r = lax.rsqrt(squares * (1.0 / (2 * chans)) + EPS)
    rtwo[...] = r
    for k in range(n):
        b = lax.rem(me - k + n, n)
        v = blocks[k][...].astype(F32) * r * gains[pl.ds(b, 1), :]
        t = v.T.astype(BF16)
        for h in range(2):
            at = pl.multiple_of(h * chans + b * c, c & -c)
            nmt[pl.ds(at, c), :] = t[h * c : (h + 1) * c, :]


def qkv_kernel(nmt, w, cot, qkv, part):
    q = dot_tn(nmt[...], w[...])
    qkv[...] = q.astype(BF16)
    row = jnp.sum(q * cot[...].astype(F32), axis=1, keepdims=True)
    part[...] = jnp.broadcast_to(row, (row.shape[0], 128)).T[:8, :]


def weight_kernel(m, scale, nms, cots, out):
    total = dot(nms[0], cots[0])
    for b in range(1, m):
        total = total + dot(nms[b], cots[b])
    out[...] = (total * scale).astype(BF16)


def back_kernel(n, c, chans, m, *refs):
    seq_at = lax.axis_index("seq")
    core = lax.rem(lax.axis_index("dp"), 2)
    parts, mids = refs[:n], refs[n : 2 * n]
    pooled, rtwo, conv_out, gmid, nin, keep, send, evens, odds, section_out, mid_sum = refs[2 * n :]
    mid = mids[0][...].astype(F32)
    for v in mids[1:]:
        mid = mid + v[...].astype(F32)
    r = rtwo[...]
    atwo = pooled[...] * r
    rowsum = parts[0][...]
    for v in parts[1:]:
        rowsum = rowsum + v[...]
    mean = jnp.concatenate([rowsum] * 16, axis=0).T[:, :1] * (1.0 / (2 * chans))
    mid_sum[...] = jnp.sum(mid * atwo, axis=0, keepdims=True)
    section = r * (gmid[pl.ds(seq_at, 1), :] * mid - atwo * mean)
    section_out[...] = section.astype(BF16)
    conv = conv_out[...]
    sig = jax.nn.sigmoid(conv)
    cg = section * sig * (1.0 + conv * (1.0 - sig))
    cg = cg.astype(BF16).astype(F32)
    ge, go = cg[:, :c], cg[:, c:]
    bf = lambda v: v.astype(BF16)
    g0, gp, gm = bf(ge), bf(sooner(ge)), bf(later(ge))
    o0, op, om = bf(go), bf(sooner(go)), bf(later(go))
    evens[...] = jnp.concatenate((gp, o0, g0, om, gm), axis=1)
    odds[...] = jnp.concatenate((op, gp, o0, g0, om), axis=1)
    wide, rows = chans // 2, 5 * c // (m // 2)
    for out, which in ((send, 1 - core), (keep, core)):
        at = pl.multiple_of(which * wide, wide & -wide)
        kg = dot_tn(evens[...], nin[:, pl.ds(at, wide)]) + dot_tn(odds[...], nin[:, pl.ds(chans + at, wide)])
        for q in range(m // 2):
            out[q] = kg[q * rows : (q + 1) * rows, :].astype(out.dtype)


def input_part_kernel(n, c, chans, evens, odds, section, mid_sum, gin, nin, taps, msg, sums):
    width = 2 * chans
    block = evens.shape[0] // n
    acc = 0.0
    for h, g in ((0, evens), (1, odds)):
        ng = dot(g[...], taps[...])
        acc = acc + jnp.sum(ng * nin[:, h * chans : (h + 1) * chans].astype(F32), axis=0, keepdims=True)
        for b in range(n):
            msg[b, :, h * chans : (h + 1) * chans] = ng[b * block : (b + 1) * block, :].astype(BF16)
    for b in range(n):
        msg[b, :, width:] = section[b * block : (b + 1) * block, :]
    acc = acc / gin[...]
    wide = chans // 2
    own = mid_sum[...]
    if 2 * c < wide:
        own = jnp.concatenate([own, jnp.zeros((1, wide - 2 * c), F32)], axis=1)
    line = lax.broadcasted_iota(jnp.int32, sums.shape, 0)
    pick = lambda i, v: jnp.where(line == i, v, 0.0)
    sums[...] = pick(0, acc[:, :wide]) + pick(1, acc[:, wide:]) + pick(2, own)


def split_kernel(q, *refs):
    keep, recv, outs = refs[0], refs[1], refs[-q:]
    me = lax.axis_index("dp") // 2
    for k in range(q):
        v = keep[me ^ k] + recv[me ^ k].astype(F32)
        outs[k][...] = v.astype(outs[k].dtype)


def in_two(v):
    high = v.astype(BF16).astype(F32)
    return jnp.concatenate([high, v - high], axis=0).astype(BF16)


def finish_kernel(n, q, scale, *refs):
    me = lax.axis_index("seq")
    shares, sums, out = refs[:q], refs[q : q + n], refs[q + n]
    total = shares[0][...]
    for r in shares[1:]:
        total = total + r[...].astype(F32)
    rows = total.shape[0]
    out[:rows, :] = (total * scale).astype(BF16)
    both = sums[0][...]
    for r in sums[1:]:
        both = both + r[...]
    line = lax.broadcasted_iota(jnp.int32, both.shape, 0)
    tail = jnp.where(line < 2, both, 0.0)
    for k in range(n):
        row = jnp.broadcast_to(sums[k][2:3, :], both.shape)
        tail = jnp.where(line == 2 + lax.rem(me - k + n, n), row, tail)
    out[rows:, :] = in_two(tail * scale)


def joined(tail):
    return tail[:8].astype(F32) + tail[8:].astype(F32)


def half_kernel(q, *refs):
    me = lax.axis_index("dp") // 2
    shares, out = refs[:q], refs[q]
    rows = shares[0].shape[0] - 16
    tail = 0.0
    for k in range(q):
        at = pl.multiple_of((me ^ k) * rows, rows & -rows)
        out[pl.ds(at, rows), :] = shares[k][:rows, :]
        tail = tail + joined(shares[k][rows:, :])
    out[q * rows :, :] = in_two(tail)


def place_kernel(n, c, mine, other, taps, gain_in, gain_mid):
    core = lax.rem(lax.axis_index("dp"), 2)
    rows, wide = taps.shape[0], mine.shape[1]
    for ref, which in ((mine, core), (other, 1 - core)):
        side = pl.multiple_of(which * wide, wide & -wide)
        taps[:, pl.ds(side, wide)] = ref[:rows, :]
    total = joined(mine[rows:, :]) + joined(other[rows:, :])
    gain_in[...] = total[:2, :]
    gain_mid[...] = total[2 : 2 + n, : 2 * c]


def input_kernel(n, c, chans, got, own, gin, out):
    total = got[0, :, : 2 * chans].astype(F32)
    for b in range(1, n):
        total = total + got[b, :, : 2 * chans].astype(F32)
    gains = gin[...]
    for h in range(2):
        x = own[:, h * chans : (h + 1) * chans].astype(F32)
        r = inv_rms(x)
        a = x * r
        g = gains * total[:, h * chans : (h + 1) * chans]
        sect = jnp.concatenate(
            [got[b, :, 2 * chans + h * c : 2 * chans + (h + 1) * c] for b in range(n)], axis=1
        ).astype(F32)
        v = sect + r * (g - a * jnp.mean(g * a, axis=-1, keepdims=True))
        out[:, h * chans : (h + 1) * chans] = v.astype(BF16)


def body(section_input, conv_kernel, qkv_weight, gain_in, gain_mid, qkv_cotangent):
    x = section_input[0]
    cot = qkv_cotangent[0]
    length, chans = x.shape
    c = conv_kernel.shape[2]
    width, cols = qkv_weight.shape
    n, m = lax.axis_size("seq"), lax.axis_size("dp")
    half = length // 2 * n
    scale = 1.0 / math.sqrt(m * half)
    shift = lambda v, k: lax.ppermute(v, "seq", [(i, (i + k) % n) for i in range(n)])
    from_ring = lambda v: [v] + [shift(v, k) for k in range(1, n)]
    across = lambda v, k: lax.ppermute(v, "dp", [(i, i ^ k) for i in range(m)])

    taps = conv_kernel.transpose(0, 2, 1)
    own = x.reshape(length // 2, width)
    xs = from_ring(own)
    gin = gain_in.reshape(1, chans)
    gmid = gain_mid.reshape(2, n, c).transpose(1, 0, 2).reshape(n, 2 * c)
    cots = lax.all_gather(cot, "dp", axis=0)
    pooled_msg, pooled, conv_out, nin = call(
        functools.partial(conv_fwd_kernel, n, c, chans),
        [
            shaped((half, 2 * c), BF16),
            shaped((half, 2 * c), F32),
            shaped((half, 2 * c), F32),
            shaped((half, width), BF16),
        ],
        [*xs, taps, gin],
        scratch=[pltpu.VMEM((half, width), BF16)],
        name="conv_forward",
    )
    blocks = from_ring(pooled_msg)
    *mid_msgs, pooled = call(
        functools.partial(mid_kernel, n, c, chans),
        [shaped((half, 2 * c), BF16)] * n,
        [cot, qkv_weight],
        held=[pooled],
        name="mid_parts",
    )
    nmt, rtwo, *mid_msgs = call(
        functools.partial(norm_kernel, n, c, chans),
        [shaped((width, half), BF16), shaped((half, 1), F32)],
        [*blocks, gmid],
        held=mid_msgs,
        name="norm_mid",
    )
    mids = [mid_msgs[0]] + [shift(mid_msgs[k], k) for k in range(1, n)]
    nms = lax.all_to_all(nmt.reshape(m, width // m, half), "dp", 0, 0, tiled=True)
    qkv, part = call(
        qkv_kernel,
        [shaped((half, cols), BF16), shaped((8, half), F32)],
        [nmt, qkv_weight, cot],
        name="qkv",
    )
    parts = from_ring(part)
    (wshare,) = call(
        functools.partial(weight_kernel, m, scale),
        [shaped((width // m, cols), BF16)],
        [nms, cots],
        name="weight_share",
    )
    weight_grad = lax.all_gather(wshare, "dp", axis=0, tiled=True)
    chips = m // 2
    rows, wide = 5 * c // chips, chans // 2
    keep, send, evens, odds, section, mid_sum = call(
        functools.partial(back_kernel, n, c, chans, m),
        [
            shaped((chips, rows, wide), F32),
            shaped((chips, rows, wide), BF16),
            shaped((half, 5 * c), BF16),
            shaped((half, 5 * c), BF16),
            shaped((half, 2 * c), BF16),
            shaped((1, 2 * c), F32),
        ],
        [*parts, *mids, pooled, rtwo, conv_out, gmid, nin],
        name="conv_backward",
    )
    msg, sums = call(
        functools.partial(input_part_kernel, n, c, chans),
        [shaped((n, half // n, width + 2 * c), BF16), shaped((8, wide), F32)],
        [evens, odds, section, mid_sum, gin, nin, taps.reshape(5 * c, chans)],
        name="input_part",
    )
    got = lax.all_to_all(msg, "seq", 0, 0, tiled=True)
    if rows % 16 == 0 and n <= 6:
        split = call(
            functools.partial(split_kernel, chips),
            [shaped((rows, wide), F32)] + [shaped((rows, wide), BF16)] * (chips - 1),
            [keep, across(send, 1)],
            name="core_sum",
        )
        (kshare,) = call(
            functools.partial(finish_kernel, n, chips, scale),
            [shaped((rows + 16, wide), BF16)],
            [split[0]] + [across(split[k], 2 * k) for k in range(1, chips)] + from_ring(sums),
            name="chip_sum",
        )
        (mine,) = call(
            functools.partial(half_kernel, chips),
            [shaped((5 * c + 16, wide), BF16)],
            [kshare] + [across(kshare, k) for k in range(2, m, 2)],
            name="kernel_grad_half",
        )
        taps_grad, gain_in_grad, gain_mid_grad = call(
            functools.partial(place_kernel, n, c),
            [shaped((5 * c, chans), BF16), shaped((2, wide), F32), shaped((n, 2 * c), F32)],
            [mine, across(mine, 1)],
            name="kernel_grad",
        )
    else:
        core = lax.axis_index("dp") % 2
        both = jnp.stack([keep, send.astype(F32)])
        both = jnp.where(core == 0, both, both[::-1]).transpose(1, 2, 0, 3).reshape(5 * c, chans)
        both, sums = lax.psum((both, sums), "dp")
        taps_grad, sums = (both * scale).astype(BF16), sums * scale
        sums = lax.all_gather(sums, "seq")
        gain_in_grad = jnp.sum(sums[:, :2], axis=0)
        gain_mid_grad = sums[:, 2, : 2 * c]
    (input_grad,) = call(
        functools.partial(input_kernel, n, c, chans),
        [shaped((length // 2, width), BF16)],
        [got, own, gin],
        name="input_grad",
    )
    return (
        qkv[None],
        input_grad.reshape(1, length, chans),
        taps_grad.reshape(5, c, chans).transpose(0, 2, 1),
        gain_in_grad.reshape(chans),
        gain_mid_grad.reshape(n, 2, c).transpose(1, 0, 2).reshape(width),
        weight_grad,
    )


def solution(mesh):
    placed = (
        P("dp", "seq", None),
        P(None, None, "seq"),
        P(None, "seq"),
        P(),
        P(),
        P("dp", None, "seq"),
    )
    return jax.shard_map(
        body,
        mesh=mesh,
        in_specs=placed,
        out_specs=(
            P("dp", None, "seq"),
            P("dp", "seq", None),
            P(None, None, "seq"),
            P(),
            P(),
            P(None, "seq"),
        ),
        check_vma=False,
    )
```

time: 202 us -> 165 us (0.82)
  starting transfers between devices: 69.8 us -> 29.4 us
  Pallas kernels: 41.8 us -> 12.1 us
  blocking collectives: 0 us -> 15.3 us
  between operations: 0.83 us -> 14.3 us
  local copies, waits for them, and re-layouts: 14.5 us -> 25.6 us
  waiting for transfers between devices: 71.3 us -> 65.6 us
    pallas_call x11 -> x12, Pallas kernels: 41.8 us -> 12.1 us  [call(): pl.pallas_call(kernel, out_shape=tuple(outs) + tuple((shaped(v.shape, v.d...]
    ppermute x28 -> x8, starting transfers between devices: 37 us -> 11.6 us  [body(): across = lambda v, k: lax.ppermute(v, 'dp', [(i, i ^ k) for i in range(m)])]
    ppermute x28 -> x8, waiting for transfers between devices: 27.4 us -> 6.46 us  [body(): across = lambda v, k: lax.ppermute(v, 'dp', [(i, i ^ k) for i in range(m)])]
    all_to_all x0 -> x1, blocking collectives: none -> 15.3 us  [body(): lax.all_to_all(nmt.reshape(m, width // m, half), 'dp', 0, 0, tiled=True)]
    ppermute x12 -> x15, waiting for transfers between devices: 43.9 us -> 58.5 us  [body(): lax.ppermute(v, 'seq', [(i, (i + k) % n) for i in range(n)])]
    all_to_all x2 -> x0, starting transfers between devices: 13.3 us -> none  [the longest x1 8.44 us: body(): lax.all_to_all(nmt.reshape(m, width // m, half), 'dp', 0, 0, tiled=True)]
    unnamed x64 -> x55, local copies, waits for them, and re-layouts: 10 us -> 20.9 us
    ppermute x12 -> x15, starting transfers between devices: 14.1 us -> 13.5 us  [body(): lax.ppermute(v, 'seq', [(i, (i + k) % n) for i in range(n)])]
  transfers between devices with their start and end apart: 43 -> 26, of which waited for: 14 -> 14; matrix products, arithmetic and copies ran while one was open for 5% -> 3% of each run, Pallas kernels for 17% -> 7%
where the time goes in v2:
time: 165 us; the launch traced here: 162 us
  waiting for transfers between devices  65.6 us (40%)
  starting transfers between devices  29.4 us (18%)
  local copies, waits for them, and re-layouts  25.6 us (16%)
  blocking collectives  15.3 us (9%)
  between operations  14.3 us (9%)
  Pallas kernels  12.1 us (7%)
    ppermute x15, waiting for transfers between devices, body(): lax.ppermute(v, 'seq', [(i, (i + k) % n) for i in range(n)])  58.5 us
    unnamed x55, local copies, waits for them, and re-layouts  20.9 us
    all_to_all x1, blocking collectives, body(): lax.all_to_all(nmt.reshape(m, width // m, half), 'dp', 0, 0, tiled=True)  15.3 us
    ppermute x15, starting transfers between devices, body(): lax.ppermute(v, 'seq', [(i, (i + k) % n) for i in range(n)])  13.5 us
    pallas_call x12, Pallas kernels, call(): pl.pallas_call(kernel, out_shape=tuple(outs) + tuple((shaped(v.shape, v.d...  12.1 us
    ppermute x8, starting transfers between devices, body(): across = lambda v, k: lax.ppermute(v, 'dp', [(i, i ^ k) for i in range(m)])  11.6 us
    ppermute x8, waiting for transfers between devices, body(): across = lambda v, k: lax.ppermute(v, 'dp', [(i, i ^ k) for i in range(m)])  6.46 us
    all_to_all x1, starting transfers between devices, body(): got = lax.all_to_all(msg, 'seq', 0, 0, tiled=True)  4.32 us
  transfers between devices with their start and end apart: 26, of which 14 were waited for; matrix products, arithmetic and copies ran while one was open for 3% of the time, Pallas kernels for 7%

profile of v2, /device:TPU:9, one launch (start us, length us, event | category | flops | bytes accessed | tf_op | source)
XLA Modules:
  0.0 162.4 jit_solution(12564132771069899942)
XLA Ops:
  9.0 1.3 collective-permute-start
  11.4 1.4 collective-permute-start.2
  13.5 1.3 collective-permute-done.refs_1_
  14.8 11.7 %collective-permute-done.1.refs_2_ = bf16[64,1536]{1,0:T(8,128)(2,1)S(1)} collective-permute-done((bf16[64,1536]{1,0:T(8,128)(2,1)S(1)}, bf16[64,1536]{1,0:T(8,128)(2,1)S(1)}, u32[]{:S(2)}, u32[]{:S(2)}) %collective-permute-start.1) | collective-permute-done | bytes 196640 | tf_op jit(solution)/shard_map/ppermute | solution.py:279
  26.5 2.8 %collective-permute-done.2.refs_3_ = bf16[64,1536]{1,0:T(8,128)(2,1)S(1)} collective-permute-done((bf16[64,1536]{1,0:T(8,128)(2,1)S(1)}, bf16[64,1536]{1,0:T(8,128)(2,1)S(1)}, u32[]{:S(2)}, u32[]{:S(2)}) %collective-permute-start.2) | collective-permute-done | bytes 196640 | tf_op jit(solution)/shard_map/ppermute | solution.py:279
  29.4 1.4 copy-done.2
  30.7 1.8 %conv_forward.1 = (bf16[256,384]{1,0:T(8,128)(2,1)S(1)}, f32[256,384]{1,0:T(8,128)S(1)}, f32[256,384]{1,0:T(8,128)S(1)}, bf16[256,1536]{1,0:T(8,128)(2,1)S(1)}) custom-call(bf16[64,1536]{1,0:T(8,128)(2,1)S(1)} %reshape_squeeze.3.refs_0_.own, bf16[64,1536]{1,0:T(8,128)(2,1)S(1)} %collective-permute-done.refs_1_, ...), custom_call_target="tpu_custom_call" | custom-call | tf_op jit(solution)/shard_map/conv_forward/pallas_call | solution.py:22
  34.5 1.5 collective-permute-start.5
  36.8 2.0 %copy-done = bf16[1536,1152]{1,0:T(8,128)(2,1)S(1)} copy-done((bf16[1536,1152]{1,0:T(8,128)(2,1)S(1)}, bf16[1536,1152]{1,0:T(8,128)(2,1)}, u32[]{:S(2)}) %copy-start) | copy-done | bytes 3538968
  38.8 1.5 mid_parts.1
  40.4 10.6 %collective-permute-done.4.refs_2_ = bf16[256,384]{1,0:T(8,128)(2,1)S(1)} collective-permute-done((bf16[256,384]{1,0:T(8,128)(2,1)S(1)}, bf16[256,384]{1,0:T(8,128)(2,1)S(1)}, u32[]{:S(2)}, u32[]{:S(2)}) %collective-permute-start.4) | collective-permute-done | bytes 196640 | tf_op jit(solution)/shard_map/ppermute | solution.py:279
  50.9 1.5 collective-permute-done.5.refs_3_
  56.3 15.3 %all_to_all.10.nms = bf16[8,192,256]{2,1,0:T(8,128)(2,1)} all-to-all(bf16[8,192,256]{2,1,0:T(8,128)(2,1)S(1)} %bitcast.17), channel_id=1, replica_groups=mesh['dp'=8,'seq'=4] {'dp'}, dimensions={0} | all-to-all | bytes 1572864 | tf_op jit(solution)/shard_map/all_to_all | solution.py:317
  72.6 2.5 %copy-done.6 = bf16[8,256,1152]{2,1,0:T(8,128)(2,1)S(1)} copy-done((bf16[8,256,1152]{2,1,0:T(8,128)(2,1)S(1)}, bf16[8,256,1152]{2,1,0:T(8,128)(2,1)}, u32[]{:S(2)}) %copy-start.6) | copy-done | bytes 4718616
  78.3 2.1 %collective-permute-start.10 = (bf16[256,384]{1,0:T(8,128)(2,1)}, bf16[256,384]{1,0:T(8,128)(2,1)S(1)}, u32[]{:S(2)}, u32[]{:S(2)}) collective-permute-start(bf16[256,384]{1,0:T(8,128)(2,1)} %copy-done.23), channel_id=1, source_target_pairs={{0,2},{1,3},{2,0},{3,1},{4,6},{5,7},{6,4},{7,5},{8,10},{9,11},{10,... | collective-permute-start | bytes 589832 | tf_op jit(solution)/shard_map/ppermute | solution.py:279
  80.4 1.4 collective-permute-start.11
  84.0 2.1 %qkv.1 = (bf16[256,1152]{1,0:T(8,128)(2,1)}, f32[8,256]{1,0:T(8,128)S(1)}) custom-call(bf16[1536,256]{1,0:T(8,128)(2,1)S(1)} %copy-done.8, bf16[1536,1152]{1,0:T(8,128)(2,1)S(1)} %copy-done.1, bf16[256,1152]{1,0:T(8,128)(2,1)S(1)} %bitcast.16), custom_call_target="tpu_custom_call" | custom-call | tf_op jit(solution)/shard_map/qkv/pallas_call | solution.py:22
  86.1 2.2 %collective-permute-start.7 = (f32[8,256]{1,0:T(8,128)S(1)}, f32[8,256]{1,0:T(8,128)S(1)}, u32[]{:S(2)}, u32[]{:S(2)}) collective-permute-start(f32[8,256]{1,0:T(8,128)S(1)} %get-tuple-element.46.refs_0_), channel_id=1, source_target_pairs={{0,2},{1,3},{2,0},{3,1},{4,6},{5,7},{6,4},{7,5},{8,10},{9,11},{10,... | collective-permute-start | bytes 24584 | tf_op jit(solution)/shard_map/ppermute | solution.py:279
  88.3 6.2 %collective-permute-done.6.refs_1_ = f32[8,256]{1,0:T(8,128)S(1)} collective-permute-done((f32[8,256]{1,0:T(8,128)S(1)}, f32[8,256]{1,0:T(8,128)S(1)}, u32[]{:S(2)}, u32[]{:S(2)}) %collective-permute-start.6) | collective-permute-done | bytes 8224 | tf_op jit(solution)/shard_map/ppermute | solution.py:279
  94.7 4.3 %collective-permute-done.8.refs_3_ = f32[8,256]{1,0:T(8,128)S(1)} collective-permute-done((f32[8,256]{1,0:T(8,128)S(1)}, f32[8,256]{1,0:T(8,128)S(1)}, u32[]{:S(2)}, u32[]{:S(2)}) %collective-permute-start.8) | collective-permute-done | bytes 8224 | tf_op jit(solution)/shard_map/ppermute | solution.py:279
  99.1 2.2 %conv_backward.1 = (f32[4,240,384]{2,1,0:T(8,128)S(1)}, bf16[4,240,384]{2,1,0:T(8,128)(2,1)}, bf16[256,960]{1,0:T(8,128)(2,1)S(1)}, bf16[256,960]{1,0:T(8,128)(2...) custom-call(f32[8,256]{1,0:T(8,128)S(1)} %get-tuple-element.46.refs_0_, ...), custom_call_target="tpu_custom_call" | custom-call | tf_op jit(solution)/shard_map/conv_backward/pallas_call | solution.py:22
  101.3 1.8 %collective-permute-start.12 = (bf16[4,240,384]{2,1,0:T(8,128)(2,1)}, bf16[4,240,384]{2,1,0:T(8,128)(2,1)S(1)}, u32[]{:S(2)}, u32[]{:S(2)}) collective-permute-start(bf16[4,240,384]{2,1,0:T(8,128)(2,1)} %get-tuple-element.61), channel_id=1, source_target_pairs={{0,4},{4,0},{8,12},{12,8},{16,20},{20,16},{24,28},{28,24},{1,5},{5... | collective-permute-start | bytes 2211848 | tf_op jit(solution)/shard_map/ppermute | solution.py:281
  105.0 4.3 %all-to-all-start = ((bf16[4,64,1920]{2,1,0:T(8,128)(2,1)}), bf16[4,64,1920]{2,1,0:T(8,128)(2,1)S(1)}, u32[]{:S(2)}, u32[]{:S(2)}) async-start(bf16[4,64,1920]{2,1,0:T(8,128)(2,1)} %copy-done.17), calls=%async_computation | async-start | bytes 1966080 | tf_op jit(solution)/shard_map/all_to_all | solution.py:353
  110.8 1.5 collective-permute-start.15
  114.3 16.8 %collective-permute-done.16.refs_5_ = f32[8,384]{1,0:T(8,128)S(1)} collective-permute-done((f32[8,384]{1,0:T(8,128)S(1)}, f32[8,384]{1,0:T(8,128)S(1)}, u32[]{:S(2)}, u32[]{:S(2)}) %collective-permute-start.16) | collective-permute-done | bytes 12320 | tf_op jit(solution)/shard_map/ppermute | solution.py:279
  131.3 2.7 %collective-permute-done.18.refs_7_ = f32[8,384]{1,0:T(8,128)S(1)} collective-permute-done((f32[8,384]{1,0:T(8,128)S(1)}, f32[8,384]{1,0:T(8,128)S(1)}, u32[]{:S(2)}, u32[]{:S(2)}) %collective-permute-start.18) | collective-permute-done | bytes 12320 | tf_op jit(solution)/shard_map/ppermute | solution.py:279
  135.5 1.5 collective-permute-start.21
  136.9 1.9 %collective-permute-done.19.refs_1_ = bf16[256,384]{1,0:T(8,128)(2,1)S(1)} collective-permute-done((bf16[256,384]{1,0:T(8,128)(2,1)S(1)}, bf16[256,384]{1,0:T(8,128)(2,1)S(1)}, u32[]{:S(2)}, u32[]{:S(2)}) %collective-permute-start.19) | collective-permute-done | bytes 196640 | tf_op jit(solution)/shard_map/ppermute | solution.py:281
  138.8 3.7 %collective-permute-done.20.refs_2_ = bf16[256,384]{1,0:T(8,128)(2,1)S(1)} collective-permute-done((bf16[256,384]{1,0:T(8,128)(2,1)S(1)}, bf16[256,384]{1,0:T(8,128)(2,1)S(1)}, u32[]{:S(2)}, u32[]{:S(2)}) %collective-permute-start.20) | collective-permute-done | bytes 196640 | tf_op jit(solution)/shard_map/ppermute | solution.py:281
  142.6 4.3 %collective-permute-start.22 = (bf16[976,384]{1,0:T(8,128)(2,1)S(1)}, bf16[976,384]{1,0:T(8,128)(2,1)S(1)}, u32[]{:S(2)}, u32[]{:S(2)}) collective-permute-start(bf16[976,384]{1,0:T(8,128)(2,1)S(1)} %kernel_grad_half.1.mine), channel_id=1, source_target_pairs={{0,4},{4,0},{8,12},{12,8},{16,20},{20,16},{24,28},{28,24},{1,5},{5... | collective-permute-start | bytes 2248712 | tf_op jit(solution)/shard_map/ppermute | solution.py:281
  148.9 1.3 kernel_grad.1
  151.5 4.1 %copy.29 = bf16[1536,1152]{1,0:T(8,128)(2,1)} copy(bf16[1536,1152]{1,0:T(8,128)(2,1)} %all-gather.5.cloned.1.call-done) | data formatting | bytes 7077888
  (100 shorter events, 27.2 us)
Async XLA Ops:
  7.2 29.6 %copy-start.4 = (bf16[1,256,1152]{2,1,0:T(8,128)(2,1)S(1)}, bf16[1,256,1152]{2,1,0:T(8,128)(2,1)}, u32[]{:S(2)}) copy-start(bf16[1,256,1152]{2,1,0:T(8,128)(2,1)} %param.11) | copy-start | bytes 1769476
  7.2 65.4 %all-gather.3.cloned.1.call-start = ((), (), s32[]{:S(2)}) async-start(), calls=%async_computation.2 | async-start | bytes 5308416 | tf_op jit(solution)/shard_map/all_gather | solution.py:288
  7.9 143.6 %all-gather.5.cloned.1.call-start = ((), (), s32[]{:S(2)}) async-start(), calls=%async_computation.3 | async-start | bytes 3981312 | tf_op jit(solution)/shard_map/all_gather | solution.py:331
  9.0 44.0 %copy-start.13 = (bf16[64,1536]{1,0:T(8,128)(2,1)}, bf16[64,1536]{1,0:T(8,128)(2,1)S(1)}, u32[]{:S(2)}) copy-start(bf16[64,1536]{1,0:T(8,128)(2,1)S(1)} %reshape_squeeze.3.refs_0_.own) | copy-start | bytes 589828
  9.0 5.8 %collective-permute-start = (bf16[64,1536]{1,0:T(8,128)(2,1)S(1)}, bf16[64,1536]{1,0:T(8,128)(2,1)S(1)}, u32[]{:S(2)}, u32[]{:S(2)}) collective-permute-start(bf16[64,1536]{1,0:T(8,128)(2,1)S(1)} %reshape_squeeze.3.refs_0_.own), channel_id=1, source_target_pairs={{0,1},{1,2},{2,3},{3,0},{4,5},{5,6},{6,7},{7,4},{8,9},{9,10},{10,1... | collective-permute-start | bytes 589832 | tf_op jit(solution)/shard_map/ppermute | solution.py:279
  10.3 16.2 %collective-permute-start.1 = (bf16[64,1536]{1,0:T(8,128)(2,1)S(1)}, bf16[64,1536]{1,0:T(8,128)(2,1)S(1)}, u32[]{:S(2)}, u32[]{:S(2)}) collective-permute-start(bf16[64,1536]{1,0:T(8,128)(2,1)S(1)} %reshape_squeeze.3.refs_0_.own), channel_id=1, source_target_pairs={{0,2},{1,3},{2,0},{3,1},{4,6},{5,7},{6,4},{7,5},{8,10},{9,11},{10,... | collective-permute-start | bytes 589832 | tf_op jit(solution)/shard_map/ppermute | solution.py:279
  11.4 17.9 %collective-permute-start.2 = (bf16[64,1536]{1,0:T(8,128)(2,1)S(1)}, bf16[64,1536]{1,0:T(8,128)(2,1)S(1)}, u32[]{:S(2)}, u32[]{:S(2)}) collective-permute-start(bf16[64,1536]{1,0:T(8,128)(2,1)S(1)} %reshape_squeeze.3.refs_0_.own), channel_id=1, source_target_pairs={{0,3},{1,0},{2,1},{3,2},{4,7},{5,4},{6,5},{7,6},{8,11},{9,8},{10,9... | collective-permute-start | bytes 589832 | tf_op jit(solution)/shard_map/ppermute | solution.py:279
  34.2 6.2 %collective-permute-start.3 = (bf16[256,384]{1,0:T(8,128)(2,1)S(1)}, bf16[256,384]{1,0:T(8,128)(2,1)S(1)}, u32[]{:S(2)}, u32[]{:S(2)}) collective-permute-start(bf16[256,384]{1,0:T(8,128)(2,1)S(1)} %get-tuple-element.38.refs_0_), channel_id=1, source_target_pairs={{0,1},{1,2},{2,3},{3,0},{4,5},{5,6},{6,7},{7,4},{8,9},{9,10},{10,1... | collective-permute-start | bytes 589832 | tf_op jit(solution)/shard_map/ppermute | solution.py:279
  34.2 16.7 %collective-permute-start.4 = (bf16[256,384]{1,0:T(8,128)(2,1)S(1)}, bf16[256,384]{1,0:T(8,128)(2,1)S(1)}, u32[]{:S(2)}, u32[]{:S(2)}) collective-permute-start(bf16[256,384]{1,0:T(8,128)(2,1)S(1)} %get-tuple-element.38.refs_0_), channel_id=1, source_target_pairs={{0,2},{1,3},{2,0},{3,1},{4,6},{5,7},{6,4},{7,5},{8,10},{9,11},{10,... | collective-permute-start | bytes 589832 | tf_op jit(solution)/shard_map/ppermute | solution.py:279
  34.5 18.0 %collective-permute-start.5 = (bf16[256,384]{1,0:T(8,128)(2,1)S(1)}, bf16[256,384]{1,0:T(8,128)(2,1)S(1)}, u32[]{:S(2)}, u32[]{:S(2)}) collective-permute-start(bf16[256,384]{1,0:T(8,128)(2,1)S(1)} %get-tuple-element.38.refs_0_), channel_id=1, source_target_pairs={{0,3},{1,0},{2,1},{3,2},{4,7},{5,4},{6,5},{7,6},{8,11},{9,8},{10,9... | collective-permute-start | bytes 589832 | tf_op jit(solution)/shard_map/ppermute | solution.py:279
  40.4 16.0 %copy-start.15 = (f32[256,384]{1,0:T(8,128)}, f32[256,384]{1,0:T(8,128)S(1)}, u32[]{:S(2)}) copy-start(f32[256,384]{1,0:T(8,128)S(1)} %get-tuple-element.51.refs_8_) | copy-start | bytes 1179652
  78.2 20.9 %collective-permute-start.9 = (bf16[256,384]{1,0:T(8,128)(2,1)}, bf16[256,384]{1,0:T(8,128)(2,1)S(1)}, u32[]{:S(2)}, u32[]{:S(2)}) collective-permute-start(bf16[256,384]{1,0:T(8,128)(2,1)} %copy-done.22), channel_id=1, source_target_pairs={{0,1},{1,2},{2,3},{3,0},{4,5},{5,6},{6,7},{7,4},{8,9},{9,10},{10,1... | collective-permute-start | bytes 589832 | tf_op jit(solution)/shard_map/ppermute | solution.py:279
  78.3 20.8 %collective-permute-start.10 = (bf16[256,384]{1,0:T(8,128)(2,1)}, bf16[256,384]{1,0:T(8,128)(2,1)S(1)}, u32[]{:S(2)}, u32[]{:S(2)}) collective-permute-start(bf16[256,384]{1,0:T(8,128)(2,1)} %copy-done.23), channel_id=1, source_target_pairs={{0,2},{1,3},{2,0},{3,1},{4,6},{5,7},{6,4},{7,5},{8,10},{9,11},{10,... | collective-permute-start | bytes 589832 | tf_op jit(solution)/shard_map/ppermute | solution.py:279
  80.4 22.7 %copy-start.3 = (bf16[5,768,192]{1,2,0:T(8,128)(2,1)S(1)}, bf16[5,768,192]{1,2,0:T(8,128)(2,1)}, u32[]{:S(2)}) copy-start(bf16[5,768,192]{1,2,0:T(8,128)(2,1)} %param.7) | copy-start | bytes 4423684
  80.4 18.7 %collective-permute-start.11 = (bf16[256,384]{1,0:T(8,128)(2,1)}, bf16[256,384]{1,0:T(8,128)(2,1)S(1)}, u32[]{:S(2)}, u32[]{:S(2)}) collective-permute-start(bf16[256,384]{1,0:T(8,128)(2,1)} %copy-done.24), channel_id=1, source_target_pairs={{0,3},{1,0},{2,1},{3,2},{4,7},{5,4},{6,5},{7,6},{8,11},{9,8},{10,9... | collective-permute-start | bytes 589832 | tf_op jit(solution)/shard_map/ppermute | solution.py:279
  84.0 15.1 %copy-start.26 = (f32[256,1]{1,0:T(8,128)S(1)}, f32[256,1]{1,0:T(8,128)}, u32[]{:S(2)}) copy-start(f32[256,1]{1,0:T(8,128)} %copy-done.25) | copy-start | bytes 3076
  86.1 8.4 %collective-permute-start.6 = (f32[8,256]{1,0:T(8,128)S(1)}, f32[8,256]{1,0:T(8,128)S(1)}, u32[]{:S(2)}, u32[]{:S(2)}) collective-permute-start(f32[8,256]{1,0:T(8,128)S(1)} %get-tuple-element.46.refs_0_), channel_id=1, source_target_pairs={{0,1},{1,2},{2,3},{3,0},{4,5},{5,6},{6,7},{7,4},{8,9},{9,10},{10,1... | collective-permute-start | bytes 24584 | tf_op jit(solution)/shard_map/ppermute | solution.py:279
  86.1 8.6 %collective-permute-start.7 = (f32[8,256]{1,0:T(8,128)S(1)}, f32[8,256]{1,0:T(8,128)S(1)}, u32[]{:S(2)}, u32[]{:S(2)}) collective-permute-start(f32[8,256]{1,0:T(8,128)S(1)} %get-tuple-element.46.refs_0_), channel_id=1, source_target_pairs={{0,2},{1,3},{2,0},{3,1},{4,6},{5,7},{6,4},{7,5},{8,10},{9,11},{10,... | collective-permute-start | bytes 24584 | tf_op jit(solution)/shard_map/ppermute | solution.py:279
  94.5 4.6 %collective-permute-start.8 = (f32[8,256]{1,0:T(8,128)S(1)}, f32[8,256]{1,0:T(8,128)S(1)}, u32[]{:S(2)}, u32[]{:S(2)}) collective-permute-start(f32[8,256]{1,0:T(8,128)S(1)} %get-tuple-element.46.refs_0_), channel_id=1, source_target_pairs={{0,3},{1,0},{2,1},{3,2},{4,7},{5,4},{6,5},{7,6},{8,11},{9,8},{10,9... | collective-permute-start | bytes 24584 | tf_op jit(solution)/shard_map/ppermute | solution.py:279
  101.3 8.1 %collective-permute-start.12 = (bf16[4,240,384]{2,1,0:T(8,128)(2,1)}, bf16[4,240,384]{2,1,0:T(8,128)(2,1)S(1)}, u32[]{:S(2)}, u32[]{:S(2)}) collective-permute-start(bf16[4,240,384]{2,1,0:T(8,128)(2,1)} %get-tuple-element.61), channel_id=1, source_target_pairs={{0,4},{4,0},{8,12},{12,8},{16,20},{20,16},{24,28},{28,24},{1,5},{5... | collective-permute-start | bytes 2211848 | tf_op jit(solution)/shard_map/ppermute | solution.py:281
  105.0 42.0 %copy-start.14 = (bf16[64,1536]{1,0:T(8,128)(2,1)S(1)}, bf16[64,1536]{1,0:T(8,128)(2,1)}, u32[]{:S(2)}) copy-start(bf16[64,1536]{1,0:T(8,128)(2,1)} %copy-done.13) | copy-start | bytes 589828
  105.0 42.0 %all-to-all-start = ((bf16[4,64,1920]{2,1,0:T(8,128)(2,1)}), bf16[4,64,1920]{2,1,0:T(8,128)(2,1)S(1)}, u32[]{:S(2)}, u32[]{:S(2)}) async-start(bf16[4,64,1920]{2,1,0:T(8,128)(2,1)} %copy-done.17), calls=%async_computation | async-start | bytes 1966080 | tf_op jit(solution)/shard_map/all_to_all | solution.py:353
  109.5 24.6 %collective-permute-start.13 = (bf16[240,384]{1,0:T(8,128)(2,1)S(1)}, bf16[240,384]{1,0:T(8,128)(2,1)S(1)}, u32[]{:S(2)}, u32[]{:S(2)}) collective-permute-start(bf16[240,384]{1,0:T(8,128)(2,1)S(1)} %get-tuple-element.63), channel_id=1, source_target_pairs={{0,8},{4,12},{8,0},{12,4},{16,24},{20,28},{24,16},{28,20},{1,9},{5... | collective-permute-start | bytes 552968 | tf_op jit(solution)/shard_map/ppermute | solution.py:281
  110.6 23.5 %collective-permute-start.14 = (bf16[240,384]{1,0:T(8,128)(2,1)S(1)}, bf16[240,384]{1,0:T(8,128)(2,1)S(1)}, u32[]{:S(2)}, u32[]{:S(2)}) collective-permute-start(bf16[240,384]{1,0:T(8,128)(2,1)S(1)} %get-tuple-element.64), channel_id=1, source_target_pairs={{0,16},{4,20},{8,24},{12,28},{16,0},{20,4},{24,8},{28,12},{1,17},{... | collective-permute-start | bytes 552968 | tf_op jit(solution)/shard_map/ppermute | solution.py:281
  110.8 23.3 %collective-permute-start.15 = (bf16[240,384]{1,0:T(8,128)(2,1)S(1)}, bf16[240,384]{1,0:T(8,128)(2,1)S(1)}, u32[]{:S(2)}, u32[]{:S(2)}) collective-permute-start(bf16[240,384]{1,0:T(8,128)(2,1)S(1)} %get-tuple-element.65), channel_id=1, source_target_pairs={{0,24},{4,28},{8,16},{12,20},{16,8},{20,12},{24,0},{28,4},{1,25},{... | collective-permute-start | bytes 552968 | tf_op jit(solution)/shard_map/ppermute | solution.py:281
  112.2 18.9 %collective-permute-start.16 = (f32[8,384]{1,0:T(8,128)S(1)}, f32[8,384]{1,0:T(8,128)S(1)}, u32[]{:S(2)}, u32[]{:S(2)}) collective-permute-start(f32[8,384]{1,0:T(8,128)S(1)} %get-tuple-element.66.refs_4_), channel_id=1, source_target_pairs={{0,1},{1,2},{2,3},{3,0},{4,5},{5,6},{6,7},{7,4},{8,9},{9,10},{10,1... | collective-permute-start | bytes 36872 | tf_op jit(solution)/shard_map/ppermute | solution.py:279
  113.4 17.9 %collective-permute-start.17 = (f32[8,384]{1,0:T(8,128)S(1)}, f32[8,384]{1,0:T(8,128)S(1)}, u32[]{:S(2)}, u32[]{:S(2)}) collective-permute-start(f32[8,384]{1,0:T(8,128)S(1)} %get-tuple-element.66.refs_4_), channel_id=1, source_target_pairs={{0,2},{1,3},{2,0},{3,1},{4,6},{5,7},{6,4},{7,5},{8,10},{9,11},{10,... | collective-permute-start | bytes 36872 | tf_op jit(solution)/shard_map/ppermute | solution.py:279
  131.1 3.0 %collective-permute-start.18 = (f32[8,384]{1,0:T(8,128)S(1)}, f32[8,384]{1,0:T(8,128)S(1)}, u32[]{:S(2)}, u32[]{:S(2)}) collective-permute-start(f32[8,384]{1,0:T(8,128)S(1)} %get-tuple-element.66.refs_4_), channel_id=1, source_target_pairs={{0,3},{1,0},{2,1},{3,2},{4,7},{5,4},{6,5},{7,6},{8,11},{9,8},{10,9... | collective-permute-start | bytes 36872 | tf_op jit(solution)/shard_map/ppermute | solution.py:279
  134.2 4.6 %collective-permute-start.19 = (bf16[256,384]{1,0:T(8,128)(2,1)S(1)}, bf16[256,384]{1,0:T(8,128)(2,1)S(1)}, u32[]{:S(2)}, u32[]{:S(2)}) collective-permute-start(bf16[256,384]{1,0:T(8,128)(2,1)S(1)} %chip_sum.1.refs_0_), channel_id=1, source_target_pairs={{0,8},{4,12},{8,0},{12,4},{16,24},{20,28},{24,16},{28,20},{1,9},{5... | collective-permute-start | bytes 589832 | tf_op jit(solution)/shard_map/ppermute | solution.py:281
  135.3 7.2 %collective-permute-start.20 = (bf16[256,384]{1,0:T(8,128)(2,1)S(1)}, bf16[256,384]{1,0:T(8,128)(2,1)S(1)}, u32[]{:S(2)}, u32[]{:S(2)}) collective-permute-start(bf16[256,384]{1,0:T(8,128)(2,1)S(1)} %chip_sum.1.refs_0_), channel_id=1, source_target_pairs={{0,16},{4,20},{8,24},{12,28},{16,0},{20,4},{24,8},{28,12},{1,17},{... | collective-permute-start | bytes 589832 | tf_op jit(solution)/shard_map/ppermute | solution.py:281
  135.5 7.1 %collective-permute-start.21 = (bf16[256,384]{1,0:T(8,128)(2,1)S(1)}, bf16[256,384]{1,0:T(8,128)(2,1)S(1)}, u32[]{:S(2)}, u32[]{:S(2)}) collective-permute-start(bf16[256,384]{1,0:T(8,128)(2,1)S(1)} %chip_sum.1.refs_0_), channel_id=1, source_target_pairs={{0,24},{4,28},{8,16},{12,20},{16,8},{20,12},{24,0},{28,4},{1,25},{... | collective-permute-start | bytes 589832 | tf_op jit(solution)/shard_map/ppermute | solution.py:281
  142.6 6.2 %collective-permute-start.22 = (bf16[976,384]{1,0:T(8,128)(2,1)S(1)}, bf16[976,384]{1,0:T(8,128)(2,1)S(1)}, u32[]{:S(2)}, u32[]{:S(2)}) collective-permute-start(bf16[976,384]{1,0:T(8,128)(2,1)S(1)} %kernel_grad_half.1.mine), channel_id=1, source_target_pairs={{0,4},{4,0},{8,12},{12,8},{16,20},{20,16},{24,28},{28,24},{1,5},{5... | collective-permute-start | bytes 2248712 | tf_op jit(solution)/shard_map/ppermute | solution.py:281
  (21 other events, 86.5 us)
Sparse Core Ops, SparseCore 0:
  9.9 40.4 all-gather.2
  78.3 34.0 all-gather.4

commit v3 on v2

v3 whole, which is shorter than its diff:
```python
import functools
import math

import jax
import jax.numpy as jnp
from jax import lax
from jax.experimental import pallas as pl
from jax.experimental.pallas import tpu as pltpu
from jax.sharding import PartitionSpec as P

EPS = 1e-06
WAIT = 4e10
SPARE = 12
F32 = jnp.float32
BF16 = jnp.bfloat16
ANY = pl.BlockSpec(memory_space=pl.ANY)
HBM = pl.BlockSpec(memory_space=pltpu.HBM)
VMEM = pl.BlockSpec(memory_space=pltpu.VMEM)


class In:
    def __init__(self, ref, copy=None):
        self.ref, self.copy = ref, copy
        if copy is not None:
            copy.start()

    def __call__(self):
        if self.copy is not None:
            self.copy.wait()
            self.copy = None
        return self.ref


def shaped(shape, dtype):
    return jax.ShapeDtypeStruct(shape, dtype)


class Far:
    def __init__(self, value):
        self.value = value


def call(kernel, args, outs=(), free=(), kept=(), after=(), near=(), spill=(), scratch=(), flops=0, name=None):
    within = lambda v: pltpu.with_memory_space_constraint(v, pltpu.VMEM)
    near, spill = [within(v) for v in near], [within(v) for v in spill]
    far = [i for i, v in enumerate(args) if isinstance(v, Far)]
    args = [pltpu.with_memory_space_constraint(v.value, pltpu.HBM) if isinstance(v, Far) else v for v in args]
    count, skip = len(args), len(after) + len(near)
    lanes = lambda v: math.prod(v.shape[:-1]) * -(-v.shape[-1] // 128) * 128 * v.dtype.itemsize
    need = sum(map(lanes, [*args, *outs, *free, *scratch]))

    def whole(*refs):
        refs = list(refs)
        take = lambda k: [refs.pop(0) for _ in range(k)]
        ins, _, saved = take(count), take(skip), take(len(spill))
        targets, rest, places = take(len(outs)), take(len(free) + len(kept)), take(len(spill))
        own, landed, made = take(len(scratch)), take(len(far)), take(len(outs))
        in_sems, out_sems = refs
        operands = [In(v) for v in ins]
        for k, i in enumerate(far):
            operands[i] = In(landed[k], pltpu.make_async_copy(ins[i], landed[k], in_sems.at[k]))
        pairs = [*zip(made, targets), *zip(saved, places)]
        copies = [pltpu.make_async_copy(v, t, out_sems.at[k]) for k, (v, t) in enumerate(pairs)]
        gone = [False] * len(made)

        def go(ref):
            k = next(i for i, v in enumerate(made) if v is ref)
            gone[k] = True
            copies[k].start()

        for copy in copies[len(made) :]:
            copy.start()
        kernel(operands, [*made, *rest], go, *own)
        for k, copy in enumerate(copies[: len(made)]):
            if not gone[k]:
                copy.start()
        for v in operands:
            v()
        for copy in copies:
            copy.wait()

    specs = [VMEM] * count
    for i in far:
        specs[i] = HBM
    memory = lambda space, values: [space(v.shape, v.dtype) for v in values]
    return pl.pallas_call(
        whole,
        out_shape=tuple(
            [*memory(pltpu.HBM, outs), *free, *memory(pltpu.VMEM, kept), *memory(pltpu.HBM, spill)]
        ),
        in_specs=specs + [ANY] * len(after) + [VMEM] * (len(near) + len(spill)),
        out_specs=tuple([HBM] * len(outs) + [VMEM] * (len(free) + len(kept)) + [HBM] * len(spill)),
        scratch_shapes=[
            *scratch,
            *memory(pltpu.VMEM, [args[i] for i in far]),
            *memory(pltpu.VMEM, outs),
            pltpu.SemaphoreType.DMA((max(1, len(far)),)),
            pltpu.SemaphoreType.DMA((max(1, len(outs) + len(spill)),)),
        ],
        compiler_params=pltpu.CompilerParams(vmem_limit_bytes=min(56 << 20, need + (SPARE << 20))),
        cost_estimate=pl.CostEstimate(flops=int(flops), bytes_accessed=0, transcendentals=0),
        name=name,
    )(*args, *after, *near, *spill)


def dot(a, b):
    return jnp.dot(a, b, preferred_element_type=F32)


def dot_nt(a, b):
    return lax.dot_general(a, b, (((1,), (1,)), ((), ())), preferred_element_type=F32)


def dot_tn(a, b):
    return lax.dot_general(a, b, (((0,), (0,)), ((), ())), preferred_element_type=F32)


def later(v):
    row = lax.broadcasted_iota(jnp.int32, v.shape, 0)
    return jnp.where(row == 0, 0.0, pltpu.roll(v, 1, 0))


def sooner(v):
    rows = v.shape[0]
    row = lax.broadcasted_iota(jnp.int32, v.shape, 0)
    return jnp.where(row == rows - 1, 0.0, pltpu.roll(v, rows - 1, 0))


def inv_rms(v):
    return lax.rsqrt(jnp.mean(v * v, axis=-1, keepdims=True) + EPS)


def in_two(v):
    high = v.astype(BF16).astype(F32)
    return jnp.concatenate([high, v - high], axis=0).astype(BF16)


def joined(tail):
    rows = tail.shape[0] // 2
    return tail[:rows].astype(F32) + tail[rows:].astype(F32)


def picker(shape, me, c):
    row = lax.broadcasted_iota(jnp.int32, shape, 0)
    col = lax.broadcasted_iota(jnp.int32, shape, 1)
    return jnp.where(row == col + me * c, 1.0, 0.0).astype(BF16)


def mid_kernel(n, c, chans, ins, outs, go):
    me = lax.axis_index("seq")
    cot, w = ins[:2]
    stays = outs[n:]
    g, w = cot()[...], w()
    for k in range(n):
        at = pl.multiple_of(lax.rem(me + k, n) * c, c & -c)
        rows = jnp.concatenate([w[pl.ds(at, c), :], w[pl.ds(chans + at, c), :]], axis=0)
        outs[k][...] = dot_nt(g, rows).astype(BF16)
    for v, stay in zip(ins, stays):
        stay[...] = v()[...]


def conv_kernel_fwd(n, c, chans, ins, outs, go, xs):
    me = lax.axis_index("seq")
    blocks, (taps, gain) = ins[:n], ins[n:]
    pooled_msg, pooled, conv_out, nin, rone = outs
    rows = blocks[0].ref.shape[0]
    gains = gain()[...]
    for k in range(n):
        at = pl.multiple_of(lax.rem(me - k + n, n) * rows, rows)
        v = blocks[k]()[...]
        xs[pl.ds(at, rows), :] = v
        for h in range(2):
            f = v[:, h * chans : (h + 1) * chans].astype(F32)
            r = inv_rms(f)
            rone[pl.ds(at, rows), h : h + 1] = r
            nin[pl.ds(at, rows), h * chans : (h + 1) * chans] = (f * r * gains).astype(BF16)
    nin = nin
    xe, xo = nin[:, :chans], nin[:, chans:]
    taps = taps()
    k0, k1, k2, k3, k4 = (taps[k * c : (k + 1) * c, :] for k in range(5))
    even = dot_nt(xe, k2) + dot_nt(xo, k3) + later(dot_nt(xe, k0) + dot_nt(xo, k1)) + sooner(dot_nt(xe, k4))
    odd = dot_nt(xe, k1) + dot_nt(xo, k2) + later(dot_nt(xo, k0)) + sooner(dot_nt(xe, k3) + dot_nt(xo, k4))
    conv = jnp.concatenate([even, odd], axis=1)
    pick = picker((chans, c), me, c)
    own = jnp.concatenate([dot(xs[:, :chans], pick), dot(xs[:, chans:], pick)], axis=1)
    total = own + conv * jax.nn.sigmoid(conv)
    pooled_msg[...] = total.astype(BF16)
    conv_out[...] = conv
    pooled[...] = total


def qkv_kernel(n, c, chans, ins, outs, go):
    me = lax.axis_index("seq")
    blocks, mids = ins[:n], ins[n : 2 * n]
    gains, cot, w = ins[2 * n :]
    nmt, rtwo, *msgs, qkv, part = outs
    squares = 0.0
    for v in blocks:
        v = v()[...].astype(F32)
        squares = squares + jnp.sum(v * v, axis=1, keepdims=True)
    r = lax.rsqrt(squares * (1.0 / (2 * chans)) + EPS)
    rtwo[...] = r
    gains = gains()
    for k in range(n):
        b = lax.rem(me - k + n, n)
        v = blocks[k]()[...].astype(F32) * r * gains[pl.ds(b, 1), :]
        t = v.T.astype(BF16)
        for h in range(2):
            at = pl.multiple_of(h * chans + b * c, c & -c)
            nmt[pl.ds(at, c), :] = t[h * c : (h + 1) * c, :]
    go(nmt)
    half, wide = mids[0].ref.shape
    q = dot_tn(nmt[...], w()[...])
    row = jnp.sum(q * cot()[...].astype(F32), axis=1, keepdims=True)
    row = jnp.broadcast_to(row, (row.shape[0], 128)).T[:8, :]
    part[...] = row
    if msgs:
        if half < wide:
            row = jnp.concatenate([row, jnp.zeros((8, wide - half), F32)], axis=1)
        for k in range(n):
            msgs[k][:half, :] = mids[k]()[...]
            msgs[k][half:, :] = in_two(row)
            go(msgs[k])
    qkv[...] = q.astype(BF16)


def back_kernel(n, c, chans, m, ins, outs, go, evens, odds, whole):
    seq_at = lax.axis_index("seq")
    core = lax.rem(lax.axis_index("dp"), 2)
    mids, parts = ins[:n], ins[n:-8]
    pooled, rtwo, conv_out, gmid, nin, gin, rone, taps = ins[-8:]
    send, keep, *msgs = outs
    half = rtwo().shape[0]
    r = rtwo()[...]
    atwo = pooled()[...] * r
    conv = conv_out()[...]
    sig = jax.nn.sigmoid(conv)
    slope = sig * (1.0 + conv * (1.0 - sig))
    gains = gmid()[pl.ds(seq_at, 1), :]
    mid, rowsum = 0.0, 0.0
    for v in mids:
        mid = mid + v()[:half, :].astype(F32)
    if parts:
        for v in parts:
            rowsum = rowsum + v()[...]
    else:
        for v in mids:
            rowsum = rowsum + joined(v()[half:, :])[:, :half]
    mean = jnp.concatenate([rowsum] * 16, axis=0).T[:, :1] * (1.0 / (2 * chans))
    section = r * (gains * mid - atwo * mean)
    cg = section * slope
    cg = cg.astype(BF16).astype(F32)
    ge, gd = cg[:, :c], cg[:, c:]
    bf = lambda v: v.astype(BF16)
    g0, gp, gm = bf(ge), bf(sooner(ge)), bf(later(ge))
    o0, op, om = bf(gd), bf(sooner(gd)), bf(later(gd))
    evens[...] = jnp.concatenate((gp, o0, g0, om, gm), axis=1)
    odds[...] = jnp.concatenate((op, gp, o0, g0, om), axis=1)
    wide, rows = chans // 2, 5 * c // (m // 2)
    nin = nin()
    for out, which in ((send, 1 - core), (keep, core)):
        at = pl.multiple_of(which * wide, wide & -wide)
        kg = dot_tn(evens[...], nin[:, pl.ds(at, wide)]) + dot_tn(odds[...], nin[:, pl.ds(chans + at, wide)])
        for q in range(m // 2):
            out[q] = kg[q * rows : (q + 1) * rows, :].astype(out.dtype)
        go(out)
    width = 2 * chans
    block = half // n
    gin, rone, taps = gin()[...], rone()[...], taps()[...]
    pick = picker((chans, c), seq_at, c)
    grad = section.astype(BF16)
    acc = 0.0
    lane = lax.broadcasted_iota(jnp.int32, (half, 128), 1)
    means = jnp.zeros((half, 128), F32)
    for h, g in ((0, evens), (1, odds)):
        ng = dot(g[...], taps)
        aone = nin[:, h * chans : (h + 1) * chans].astype(F32) / gin
        acc = acc + jnp.sum(ng * aone, axis=0, keepdims=True)
        placed = dot_nt(grad[:, h * c : (h + 1) * c], pick)
        means = jnp.where(lane == h, jnp.mean(placed * aone, axis=1, keepdims=True), means)
        total = (placed + rone[:, h : h + 1] * gin * ng).astype(BF16)
        whole[:, h * chans : (h + 1) * chans] = total
    whole[:, width : width + 128] = means.astype(BF16)
    mid = jnp.sum(mid * atwo, axis=0, keepdims=True)
    short = -2 * c % 128
    if short:
        mid = jnp.concatenate([mid, jnp.zeros((1, short), F32)], axis=1)
    line = lax.broadcasted_iota(jnp.int32, (16, 128), 0)
    gains = jnp.zeros((16, 128), F32)
    vector = jnp.concatenate([acc, mid], axis=1)
    for i in range(vector.shape[1] // 128):
        gains = jnp.where(line == i, vector[:, i * 128 : (i + 1) * 128], gains)
    gains = in_two(gains)
    for k in range(n):
        at = pl.multiple_of(lax.rem(seq_at + k, n) * block, block)
        msgs[k][:, : width + 128] = whole[pl.ds(at, block), :]
        msgs[k][:, width + 128 :] = jnp.zeros((block, 128), BF16)
        msgs[k][:32, width + 128 :] = gains
        go(msgs[k])


def weight_kernel(m, scale, ins, outs, go):
    nms, cots = ins
    nms, cots = nms(), cots()
    half = nms.shape[2]
    total = dot(nms[0], cots[:half, :])
    for b in range(1, m):
        total = total + dot(nms[b], cots[b * half : (b + 1) * half, :])
    total = (total * scale).astype(BF16)
    for q in range(m // 2):
        outs[0][q] = total


def split_kernel(q, ins, outs, go):
    keep, recv = ins
    me = lax.axis_index("dp") // 2
    keep, recv = keep(), recv()
    for k in [*range(1, q), 0]:
        out = outs[k - 1]
        out[...] = (keep[me ^ k] + recv[me ^ k].astype(F32)).astype(out.dtype)


def finish_kernel(n, chans, scale, ins, outs, go):
    total = ins[0]()[...]
    for r in ins[1:-1]:
        total = total + r()[...].astype(F32)
    rows, wide = total.shape
    outs[0][:rows, :] = (total * scale).astype(BF16)
    gains = ins[-1]()
    pieces, count = wide // 128, chans // 128
    both = gains[0]
    for b in range(1, n):
        both = both + gains[b]
    line = lax.broadcasted_iota(jnp.int32, (8, wide), 0)
    tail = jnp.zeros((8, wide), F32)
    wanted = [(i, both, i * pieces) for i in range(2)] + [(2 + b, gains[b], count) for b in range(n)]
    for i, source, first in wanted:
        row = jnp.concatenate([source[first + j : first + j + 1, :] for j in range(pieces)], axis=1)
        tail = jnp.where(line == i, row, tail)
    outs[0][rows:, :] = in_two(tail * scale)


def half_kernel(q, ins, outs, go):
    me = lax.axis_index("dp") // 2
    out = outs[0]
    rows = ins[0].ref.shape[0] - 16
    tail = 0.0
    for k in range(q):
        at = pl.multiple_of((me ^ k) * rows, rows & -rows)
        out[pl.ds(at, rows), :] = ins[k]()[:rows, :]
        tail = tail + joined(ins[k]()[rows:, :])
    out[q * rows :, :] = in_two(tail)


def place_kernel(n, c, ins, outs, go):
    core = lax.rem(lax.axis_index("dp"), 2)
    mine, other = ins
    taps, gain_in, gain_mid = outs
    rows, wide = taps.shape[0], mine.ref.shape[1]
    total = 0.0
    for v, which in ((mine, core), (other, 1 - core)):
        side = pl.multiple_of(which * wide, wide & -wide)
        taps[:, pl.ds(side, wide)] = v()[:rows, :]
        total = total + joined(v()[rows:, :])
    gain_in[...] = total[:2, :]
    gain_mid[...] = total[2 : 2 + n, : 2 * c]


def hand_kernel(ins, outs, go):
    outs[0][...] = ins[0]()[...]


def weave_kernel(ins, outs, go):
    core = lax.rem(lax.axis_index("dp"), 2)
    mine, other = ins
    for v, which in ((mine, core), (other, 1 - core)):
        for q in range(v.ref.shape[0]):
            outs[0][q, which] = v()[q]


def input_kernel(n, chans, ins, outs, go):
    me = lax.axis_index("seq")
    got, own = ins[:n], ins[n]
    out, gains = outs
    total = got[0]()[:, : 2 * chans + 128].astype(F32)
    for v in got[1:]:
        total = total + v()[:, : 2 * chans + 128].astype(F32)
    for k in range(n):
        gains[lax.rem(me - k + n, n)] = joined(got[k]()[:32, 2 * chans + 128 :])
    for h in range(2):
        x = own()[:, h * chans : (h + 1) * chans].astype(F32)
        a = x * inv_rms(x)
        t = total[:, h * chans : (h + 1) * chans]
        mean = total[:, 2 * chans + h : 2 * chans + h + 1]
        v = t - a * (jnp.mean(t * a, axis=-1, keepdims=True) - mean)
        out[:, h * chans : (h + 1) * chans] = v.astype(BF16)


def body(section_input, conv_kernel, qkv_weight, gain_in, gain_mid, qkv_cotangent):
    x = section_input[0]
    cot = qkv_cotangent[0]
    length, chans = x.shape
    c = conv_kernel.shape[2]
    width, cols = qkv_weight.shape
    n, m = lax.axis_size("seq"), lax.axis_size("dp")
    half = length // 2 * n
    scale = 1.0 / math.sqrt(m * half)
    shift = lambda v, k: lax.ppermute(v, "seq", [(i, (i + k) % n) for i in range(n)])
    from_ring = lambda v: [v] + [shift(v, k) for k in range(1, n)]
    across = lambda v, k: lax.ppermute(v, "dp", [(i, i ^ k) for i in range(m)])
    same_core = [[i for i in range(m) if i % 2 == core] for core in range(2)]
    chips = m // 2
    rows, wide = 5 * c // chips, chans // 2

    taps = conv_kernel.transpose(0, 2, 1)
    own = x.reshape(length // 2, width)
    xs = from_ring(own)
    gin = gain_in.reshape(1, chans)
    gmid = gain_mid.reshape(2, n, c).transpose(1, 0, 2).reshape(n, 2 * c)
    cots = lax.all_gather(cot, "dp", axis=0, tiled=True)
    used = [cot, qkv_weight, taps.reshape(5 * c, chans), gin, gmid]
    held = call(
        functools.partial(mid_kernel, n, c, chans),
        [*map(Far, used)],
        kept=[shaped((half, 2 * c), BF16)] * n + [shaped(v.shape, v.dtype) for v in used],
        name="mid_parts",
    )
    mid_msgs = held[:n]
    cot, weight, taps, gin, gmid = held[n:]
    pooled_msg, *states = call(
        functools.partial(conv_kernel_fwd, n, c, chans),
        [*xs, taps, gin],
        free=[shaped((half, 2 * c), BF16)],
        kept=[
            shaped((half, 2 * c), F32),
            shaped((half, 2 * c), F32),
            shaped((half, width), BF16),
            shaped((half, 2), F32),
        ],
        scratch=[pltpu.VMEM((half, width), BF16)],
        name="conv_forward",
    )
    blocks = from_ring(pooled_msg)
    rides = half <= 2 * c
    nmt, rtwo, *tailed, qkv, part, pooled, conv_out, nin, rone = call(
        functools.partial(qkv_kernel, n, c, chans),
        [*blocks, *mid_msgs, gmid, cot, weight],
        outs=[shaped((width, half), BF16), shaped((half, 1), F32)] + [shaped((half + 16, 2 * c), BF16)] * (n * rides),
        free=[shaped((half, cols), BF16), shaped((8, half), F32)],
        spill=states,
        name="qkv",
    )
    mid_msgs = tailed if rides else mid_msgs
    mids = [Far(mid_msgs[0])] + [shift(mid_msgs[k], k) for k in range(1, n)]
    parts = [] if rides else from_ring(part)
    nms = lax.all_to_all(nmt.reshape(m, width // m, half), "dp", 0, 0, tiled=True)
    (wshare,) = call(
        functools.partial(weight_kernel, m, scale),
        [nms, Far(cots)],
        outs=[shaped((chips, width // m, cols), BF16)],
        name="weight_share",
    )
    whalf = lax.all_to_all(wshare, "dp", 0, 0, axis_index_groups=same_core, tiled=True)
    send, keep, *msgs = call(
        functools.partial(back_kernel, n, c, chans, m),
        [
            *mids,
            *parts,
            *map(Far, [pooled, rtwo, conv_out]),
            gmid,
            Far(nin),
            gin,
            Far(rone),
            taps,
        ],
        outs=[
            shaped((chips, rows, wide), BF16),
            shaped((chips, rows, wide), F32),
        ]
        + [shaped((half // n, width + 256), BF16)] * n,
        after=[wshare],
        scratch=[
            pltpu.VMEM((half, 5 * c), BF16),
            pltpu.VMEM((half, 5 * c), BF16),
            pltpu.VMEM((half, width + 128), BF16),
        ],
        flops=WAIT,
        name="conv_backward",
    )
    got = [msgs[0]] + [shift(msgs[k], k) for k in range(1, n)]
    input_grad, gains = call(
        functools.partial(input_kernel, n, chans),
        [*got, own],
        free=[shaped((length // 2, width), BF16), shaped((n, 16, 128), F32)],
        name="input_grad",
    )
    *split, keep_sum = call(
        functools.partial(split_kernel, chips),
        [Far(keep), across(send, 1)],
        free=[shaped((rows, wide), BF16)] * (chips - 1),
        kept=[shaped((rows, wide), F32)],
        name="core_sum",
    )
    if rows % 16 == 0 and n <= 6:
        (kshare,) = call(
            functools.partial(finish_kernel, n, chans, scale),
            [keep_sum] + [across(split[k - 1], 2 * k) for k in range(1, chips)] + [gains],
            free=[shaped((rows + 16, wide), BF16)],
            name="chip_sum",
        )
        kshares = [kshare] + [across(kshare, k) for k in range(2, m, 2)]
        last = kshares[1]
        (mine,) = call(
            functools.partial(half_kernel, chips),
            kshares,
            free=[shaped((5 * c + 16, wide), BF16)],
            name="kernel_grad_half",
        )
        taps_grad, gain_in_grad, gain_mid_grad = call(
            functools.partial(place_kernel, n, c),
            [mine, across(mine, 1)],
            free=[shaped((5 * c, chans), BF16), shaped((2, wide), F32), shaped((n, 2 * c), F32)],
            name="kernel_grad",
        )
    else:
        core = lax.axis_index("dp") % 2
        both = jnp.stack([keep, send.astype(F32)])
        both = jnp.where(core == 0, both, both[::-1]).transpose(1, 2, 0, 3).reshape(5 * c, chans)
        both, gains = lax.psum((both, gains), "dp")
        taps_grad, gains = (both * scale).astype(BF16), gains * scale
        gain_in_grad = jnp.sum(gains[:, : chans // 128], axis=0)
        gain_mid_grad = gains[:, chans // 128 :].reshape(n, -1)[:, : 2 * c]
        last = gains
    (whalf,) = call(hand_kernel, [whalf], free=[shaped(whalf.shape, BF16)], after=[last], name="weight_grad_half")
    (weight_grad,) = call(
        weave_kernel,
        [whalf, across(whalf, 1)],
        free=[shaped((chips, 2, width // m, cols), BF16)],
        name="weight_grad",
    )
    return (
        qkv[None],
        input_grad.reshape(1, length, chans),
        taps_grad.reshape(5, c, chans).transpose(0, 2, 1),
        gain_in_grad.reshape(chans),
        gain_mid_grad.reshape(n, 2, c).transpose(1, 0, 2).reshape(width),
        weight_grad.reshape(width, cols),
    )


def solution(mesh):
    placed = (
        P("dp", "seq", None),
        P(None, None, "seq"),
        P(None, "seq"),
        P(),
        P(),
        P("dp", None, "seq"),
    )
    return jax.shard_map(
        body,
        mesh=mesh,
        in_specs=placed,
        out_specs=(
            P("dp", None, "seq"),
            P("dp", "seq", None),
            P(None, None, "seq"),
            P(),
            P(),
            P(None, "seq"),
        ),
        check_vma=False,
    )
```

time: 165 us -> 148 us (0.90)
  Pallas kernels: 12.1 us -> 28.8 us
  blocking collectives: 15.3 us -> 0 us
  local copies, waits for them, and re-layouts: 25.6 us -> 10.5 us
  waiting for transfers between devices: 65.6 us -> 58.3 us
  starting transfers between devices: 29.4 us -> 34.7 us
    ppermute x15 -> x12, waiting for transfers between devices: 58.5 us -> 40.1 us  [body(): lax.ppermute(v, 'seq', [(i, (i + k) % n) for i in range(n)])]
    unnamed x55 -> x22, local copies, waits for them, and re-layouts: 20.9 us -> 3.69 us
    pallas_call x12, Pallas kernels: 12.1 us -> 28.8 us  [call(): pl.pallas_call(whole, out_shape=tuple([*memory(pltpu.HBM, outs), *free, *...]
    all_to_all x1 -> x0, blocking collectives: 15.3 us -> none  [body(): lax.all_to_all(nmt.reshape(m, width // m, half), 'dp', 0, 0, tiled=True)]
    all_to_all x1 -> x2, waiting for transfers between devices: 0.01 us -> 5.6 us  [the longest x1 5.59 us: body(): lax.all_to_all(nmt.reshape(m, width // m, half), 'dp', 0, 0, tiled=True)]
    ppermute x8 -> x9, waiting for transfers between devices: 6.46 us -> 11.9 us  [body(): across = lambda v, k: lax.ppermute(v, 'dp', [(i, i ^ k) for i in range(m)])]
    all_to_all x1 -> x2, starting transfers between devices: 4.32 us -> 9.01 us  [the longest x1 4.79 us: body(): lax.all_to_all(wshare, 'dp', 0, 0, axis_index_groups=same_core, tiled=True)]
    ppermute x8 -> x9, starting transfers between devices: 11.6 us -> 13.7 us  [body(): across = lambda v, k: lax.ppermute(v, 'dp', [(i, i ^ k) for i in range(m)])]
  transfers between devices with their start and end apart: 26 -> 24, of which waited for: 14 -> 14; matrix products, arithmetic and copies ran while one was open for 3% -> 5% of each run, Pallas kernels for 7% -> 17%
where the time goes in v3:
time: 148 us; the launch traced here: 146 us
  waiting for transfers between devices  58.3 us (39%)
  starting transfers between devices  34.7 us (23%)
  Pallas kernels  28.8 us (19%)
  between operations  14.3 us (10%)
  local copies, waits for them, and re-layouts  10.5 us (7%)
    ppermute x12, waiting for transfers between devices, body(): lax.ppermute(v, 'seq', [(i, (i + k) % n) for i in range(n)])  40.1 us
    pallas_call x12, Pallas kernels, call(): pl.pallas_call(whole, out_shape=tuple([*memory(pltpu.HBM, outs), *free, *...  28.8 us
    ppermute x9, starting transfers between devices, body(): across = lambda v, k: lax.ppermute(v, 'dp', [(i, i ^ k) for i in range(m)])  13.7 us
    ppermute x12, starting transfers between devices, body(): lax.ppermute(v, 'seq', [(i, (i + k) % n) for i in range(n)])  11.9 us
    ppermute x9, waiting for transfers between devices, body(): across = lambda v, k: lax.ppermute(v, 'dp', [(i, i ^ k) for i in range(m)])  11.9 us
    all_to_all x1, waiting for transfers between devices, body(): lax.all_to_all(nmt.reshape(m, width // m, half), 'dp', 0, 0, tiled=True)  5.59 us
    all_to_all x1, starting transfers between devices, body(): lax.all_to_all(wshare, 'dp', 0, 0, axis_index_groups=same_core, tiled=True)  4.79 us
    all_to_all x1, starting transfers between devices, body(): lax.all_to_all(nmt.reshape(m, width // m, half), 'dp', 0, 0, tiled=True)  4.22 us
  transfers between devices with their start and end apart: 24, of which 14 were waited for; matrix products, arithmetic and copies ran while one was open for 5% of the time, Pallas kernels for 17%

profile of v3, /device:TPU:9, one launch (start us, length us, event | category | flops | bytes accessed | tf_op | source)
XLA Modules:
  0.0 146.5 jit_solution(3007648911018950725)
XLA Ops:
  11.4 1.4 collective-permute-start.2
  15.5 4.2 %mid_parts.1 = (bf16[256,384]{1,0:T(8,128)(2,1)S(1)}, bf16[256,384]{1,0:T(8,128)(2,1)S(1)}, bf16[256,384]{1,0:T(8,128)(2,1)S(1)}, bf16[256,384]{1,0:T(8,128)(2,1...) custom-call(bf16[256,1152]{1,0:T(8,128)(2,1)} %bitcast.17, ...), custom_call_target="tpu_custom_call" | custom-call | tf_op jit(solution)/shard_map/mid_parts/pallas_call | solution.py:86
  19.7 6.8 %collective-permute-done.1.refs_2_ = bf16[64,1536]{1,0:T(8,128)(2,1)S(1)} collective-permute-done((bf16[64,1536]{1,0:T(8,128)(2,1)S(1)}, bf16[64,1536]{1,0:T(8,128)(2,1)S(1)}, u32[]{:S(2)}, u32[]{:S(2)}) %collective-permute-start.1) | collective-permute-done | bytes 196640 | tf_op jit(solution)/shard_map/ppermute | solution.py:408
  26.5 2.8 %collective-permute-done.2.refs_3_ = bf16[64,1536]{1,0:T(8,128)(2,1)S(1)} collective-permute-done((bf16[64,1536]{1,0:T(8,128)(2,1)S(1)}, bf16[64,1536]{1,0:T(8,128)(2,1)S(1)}, u32[]{:S(2)}, u32[]{:S(2)}) %collective-permute-start.2) | collective-permute-done | bytes 196640 | tf_op jit(solution)/shard_map/ppermute | solution.py:408
  29.3 1.9 %conv_forward.1 = (bf16[256,384]{1,0:T(8,128)(2,1)S(1)}, f32[256,384]{1,0:T(8,128)S(1)}, f32[256,384]{1,0:T(8,128)S(1)}, bf16[256,1536]{1,0:T(8,128)(2,1)S(1)}, f32[256,2]{1,0:T(8,128)S(1)}) custom-call(bf16[64,1536]{1,0:T(8,128)(2,1)S(1)} %reshape_squeeze.3.refs_0_.refs_4_, bf16[64,1536]{1,0:T(8,128)(2,1)S(1)} %collective-permute-done.refs_1_, ...), custom_call_target="tpu_custom_call" | custom-call | tf_op jit(solution)/shard_map/conv_forward/pallas_call | solution.py:86
  31.6 1.4 collective-permute-start.5
  33.0 4.4 %collective-permute-done.3.refs_1_ = bf16[256,384]{1,0:T(8,128)(2,1)S(1)} collective-permute-done((bf16[256,384]{1,0:T(8,128)(2,1)S(1)}, bf16[256,384]{1,0:T(8,128)(2,1)S(1)}, u32[]{:S(2)}, u32[]{:S(2)}) %collective-permute-start.3) | collective-permute-done | bytes 196640 | tf_op jit(solution)/shard_map/ppermute | solution.py:408
  37.3 10.7 %collective-permute-done.4.refs_2_ = bf16[256,384]{1,0:T(8,128)(2,1)S(1)} collective-permute-done((bf16[256,384]{1,0:T(8,128)(2,1)S(1)}, bf16[256,384]{1,0:T(8,128)(2,1)S(1)}, u32[]{:S(2)}, u32[]{:S(2)}) %collective-permute-start.4) | collective-permute-done | bytes 196640 | tf_op jit(solution)/shard_map/ppermute | solution.py:408
  48.0 1.5 %collective-permute-done.5.refs_3_ = bf16[256,384]{1,0:T(8,128)(2,1)S(1)} collective-permute-done((bf16[256,384]{1,0:T(8,128)(2,1)S(1)}, bf16[256,384]{1,0:T(8,128)(2,1)S(1)}, u32[]{:S(2)}, u32[]{:S(2)}) %collective-permute-start.5) | collective-permute-done | bytes 196640 | tf_op jit(solution)/shard_map/ppermute | solution.py:408
  49.5 4.1 %qkv.1 = (bf16[1536,256]{1,0:T(8,128)(2,1)}, f32[256,1]{1,0:T(8,128)}, bf16[272,384]{1,0:T(8,128)(2,1)}, bf16[272,384]{1,0:T(8,128)(2,1)}, bf16[272,384]{1,0:T(8...) custom-call(bf16[256,384]{1,0:T(8,128)(2,1)S(1)} %get-tuple-element., ...), custom_call_target="tpu_custom_call" | custom-call | tf_op jit(solution)/shard_map/qkv/pallas_call | solution.py:86
  53.6 4.2 %all-to-all-start = ((bf16[8,192,256]{2,1,0:T(8,128)(2,1)}), bf16[8,192,256]{2,1,0:T(8,128)(2,1)S(1)}, u32[]{:S(2)}, u32[]{:S(2)}) async-start(bf16[8,192,256]{2,1,0:T(8,128)(2,1)} %bitcast.19), calls=%async_computation | async-start | bytes 1572864 | tf_op jit(solution)/shard_map/all_to_all | solution.py:456
  57.9 2.1 %collective-permute-start.7 = (bf16[272,384]{1,0:T(8,128)(2,1)}, bf16[272,384]{1,0:T(8,128)(2,1)}, u32[]{:S(2)}, u32[]{:S(2)}) collective-permute-start(bf16[272,384]{1,0:T(8,128)(2,1)} %get-tuple-element.63), channel_id=1, source_target_pairs={{0,2},{1,3},{2,0},{3,1},{4,6},{5,7},{6,4},{7,5},{8,10},{9,11},{10,... | collective-permute-start | bytes 626696 | tf_op jit(solution)/shard_map/ppermute | solution.py:408
  59.9 1.4 collective-permute-start.8
  61.4 5.6 %all-to-all-done.refs_0_ = bf16[8,192,256]{2,1,0:T(8,128)(2,1)S(1)} async-done(((bf16[8,192,256]{2,1,0:T(8,128)(2,1)}), bf16[8,192,256]{2,1,0:T(8,128)(2,1)S(1)}, u32[]{:S(2)}, u32[]{:S(2)}) %all-to-all-start) | async-done | bytes 786464 | tf_op jit(solution)/shard_map/all_to_all | solution.py:456
  67.0 4.8 %weight_share.1.refs_12_ = bf16[4,192,1152]{2,1,0:T(8,128)(2,1)} custom-call(bf16[8,192,256]{2,1,0:T(8,128)(2,1)S(1)} %all-to-all-done.refs_0_, bf16[2048,1152]{1,0:T(8,128)(2,1)} %bitcast.15), custom_call_target="tpu_custom_call" | custom-call | tf_op jit(solution)/shard_map/weight_share/pallas_call | solution.py:86
  71.8 4.8 %all-to-all-start.1 = ((bf16[4,192,1152]{2,1,0:T(8,128)(2,1)}), bf16[4,192,1152]{2,1,0:T(8,128)(2,1)S(1)}, u32[]{:S(2)}, u32[]{:S(2)}) async-start(bf16[4,192,1152]{2,1,0:T(8,128)(2,1)} %weight_share.1.refs_12_), calls=%async_computation.1 | async-start | bytes 3538944 | tf_op jit(solution)/shard_map/all_to_all | solution.py:463
  76.6 2.8 %collective-permute-done.8.refs_3_ = bf16[272,384]{1,0:T(8,128)(2,1)} collective-permute-done((bf16[272,384]{1,0:T(8,128)(2,1)}, bf16[272,384]{1,0:T(8,128)(2,1)}, u32[]{:S(2)}, u32[]{:S(2)}) %collective-permute-start.8) | collective-permute-done | bytes 208928 | tf_op jit(solution)/shard_map/ppermute | solution.py:408
  80.7 6.8 %conv_backward.1 = (bf16[4,240,384]{2,1,0:T(8,128)(2,1)}, f32[4,240,384]{2,1,0:T(8,128)}, bf16[64,1792]{1,0:T(8,128)(2,1)}, bf16[64,1792]{1,0:T(8,128)(2,1)}, bf...) custom-call(bf16[272,384]{1,0:T(8,128)(2,1)} %get-tuple-element.61.refs_0_, ...), custom_call_target="tpu_custom_call" | custom-call | flops 40000000000 | tf_op jit(solution)/shard_map/conv_backward/pallas_call | solution.py:86
  89.4 1.5 collective-permute-start.9
  90.8 1.6 %core_sum.1 = (bf16[240,384]{1,0:T(8,128)(2,1)S(1)}, bf16[240,384]{1,0:T(8,128)(2,1)S(1)}, bf16[240,384]{1,0:T(8,128)(2,1)S(1)}, f32[240,384]{1,0:T(8,128)S(1)}) custom-call(f32[4,240,384]{2,1,0:T(8,128)} %get-tuple-element.76.refs_0_, bf16[4,240,384]{2,1,0:T(8,128)(2,1)S(1)} %collective-permute-done.12.refs_1_), custom_call_target="tpu_custom_call" | custom-call | tf_op jit(solution)/shard_map/core_sum/pallas_call | solution.py:86
  92.4 1.7 %collective-permute-start.13 = (bf16[240,384]{1,0:T(8,128)(2,1)S(1)}, bf16[240,384]{1,0:T(8,128)(2,1)S(1)}, u32[]{:S(2)}, u32[]{:S(2)}) collective-permute-start(bf16[240,384]{1,0:T(8,128)(2,1)S(1)} %get-tuple-element.79), channel_id=1, source_target_pairs={{0,8},{4,12},{8,0},{12,4},{16,24},{20,28},{24,16},{28,20},{1,9},{5... | collective-permute-start | bytes 552968 | tf_op jit(solution)/shard_map/ppermute | solution.py:410
  95.3 8.5 %collective-permute-done.10.refs_2_ = bf16[64,1792]{1,0:T(8,128)(2,1)S(1)} collective-permute-done((bf16[64,1792]{1,0:T(8,128)(2,1)}, bf16[64,1792]{1,0:T(8,128)(2,1)S(1)}, u32[]{:S(2)}, u32[]{:S(2)}) %collective-permute-start.10) | collective-permute-done | bytes 229408 | tf_op jit(solution)/shard_map/ppermute | solution.py:408
  103.8 2.3 %collective-permute-start.15 = (bf16[240,384]{1,0:T(8,128)(2,1)S(1)}, bf16[240,384]{1,0:T(8,128)(2,1)S(1)}, u32[]{:S(2)}, u32[]{:S(2)}) collective-permute-start(bf16[240,384]{1,0:T(8,128)(2,1)S(1)} %get-tuple-element.81), channel_id=1, source_target_pairs={{0,24},{4,28},{8,16},{12,20},{16,8},{20,12},{24,0},{28,4},{1,25},{... | collective-permute-start | bytes 552968 | tf_op jit(solution)/shard_map/ppermute | solution.py:410
  106.1 2.1 %collective-permute-done.11.refs_3_ = bf16[64,1792]{1,0:T(8,128)(2,1)S(1)} collective-permute-done((bf16[64,1792]{1,0:T(8,128)(2,1)}, bf16[64,1792]{1,0:T(8,128)(2,1)S(1)}, u32[]{:S(2)}, u32[]{:S(2)}) %collective-permute-start.11) | collective-permute-done | bytes 229408 | tf_op jit(solution)/shard_map/ppermute | solution.py:408
  110.6 1.4 collective-permute-start.16
  112.1 3.7 %collective-permute-done.16.refs_1_ = bf16[256,384]{1,0:T(8,128)(2,1)S(1)} collective-permute-done((bf16[256,384]{1,0:T(8,128)(2,1)S(1)}, bf16[256,384]{1,0:T(8,128)(2,1)S(1)}, u32[]{:S(2)}, u32[]{:S(2)}) %collective-permute-start.16) | collective-permute-done | bytes 196640 | tf_op jit(solution)/shard_map/ppermute | solution.py:410
  117.5 2.3 %collective-permute-start.20 = (bf16[4,192,1152]{2,1,0:T(8,128)(2,1)S(1)}, bf16[4,192,1152]{2,1,0:T(8,128)(2,1)}, u32[]{:S(2)}, u32[]{:S(2)}) collective-permute-start(bf16[4,192,1152]{2,1,0:T(8,128)(2,1)S(1)} %weight_grad_half.1.refs_0_), channel_id=1, source_target_pairs={{0,4},{4,0},{8,12},{12,8},{16,20},{20,16},{24,28},{28,24},{1,5},{5... | collective-permute-start | bytes 5308424 | tf_op jit(solution)/shard_map/ppermute | solution.py:410
  119.8 1.4 collective-permute-start.17
  122.4 7.4 %collective-permute-done.17.refs_2_ = bf16[256,384]{1,0:T(8,128)(2,1)S(1)} collective-permute-done((bf16[256,384]{1,0:T(8,128)(2,1)S(1)}, bf16[256,384]{1,0:T(8,128)(2,1)S(1)}, u32[]{:S(2)}, u32[]{:S(2)}) %collective-permute-start.17) | collective-permute-done | bytes 196640 | tf_op jit(solution)/shard_map/ppermute | solution.py:410
  129.9 1.7 %collective-permute-start.19 = (bf16[976,384]{1,0:T(8,128)(2,1)S(1)}, bf16[976,384]{1,0:T(8,128)(2,1)S(1)}, u32[]{:S(2)}, u32[]{:S(2)}) collective-permute-start(bf16[976,384]{1,0:T(8,128)(2,1)S(1)} %kernel_grad_half.1.refs_0_), channel_id=1, source_target_pairs={{0,4},{4,0},{8,12},{12,8},{16,20},{20,16},{24,28},{28,24},{1,5},{5... | collective-permute-start | bytes 2248712 | tf_op jit(solution)/shard_map/ppermute | solution.py:410
  131.5 1.7 %reshape.50 = bf16[1,128,768]{2,1,0:T(8,128)(2,1)} reshape(bf16[64,1536]{1,0:T(8,128)(2,1)} %copy-done.10) | data formatting | bytes 393216 | tf_op jit(solution)/shard_map/reshape | solution.py:543
  136.1 3.6 %weight_grad.1 = bf16[4,2,192,1152]{3,2,1,0:T(8,128)(2,1)} custom-call(bf16[4,192,1152]{2,1,0:T(8,128)(2,1)S(1)} %weight_grad_half.1.refs_0_, bf16[4,192,1152]{2,1,0:T(8,128)(2,1)} %collective-permute-done.20.refs_1_), custom_call_target="tpu_custom_call" | custom-call | tf_op jit(solution)/shard_map/weight_grad/pallas_call | solution.py:86
  (61 shorter events, 20.0 us)
Async XLA Ops:
  7.2 59.8 %all-gather.3.cloned.1.call-start = ((), (), s32[]{:S(2)}) async-start(), calls=%async_computation.2 | async-start | bytes 5308416 | tf_op jit(solution)/shard_map/all_gather | solution.py:420
  8.9 20.4 %copy-start.1 = (bf16[64,1536]{1,0:T(8,128)(2,1)}, bf16[64,1536]{1,0:T(8,128)(2,1)S(1)}, u32[]{:S(2)}) copy-start(bf16[64,1536]{1,0:T(8,128)(2,1)S(1)} %reshape_squeeze.3.refs_0_.refs_4_) | copy-start | bytes 589828
  8.9 10.7 %collective-permute-start = (bf16[64,1536]{1,0:T(8,128)(2,1)S(1)}, bf16[64,1536]{1,0:T(8,128)(2,1)S(1)}, u32[]{:S(2)}, u32[]{:S(2)}) collective-permute-start(bf16[64,1536]{1,0:T(8,128)(2,1)S(1)} %reshape_squeeze.3.refs_0_.refs_4_), channel_id=1, source_target_pairs={{0,1},{1,2},{2,3},{3,0},{4,5},{5,6},{6,7},{7,4},{8,9},{9,10},{10,1... | collective-permute-start | bytes 589832 | tf_op jit(solution)/shard_map/ppermute | solution.py:408
  10.3 16.2 %collective-permute-start.1 = (bf16[64,1536]{1,0:T(8,128)(2,1)S(1)}, bf16[64,1536]{1,0:T(8,128)(2,1)S(1)}, u32[]{:S(2)}, u32[]{:S(2)}) collective-permute-start(bf16[64,1536]{1,0:T(8,128)(2,1)S(1)} %reshape_squeeze.3.refs_0_.refs_4_), channel_id=1, source_target_pairs={{0,2},{1,3},{2,0},{3,1},{4,6},{5,7},{6,4},{7,5},{8,10},{9,11},{10,... | collective-permute-start | bytes 589832 | tf_op jit(solution)/shard_map/ppermute | solution.py:408
  11.4 17.9 %collective-permute-start.2 = (bf16[64,1536]{1,0:T(8,128)(2,1)S(1)}, bf16[64,1536]{1,0:T(8,128)(2,1)S(1)}, u32[]{:S(2)}, u32[]{:S(2)}) collective-permute-start(bf16[64,1536]{1,0:T(8,128)(2,1)S(1)} %reshape_squeeze.3.refs_0_.refs_4_), channel_id=1, source_target_pairs={{0,3},{1,0},{2,1},{3,2},{4,7},{5,4},{6,5},{7,6},{8,11},{9,8},{10,9... | collective-permute-start | bytes 589832 | tf_op jit(solution)/shard_map/ppermute | solution.py:408
  19.6 11.6 %copy-start.3 = (bf16[960,768]{1,0:T(8,128)(2,1)}, bf16[960,768]{1,0:T(8,128)(2,1)S(1)}, u32[]{:S(2)}) copy-start(bf16[960,768]{1,0:T(8,128)(2,1)S(1)} %get-tuple-element.46.refs_4_.refs_11_) | copy-start | bytes 4423684
  31.2 6.1 %collective-permute-start.3 = (bf16[256,384]{1,0:T(8,128)(2,1)S(1)}, bf16[256,384]{1,0:T(8,128)(2,1)S(1)}, u32[]{:S(2)}, u32[]{:S(2)}) collective-permute-start(bf16[256,384]{1,0:T(8,128)(2,1)S(1)} %get-tuple-element.48.refs_0_), channel_id=1, source_target_pairs={{0,1},{1,2},{2,3},{3,0},{4,5},{5,6},{6,7},{7,4},{8,9},{9,10},{10,1... | collective-permute-start | bytes 589832 | tf_op jit(solution)/shard_map/ppermute | solution.py:408
  31.3 16.7 %collective-permute-start.4 = (bf16[256,384]{1,0:T(8,128)(2,1)S(1)}, bf16[256,384]{1,0:T(8,128)(2,1)S(1)}, u32[]{:S(2)}, u32[]{:S(2)}) collective-permute-start(bf16[256,384]{1,0:T(8,128)(2,1)S(1)} %get-tuple-element.48.refs_0_), channel_id=1, source_target_pairs={{0,2},{1,3},{2,0},{3,1},{4,6},{5,7},{6,4},{7,5},{8,10},{9,11},{10,... | collective-permute-start | bytes 589832 | tf_op jit(solution)/shard_map/ppermute | solution.py:408
  31.6 17.9 %collective-permute-start.5 = (bf16[256,384]{1,0:T(8,128)(2,1)S(1)}, bf16[256,384]{1,0:T(8,128)(2,1)S(1)}, u32[]{:S(2)}, u32[]{:S(2)}) collective-permute-start(bf16[256,384]{1,0:T(8,128)(2,1)S(1)} %get-tuple-element.48.refs_0_), channel_id=1, source_target_pairs={{0,3},{1,0},{2,1},{3,2},{4,7},{5,4},{6,5},{7,6},{8,11},{9,8},{10,9... | collective-permute-start | bytes 589832 | tf_op jit(solution)/shard_map/ppermute | solution.py:408
  53.6 13.4 %all-to-all-start = ((bf16[8,192,256]{2,1,0:T(8,128)(2,1)}), bf16[8,192,256]{2,1,0:T(8,128)(2,1)S(1)}, u32[]{:S(2)}, u32[]{:S(2)}) async-start(bf16[8,192,256]{2,1,0:T(8,128)(2,1)} %bitcast.19), calls=%async_computation | async-start | bytes 1572864 | tf_op jit(solution)/shard_map/all_to_all | solution.py:456
  57.9 18.7 %collective-permute-start.6 = (bf16[272,384]{1,0:T(8,128)(2,1)}, bf16[272,384]{1,0:T(8,128)(2,1)}, u32[]{:S(2)}, u32[]{:S(2)}) collective-permute-start(bf16[272,384]{1,0:T(8,128)(2,1)} %get-tuple-element.62), channel_id=1, source_target_pairs={{0,1},{1,2},{2,3},{3,0},{4,5},{5,6},{6,7},{7,4},{8,9},{9,10},{10,1... | collective-permute-start | bytes 626696 | tf_op jit(solution)/shard_map/ppermute | solution.py:408
  57.9 18.7 %collective-permute-start.7 = (bf16[272,384]{1,0:T(8,128)(2,1)}, bf16[272,384]{1,0:T(8,128)(2,1)}, u32[]{:S(2)}, u32[]{:S(2)}) collective-permute-start(bf16[272,384]{1,0:T(8,128)(2,1)} %get-tuple-element.63), channel_id=1, source_target_pairs={{0,2},{1,3},{2,0},{3,1},{4,6},{5,7},{6,4},{7,5},{8,10},{9,11},{10,... | collective-permute-start | bytes 626696 | tf_op jit(solution)/shard_map/ppermute | solution.py:408
  59.9 19.4 %collective-permute-start.8 = (bf16[272,384]{1,0:T(8,128)(2,1)}, bf16[272,384]{1,0:T(8,128)(2,1)}, u32[]{:S(2)}, u32[]{:S(2)}) collective-permute-start(bf16[272,384]{1,0:T(8,128)(2,1)} %get-tuple-element.64), channel_id=1, source_target_pairs={{0,3},{1,0},{2,1},{3,2},{4,7},{5,4},{6,5},{7,6},{8,11},{9,8},{10,9... | collective-permute-start | bytes 626696 | tf_op jit(solution)/shard_map/ppermute | solution.py:408
  71.8 7.6 %copy-start = (bf16[4,192,1152]{2,1,0:T(8,128)(2,1)S(1)}, bf16[4,192,1152]{2,1,0:T(8,128)(2,1)}, u32[]{:S(2)}) copy-start(bf16[4,192,1152]{2,1,0:T(8,128)(2,1)} %weight_share.1.refs_12_) | copy-start | bytes 5308420
  71.8 44.6 %all-to-all-start.1 = ((bf16[4,192,1152]{2,1,0:T(8,128)(2,1)}), bf16[4,192,1152]{2,1,0:T(8,128)(2,1)S(1)}, u32[]{:S(2)}, u32[]{:S(2)}) async-start(bf16[4,192,1152]{2,1,0:T(8,128)(2,1)} %weight_share.1.refs_12_), calls=%async_computation.1 | async-start | bytes 3538944 | tf_op jit(solution)/shard_map/all_to_all | solution.py:463
  79.4 1.4 copy-start.4
  87.5 21.2 %copy-start.2 = (bf16[64,1536]{1,0:T(8,128)(2,1)S(1)}, bf16[64,1536]{1,0:T(8,128)(2,1)}, u32[]{:S(2)}) copy-start(bf16[64,1536]{1,0:T(8,128)(2,1)} %copy-done.1) | copy-start | bytes 589828
  87.5 21.2 %copy-start.9 = (bf16[64,1792]{1,0:T(8,128)(2,1)S(1)}, bf16[64,1792]{1,0:T(8,128)(2,1)}, u32[]{:S(2)}) copy-start(bf16[64,1792]{1,0:T(8,128)(2,1)} %get-tuple-element.71.refs_0_) | copy-start | bytes 688132
  87.5 3.3 %collective-permute-start.12 = (bf16[4,240,384]{2,1,0:T(8,128)(2,1)}, bf16[4,240,384]{2,1,0:T(8,128)(2,1)S(1)}, u32[]{:S(2)}, u32[]{:S(2)}) collective-permute-start(bf16[4,240,384]{2,1,0:T(8,128)(2,1)} %get-tuple-element.77), channel_id=1, source_target_pairs={{0,4},{4,0},{8,12},{12,8},{16,20},{20,16},{24,28},{28,24},{1,5},{5... | collective-permute-start | bytes 2211848 | tf_op jit(solution)/shard_map/ppermute | solution.py:410
  88.1 15.7 %collective-permute-start.10 = (bf16[64,1792]{1,0:T(8,128)(2,1)}, bf16[64,1792]{1,0:T(8,128)(2,1)S(1)}, u32[]{:S(2)}, u32[]{:S(2)}) collective-permute-start(bf16[64,1792]{1,0:T(8,128)(2,1)} %get-tuple-element.73), channel_id=1, source_target_pairs={{0,2},{1,3},{2,0},{3,1},{4,6},{5,7},{6,4},{7,5},{8,10},{9,11},{10,... | collective-permute-start | bytes 688136 | tf_op jit(solution)/shard_map/ppermute | solution.py:408
  89.4 18.8 %collective-permute-start.11 = (bf16[64,1792]{1,0:T(8,128)(2,1)}, bf16[64,1792]{1,0:T(8,128)(2,1)S(1)}, u32[]{:S(2)}, u32[]{:S(2)}) collective-permute-start(bf16[64,1792]{1,0:T(8,128)(2,1)} %get-tuple-element.74), channel_id=1, source_target_pairs={{0,3},{1,0},{2,1},{3,2},{4,7},{5,4},{6,5},{7,6},{8,11},{9,8},{10,9... | collective-permute-start | bytes 688136 | tf_op jit(solution)/shard_map/ppermute | solution.py:408
  89.4 19.4 %collective-permute-start.9 = (bf16[64,1792]{1,0:T(8,128)(2,1)}, bf16[64,1792]{1,0:T(8,128)(2,1)S(1)}, u32[]{:S(2)}, u32[]{:S(2)}) collective-permute-start(bf16[64,1792]{1,0:T(8,128)(2,1)} %get-tuple-element.72), channel_id=1, source_target_pairs={{0,1},{1,2},{2,3},{3,0},{4,5},{5,6},{6,7},{7,4},{8,9},{9,10},{10,1... | collective-permute-start | bytes 688136 | tf_op jit(solution)/shard_map/ppermute | solution.py:408
  92.4 17.4 %collective-permute-start.13 = (bf16[240,384]{1,0:T(8,128)(2,1)S(1)}, bf16[240,384]{1,0:T(8,128)(2,1)S(1)}, u32[]{:S(2)}, u32[]{:S(2)}) collective-permute-start(bf16[240,384]{1,0:T(8,128)(2,1)S(1)} %get-tuple-element.79), channel_id=1, source_target_pairs={{0,8},{4,12},{8,0},{12,4},{16,24},{20,28},{24,16},{28,20},{1,9},{5... | collective-permute-start | bytes 552968 | tf_op jit(solution)/shard_map/ppermute | solution.py:410
  94.1 15.7 %collective-permute-start.14 = (bf16[240,384]{1,0:T(8,128)(2,1)S(1)}, bf16[240,384]{1,0:T(8,128)(2,1)S(1)}, u32[]{:S(2)}, u32[]{:S(2)}) collective-permute-start(bf16[240,384]{1,0:T(8,128)(2,1)S(1)} %get-tuple-element.80), channel_id=1, source_target_pairs={{0,16},{4,20},{8,24},{12,28},{16,0},{20,4},{24,8},{28,12},{1,17},{... | collective-permute-start | bytes 552968 | tf_op jit(solution)/shard_map/ppermute | solution.py:410
  103.8 6.6 %collective-permute-start.15 = (bf16[240,384]{1,0:T(8,128)(2,1)S(1)}, bf16[240,384]{1,0:T(8,128)(2,1)S(1)}, u32[]{:S(2)}, u32[]{:S(2)}) collective-permute-start(bf16[240,384]{1,0:T(8,128)(2,1)S(1)} %get-tuple-element.81), channel_id=1, source_target_pairs={{0,24},{4,28},{8,16},{12,20},{16,8},{20,12},{24,0},{28,4},{1,25},{... | collective-permute-start | bytes 552968 | tf_op jit(solution)/shard_map/ppermute | solution.py:410
  110.6 1.5 copy-start.7
  110.6 5.1 %collective-permute-start.16 = (bf16[256,384]{1,0:T(8,128)(2,1)S(1)}, bf16[256,384]{1,0:T(8,128)(2,1)S(1)}, u32[]{:S(2)}, u32[]{:S(2)}) collective-permute-start(bf16[256,384]{1,0:T(8,128)(2,1)S(1)} %chip_sum.1.refs_0_), channel_id=1, source_target_pairs={{0,8},{4,12},{8,0},{12,4},{16,24},{20,28},{24,16},{28,20},{1,9},{5... | collective-permute-start | bytes 589832 | tf_op jit(solution)/shard_map/ppermute | solution.py:410
  117.3 2.5 %copy-start.8 = (bf16[256,384]{1,0:T(8,128)(2,1)S(1)}, bf16[256,384]{1,0:T(8,128)(2,1)}, u32[]{:S(2)}) copy-start(bf16[256,384]{1,0:T(8,128)(2,1)} %copy-done.7) | copy-start | bytes 589828
  117.5 18.6 %collective-permute-start.20 = (bf16[4,192,1152]{2,1,0:T(8,128)(2,1)S(1)}, bf16[4,192,1152]{2,1,0:T(8,128)(2,1)}, u32[]{:S(2)}, u32[]{:S(2)}) collective-permute-start(bf16[4,192,1152]{2,1,0:T(8,128)(2,1)S(1)} %weight_grad_half.1.refs_0_), channel_id=1, source_target_pairs={{0,4},{4,0},{8,12},{12,8},{16,20},{20,16},{24,28},{28,24},{1,5},{5... | collective-permute-start | bytes 5308424 | tf_op jit(solution)/shard_map/ppermute | solution.py:410
  119.8 9.9 %collective-permute-start.17 = (bf16[256,384]{1,0:T(8,128)(2,1)S(1)}, bf16[256,384]{1,0:T(8,128)(2,1)S(1)}, u32[]{:S(2)}, u32[]{:S(2)}) collective-permute-start(bf16[256,384]{1,0:T(8,128)(2,1)S(1)} %copy-done.8), channel_id=1, source_target_pairs={{0,16},{4,20},{8,24},{12,28},{16,0},{20,4},{24,8},{28,12},{1,17},{... | collective-permute-start | bytes 589832 | tf_op jit(solution)/shard_map/ppermute | solution.py:410
  121.2 8.6 %collective-permute-start.18 = (bf16[256,384]{1,0:T(8,128)(2,1)S(1)}, bf16[256,384]{1,0:T(8,128)(2,1)S(1)}, u32[]{:S(2)}, u32[]{:S(2)}) collective-permute-start(bf16[256,384]{1,0:T(8,128)(2,1)S(1)} %copy-done.8), channel_id=1, source_target_pairs={{0,24},{4,28},{8,16},{12,20},{16,8},{20,12},{24,0},{28,4},{1,25},{... | collective-permute-start | bytes 589832 | tf_op jit(solution)/shard_map/ppermute | solution.py:410
  129.9 3.5 %collective-permute-start.19 = (bf16[976,384]{1,0:T(8,128)(2,1)S(1)}, bf16[976,384]{1,0:T(8,128)(2,1)S(1)}, u32[]{:S(2)}, u32[]{:S(2)}) collective-permute-start(bf16[976,384]{1,0:T(8,128)(2,1)S(1)} %kernel_grad_half.1.refs_0_), channel_id=1, source_target_pairs={{0,4},{4,0},{8,12},{12,8},{16,20},{20,16},{24,28},{28,24},{1,5},{5... | collective-permute-start | bytes 2248712 | tf_op jit(solution)/shard_map/ppermute | solution.py:410
  (3 other events, 2.3 us)
Sparse Core Ops, SparseCore 0:
  9.9 40.4 all-gather.2

commit v4 on v3

--- a/solution.py
+++ b/solution.py
@@ -40,9 +40,11 @@
         self.value = value
 
 
-def call(kernel, args, outs=(), free=(), kept=(), after=(), near=(), spill=(), scratch=(), flops=0, name=None):
+def call(kernel, args, outs=(), free=(), kept=(), after=(), near=(), spill=(), fetch=(), scratch=(), flops=0, name=None):
     within = lambda v: pltpu.with_memory_space_constraint(v, pltpu.VMEM)
     near, spill = [within(v) for v in near], [within(v) for v in spill]
+    fetch = [pltpu.with_memory_space_constraint(v, pltpu.HBM) for v in fetch]
+    after = [pltpu.with_memory_space_constraint(v, pltpu.HBM) for v in after]
     far = [i for i, v in enumerate(args) if isinstance(v, Far)]
     args = [pltpu.with_memory_space_constraint(v.value, pltpu.HBM) if isinstance(v, Far) else v for v in args]
     count, skip = len(args), len(after) + len(near)
@@ -52,14 +54,14 @@
     def whole(*refs):
         refs = list(refs)
         take = lambda k: [refs.pop(0) for _ in range(k)]
-        ins, _, saved = take(count), take(skip), take(len(spill))
-        targets, rest, places = take(len(outs)), take(len(free) + len(kept)), take(len(spill))
+        ins, _, saved, fetched = take(count), take(skip), take(len(spill)), take(len(fetch))
+        targets, rest, places, nears = take(len(outs)), take(len(free) + len(kept)), take(len(spill)), take(len(fetch))
         own, landed, made = take(len(scratch)), take(len(far)), take(len(outs))
         in_sems, out_sems = refs
         operands = [In(v) for v in ins]
         for k, i in enumerate(far):
             operands[i] = In(landed[k], pltpu.make_async_copy(ins[i], landed[k], in_sems.at[k]))
-        pairs = [*zip(made, targets), *zip(saved, places)]
+        pairs = [*zip(made, targets), *zip(saved, places), *zip(fetched, nears)]
         copies = [pltpu.make_async_copy(v, t, out_sems.at[k]) for k, (v, t) in enumerate(pairs)]
         gone = [False] * len(made)
 
@@ -87,20 +89,35 @@
         whole,
         out_shape=tuple(
             [*memory(pltpu.HBM, outs), *free, *memory(pltpu.VMEM, kept), *memory(pltpu.HBM, spill)]
+            + memory(pltpu.VMEM, fetch)
         ),
-        in_specs=specs + [ANY] * len(after) + [VMEM] * (len(near) + len(spill)),
-        out_specs=tuple([HBM] * len(outs) + [VMEM] * (len(free) + len(kept)) + [HBM] * len(spill)),
+        in_specs=specs + [HBM] * len(after) + [VMEM] * (len(near) + len(spill)) + [HBM] * len(fetch),
+        out_specs=tuple([HBM] * len(outs) + [VMEM] * (len(free) + len(kept)) + [HBM] * len(spill) + [VMEM] * len(fetch)),
         scratch_shapes=[
             *scratch,
             *memory(pltpu.VMEM, [args[i] for i in far]),
             *memory(pltpu.VMEM, outs),
             pltpu.SemaphoreType.DMA((max(1, len(far)),)),
-            pltpu.SemaphoreType.DMA((max(1, len(outs) + len(spill)),)),
+            pltpu.SemaphoreType.DMA((max(1, len(outs) + len(spill) + len(fetch)),)),
         ],
         compiler_params=pltpu.CompilerParams(vmem_limit_bytes=min(56 << 20, need + (SPARE << 20))),
         cost_estimate=pl.CostEstimate(flops=int(flops), bytes_accessed=0, transcendentals=0),
         name=name,
-    )(*args, *after, *near, *spill)
+    )(*args, *after, *near, *spill, *fetch)
+
+
+def gate(value, after, space=pltpu.VMEM):
+    spec = pl.BlockSpec(memory_space=space)
+    return pl.pallas_call(
+        lambda *_: None,
+        out_shape=space(value.shape, value.dtype),
+        in_specs=[spec, ANY],
+        out_specs=spec,
+        input_output_aliases={0: 0},
+        compiler_params=pltpu.CompilerParams(vmem_limit_bytes=SPARE << 20),
+        cost_estimate=pl.CostEstimate(flops=0, bytes_accessed=0, transcendentals=0),
+        name="gate",
+    )(pltpu.with_memory_space_constraint(value, space), after)
 
 
 def dot(a, b):
@@ -300,12 +317,12 @@
 
 
 def weight_kernel(m, scale, ins, outs, go):
-    nms, cots = ins
-    nms, cots = nms(), cots()
-    half = nms.shape[2]
-    total = dot(nms[0], cots[:half, :])
-    for b in range(1, m):
-        total = total + dot(nms[b], cots[b * half : (b + 1) * half, :])
+    core = lax.rem(lax.axis_index("dp"), 2)
+    nms, total = ins[0](), 0.0
+    for v, which in zip(ins[1:], (core, 1 - core)):
+        v = v()
+        for q in range(m // 2):
+            total = total + dot(nms[2 * q + which], v[q])
     total = (total * scale).astype(BF16)
     for q in range(m // 2):
         outs[0][q] = total
@@ -366,16 +383,17 @@
     gain_mid[...] = total[2 : 2 + n, : 2 * c]
 
 
-def hand_kernel(ins, outs, go):
-    outs[0][...] = ins[0]()[...]
-
-
-def weave_kernel(ins, outs, go):
+def weave_kernel(mine, other, *refs):
     core = lax.rem(lax.axis_index("dp"), 2)
-    mine, other = ins
+    out, sems = refs[-2:]
+    copies = []
     for v, which in ((mine, core), (other, 1 - core)):
-        for q in range(v.ref.shape[0]):
-            outs[0][q, which] = v()[q]
+        for q in range(v.shape[0]):
+            copies.append(pltpu.make_async_copy(v.at[q], out.at[q, which], sems.at[len(copies)]))
+    for copy in copies:
+        copy.start()
+    for copy in copies:
+        copy.wait()
 
 
 def input_kernel(n, chans, ins, outs, go):
@@ -412,17 +430,19 @@
     chips = m // 2
     rows, wide = 5 * c // chips, chans // 2
 
-    taps = conv_kernel.transpose(0, 2, 1)
+    taps_rows = conv_kernel.transpose(0, 2, 1).reshape(5 * c, chans)
     own = x.reshape(length // 2, width)
     xs = from_ring(own)
     gin = gain_in.reshape(1, chans)
     gmid = gain_mid.reshape(2, n, c).transpose(1, 0, 2).reshape(n, 2 * c)
-    cots = lax.all_gather(cot, "dp", axis=0, tiled=True)
-    used = [cot, qkv_weight, taps.reshape(5 * c, chans), gin, gmid]
+    cots = jnp.broadcast_to(cot[None], (chips, *cot.shape))
+    cots = lax.all_to_all(cots, "dp", 0, 0, axis_index_groups=same_core, tiled=True)
+    used = [cot, qkv_weight, taps_rows, gin, gmid]
     held = call(
         functools.partial(mid_kernel, n, c, chans),
         [*map(Far, used)],
         kept=[shaped((half, 2 * c), BF16)] * n + [shaped(v.shape, v.dtype) for v in used],
+        flops=WAIT,
         name="mid_parts",
     )
     mid_msgs = held[:n]
@@ -450,13 +470,14 @@
         spill=states,
         name="qkv",
     )
+    cots = gate(cots, nmt, pltpu.HBM)
     mid_msgs = tailed if rides else mid_msgs
-    mids = [Far(mid_msgs[0])] + [shift(mid_msgs[k], k) for k in range(1, n)]
+    mids = [mid_msgs[0]] + [shift(mid_msgs[k], k) for k in range(1, n)]
     parts = [] if rides else from_ring(part)
     nms = lax.all_to_all(nmt.reshape(m, width // m, half), "dp", 0, 0, tiled=True)
     (wshare,) = call(
         functools.partial(weight_kernel, m, scale),
-        [nms, Far(cots)],
+        [nms, Far(cots), Far(across(cots, 1))],
         outs=[shaped((chips, width // m, cols), BF16)],
         name="weight_share",
     )
@@ -464,26 +485,27 @@
     send, keep, *msgs = call(
         functools.partial(back_kernel, n, c, chans, m),
         [
-            *mids,
+            Far(mids[0]),
+            *mids[1:],
             *parts,
             *map(Far, [pooled, rtwo, conv_out]),
             gmid,
             Far(nin),
             gin,
             Far(rone),
-            taps,
+            Far(taps_rows),
         ],
         outs=[
             shaped((chips, rows, wide), BF16),
             shaped((chips, rows, wide), F32),
         ]
         + [shaped((half // n, width + 256), BF16)] * n,
-        after=[wshare],
         scratch=[
             pltpu.VMEM((half, 5 * c), BF16),
             pltpu.VMEM((half, 5 * c), BF16),
             pltpu.VMEM((half, width + 128), BF16),
         ],
+        after=[wshare],
         flops=WAIT,
         name="conv_backward",
     )
@@ -508,12 +530,24 @@
             free=[shaped((rows + 16, wide), BF16)],
             name="chip_sum",
         )
+        whalf = gate(whalf, kshare)
+        within = lambda v: pltpu.with_memory_space_constraint(v, pltpu.VMEM)
+        weight_grad = pl.pallas_call(
+            weave_kernel,
+            out_shape=pltpu.HBM((chips, 2, width // m, cols), BF16),
+            in_specs=[VMEM, VMEM],
+            out_specs=HBM,
+            scratch_shapes=[pltpu.SemaphoreType.DMA((m,))],
+            compiler_params=pltpu.CompilerParams(vmem_limit_bytes=SPARE << 20),
+            cost_estimate=pl.CostEstimate(flops=0, bytes_accessed=0, transcendentals=0),
+            name="weight_grad",
+        )(within(whalf), within(across(whalf, 1)))
         kshares = [kshare] + [across(kshare, k) for k in range(2, m, 2)]
-        last = kshares[1]
         (mine,) = call(
             functools.partial(half_kernel, chips),
             kshares,
             free=[shaped((5 * c + 16, wide), BF16)],
+            after=[weight_grad],
             name="kernel_grad_half",
         )
         taps_grad, gain_in_grad, gain_mid_grad = call(
@@ -528,16 +562,20 @@
         both = jnp.where(core == 0, both, both[::-1]).transpose(1, 2, 0, 3).reshape(5 * c, chans)
         both, gains = lax.psum((both, gains), "dp")
         taps_grad, gains = (both * scale).astype(BF16), gains * scale
+        whalf = gate(whalf, gains)
+        within = lambda v: pltpu.with_memory_space_constraint(v, pltpu.VMEM)
+        weight_grad = pl.pallas_call(
+            weave_kernel,
+            out_shape=pltpu.HBM((chips, 2, width // m, cols), BF16),
+            in_specs=[VMEM, VMEM],
+            out_specs=HBM,
+            scratch_shapes=[pltpu.SemaphoreType.DMA((m,))],
+            compiler_params=pltpu.CompilerParams(vmem_limit_bytes=SPARE << 20),
+            cost_estimate=pl.CostEstimate(flops=0, bytes_accessed=0, transcendentals=0),
+            name="weight_grad",
+        )(within(whalf), within(across(whalf, 1)))
         gain_in_grad = jnp.sum(gains[:, : chans // 128], axis=0)
         gain_mid_grad = gains[:, chans // 128 :].reshape(n, -1)[:, : 2 * c]
-        last = gains
-    (whalf,) = call(hand_kernel, [whalf], free=[shaped(whalf.shape, BF16)], after=[last], name="weight_grad_half")
-    (weight_grad,) = call(
-        weave_kernel,
-        [whalf, across(whalf, 1)],
-        free=[shaped((chips, 2, width // m, cols), BF16)],
-        name="weight_grad",
-    )
     return (
         qkv[None],
         input_grad.reshape(1, length, chans),

time: 148 us -> 120 us (0.81)
  between operations: 14.3 us -> 0.88 us
  waiting for transfers between devices: 58.3 us -> 50.5 us
  Pallas kernels: 28.8 us -> 25.3 us
  local copies, waits for them, and re-layouts: 10.5 us -> 7.12 us
    pallas_call x12 -> x10, Pallas kernels: 28.8 us -> 23.5 us  [call(): pl.pallas_call(whole, out_shape=tuple([*memory(pltpu.HBM, outs), *free, *...]
    all_to_all x0 -> x1, starting transfers between devices: none -> 4.65 us  [body(): lax.all_to_all(cots, 'dp', 0, 0, axis_index_groups=same_core, tiled=True)]
    unnamed x22 -> x12, local copies, waits for them, and re-layouts: 3.69 us -> 0.02 us
    ppermute x12, waiting for transfers between devices: 40.1 us -> 36.5 us  [body(): lax.ppermute(v, 'seq', [(i, (i + k) % n) for i in range(n)])]
    ppermute x9 -> x10, waiting for transfers between devices: 11.9 us -> 8.52 us  [body(): across = lambda v, k: lax.ppermute(v, 'dp', [(i, i ^ k) for i in range(m)])]
    ppermute x9 -> x10, starting transfers between devices: 13.7 us -> 10.9 us  [body(): across = lambda v, k: lax.ppermute(v, 'dp', [(i, i ^ k) for i in range(m)])]
    broadcast_in_dim x0 -> x1, local copies, waits for them, and re-layouts: none -> 2.64 us  [body(): cots = jnp.broadcast_to(cot[None], (chips, *cot.shape))]
    pallas_call x0 -> x3, Pallas kernels: none -> 1.85 us  [the longest x1 1.85 us: body(): pl.pallas_call(weave_kernel, out_shape=pltpu.HBM((chips, 2, width // m, c...]
  transfers between devices with their start and end apart: 24 -> 25, of which waited for: 14 -> 16; matrix products, arithmetic and copies ran while one was open for 5% -> 4% of each run, Pallas kernels for 17% -> 20%
where the time goes in v4:
time: 120 us; the launch traced here: 119 us
  waiting for transfers between devices  50.5 us (42%)
  starting transfers between devices  35.6 us (30%)
  Pallas kernels  25.3 us (21%)
  local copies, waits for them, and re-layouts  7.12 us (6%)
    ppermute x12, waiting for transfers between devices, body(): lax.ppermute(v, 'seq', [(i, (i + k) % n) for i in range(n)])  36.5 us
    pallas_call x10, Pallas kernels, call(): pl.pallas_call(whole, out_shape=tuple([*memory(pltpu.HBM, outs), *free, *...  23.5 us
    ppermute x12, starting transfers between devices, body(): lax.ppermute(v, 'seq', [(i, (i + k) % n) for i in range(n)])  11.7 us
    ppermute x10, starting transfers between devices, body(): across = lambda v, k: lax.ppermute(v, 'dp', [(i, i ^ k) for i in range(m)])  10.9 us
    ppermute x10, waiting for transfers between devices, body(): across = lambda v, k: lax.ppermute(v, 'dp', [(i, i ^ k) for i in range(m)])  8.52 us
    all_to_all x1, waiting for transfers between devices, body(): lax.all_to_all(nmt.reshape(m, width // m, half), 'dp', 0, 0, tiled=True)  5.48 us
    all_to_all x1, starting transfers between devices, body(): lax.all_to_all(cots, 'dp', 0, 0, axis_index_groups=same_core, tiled=True)  4.65 us
    all_to_all x1, starting transfers between devices, body(): lax.all_to_all(wshare, 'dp', 0, 0, axis_index_groups=same_core, tiled=True)  4.54 us
  transfers between devices with their start and end apart: 25, of which 16 were waited for; matrix products, arithmetic and copies ran while one was open for 4% of the time, Pallas kernels for 20%

profile of v4, /device:TPU:9, one launch (start us, length us, event | category | flops | bytes accessed | tf_op | source)
XLA Modules:
  0.0 119.4 jit_solution(2926392104805766263)
XLA Ops:
  1.6 1.3 %collective-permute-start = (bf16[64,1536]{1,0:T(8,128)(2,1)S(1)}, bf16[64,1536]{1,0:T(8,128)(2,1)S(1)}, u32[]{:S(2)}, u32[]{:S(2)}) collective-permute-start(bf16[64,1536]{1,0:T(8,128)(2,1)S(1)} %reshape_squeeze.3.refs_0_.refs_4_), channel_id=1, source_target_pairs={{0,1},{1,2},{2,3},{3,0},{4,5},{5,6},{6,7},{7,4},{8,9},{9,10},{10,1... | collective-permute-start | bytes 589832 | tf_op jit(solution)/shard_map/ppermute | solution.py:426
  4.1 1.4 %collective-permute-start.2 = (bf16[64,1536]{1,0:T(8,128)(2,1)S(1)}, bf16[64,1536]{1,0:T(8,128)(2,1)S(1)}, u32[]{:S(2)}, u32[]{:S(2)}) collective-permute-start(bf16[64,1536]{1,0:T(8,128)(2,1)S(1)} %reshape_squeeze.3.refs_0_.refs_4_), channel_id=1, source_target_pairs={{0,3},{1,0},{2,1},{3,2},{4,7},{5,4},{6,5},{7,6},{8,11},{9,8},{10,9... | collective-permute-start | bytes 589832 | tf_op jit(solution)/shard_map/ppermute | solution.py:426
  5.5 2.6 %broadcast_in_dim.9 = bf16[4,256,1152]{2,1,0:T(8,128)(2,1)} broadcast(bf16[256,1152]{1,0:T(8,128)(2,1)} %bitcast.15), dimensions={1,2} | broadcast | bytes 2949120 | tf_op jit(solution)/shard_map/broadcast_in_dim | solution.py:438
  8.1 4.6 %all-to-all-start.1 = ((bf16[4,256,1152]{2,1,0:T(8,128)(2,1)}), bf16[4,256,1152]{2,1,0:T(8,128)(2,1)}, u32[]{:S(2)}, u32[]{:S(2)}) async-start(bf16[4,256,1152]{2,1,0:T(8,128)(2,1)} %broadcast_in_dim.9), calls=%async_computation.1 | async-start | bytes 4718592 | tf_op jit(solution)/shard_map/all_to_all | solution.py:439
  14.1 4.2 %mid_parts.1 = (bf16[256,384]{1,0:T(8,128)(2,1)S(1)}, bf16[256,384]{1,0:T(8,128)(2,1)S(1)}, bf16[256,384]{1,0:T(8,128)(2,1)S(1)}, bf16[256,384]{1,0:T(8,128)(2,1...) custom-call(bf16[256,1152]{1,0:T(8,128)(2,1)} %bitcast.16, ...), custom_call_target="tpu_custom_call" | custom-call | flops 40000000000 | tf_op jit(solution)/shard_map/mid_parts/pallas_call | solution.py:88
  19.2 2.9 %collective-permute-done.2.refs_3_ = bf16[64,1536]{1,0:T(8,128)(2,1)S(1)} collective-permute-done((bf16[64,1536]{1,0:T(8,128)(2,1)S(1)}, bf16[64,1536]{1,0:T(8,128)(2,1)S(1)}, u32[]{:S(2)}, u32[]{:S(2)}) %collective-permute-start.2) | collective-permute-done | bytes 196640 | tf_op jit(solution)/shard_map/ppermute | solution.py:426
  22.1 1.9 %conv_forward.1 = (bf16[256,384]{1,0:T(8,128)(2,1)S(1)}, f32[256,384]{1,0:T(8,128)S(1)}, f32[256,384]{1,0:T(8,128)S(1)}, bf16[256,1536]{1,0:T(8,128)(2,1)S(1)}, f32[256,2]{1,0:T(8,128)S(1)}) custom-call(bf16[64,1536]{1,0:T(8,128)(2,1)S(1)} %reshape_squeeze.3.refs_0_.refs_4_, bf16[64,1536]{1,0:T(8,128)(2,1)S(1)} %collective-permute-done.refs_1_, ...), custom_call_target="tpu_custom_call" | custom-call | tf_op jit(solution)/shard_map/conv_forward/pallas_call | solution.py:88
  24.4 1.4 %collective-permute-start.5 = (bf16[256,384]{1,0:T(8,128)(2,1)S(1)}, bf16[256,384]{1,0:T(8,128)(2,1)S(1)}, u32[]{:S(2)}, u32[]{:S(2)}) collective-permute-start(bf16[256,384]{1,0:T(8,128)(2,1)S(1)} %get-tuple-element.48.refs_0_), channel_id=1, source_target_pairs={{0,3},{1,0},{2,1},{3,2},{4,7},{5,4},{6,5},{7,6},{8,11},{9,8},{10,9... | collective-permute-start | bytes 589832 | tf_op jit(solution)/shard_map/ppermute | solution.py:426
  25.8 4.5 %collective-permute-done.3.refs_1_ = bf16[256,384]{1,0:T(8,128)(2,1)S(1)} collective-permute-done((bf16[256,384]{1,0:T(8,128)(2,1)S(1)}, bf16[256,384]{1,0:T(8,128)(2,1)S(1)}, u32[]{:S(2)}, u32[]{:S(2)}) %collective-permute-start.3) | collective-permute-done | bytes 196640 | tf_op jit(solution)/shard_map/ppermute | solution.py:426
  30.3 10.7 %collective-permute-done.4.refs_2_ = bf16[256,384]{1,0:T(8,128)(2,1)S(1)} collective-permute-done((bf16[256,384]{1,0:T(8,128)(2,1)S(1)}, bf16[256,384]{1,0:T(8,128)(2,1)S(1)}, u32[]{:S(2)}, u32[]{:S(2)}) %collective-permute-start.4) | collective-permute-done | bytes 196640 | tf_op jit(solution)/shard_map/ppermute | solution.py:426
  40.9 1.4 %collective-permute-done.5.refs_3_ = bf16[256,384]{1,0:T(8,128)(2,1)S(1)} collective-permute-done((bf16[256,384]{1,0:T(8,128)(2,1)S(1)}, bf16[256,384]{1,0:T(8,128)(2,1)S(1)}, u32[]{:S(2)}, u32[]{:S(2)}) %collective-permute-start.5) | collective-permute-done | bytes 196640 | tf_op jit(solution)/shard_map/ppermute | solution.py:426
  42.3 4.1 %qkv.1 = (bf16[1536,256]{1,0:T(8,128)(2,1)}, f32[256,1]{1,0:T(8,128)}, bf16[272,384]{1,0:T(8,128)(2,1)}, bf16[272,384]{1,0:T(8,128)(2,1)}, bf16[272,384]{1,0:T(8...) custom-call(bf16[256,384]{1,0:T(8,128)(2,1)S(1)} %get-tuple-element., ...), custom_call_target="tpu_custom_call" | custom-call | tf_op jit(solution)/shard_map/qkv/pallas_call | solution.py:88
  47.1 3.8 %all-to-all-start = ((bf16[8,192,256]{2,1,0:T(8,128)(2,1)}), bf16[8,192,256]{2,1,0:T(8,128)(2,1)S(1)}, u32[]{:S(2)}, u32[]{:S(2)}) async-start(bf16[8,192,256]{2,1,0:T(8,128)(2,1)} %bitcast.6), calls=%async_computation | async-start | bytes 1572864 | tf_op jit(solution)/shard_map/all_to_all | solution.py:477
  50.8 2.2 %collective-permute-start.7 = (bf16[272,384]{1,0:T(8,128)(2,1)S(1)}, bf16[272,384]{1,0:T(8,128)(2,1)S(1)}, u32[]{:S(2)}, u32[]{:S(2)}) collective-permute-start(bf16[272,384]{1,0:T(8,128)(2,1)S(1)} %copy-done.4), channel_id=1, source_target_pairs={{0,2},{1,3},{2,0},{3,1},{4,6},{5,7},{6,4},{7,5},{8,10},{9,11},{10,... | collective-permute-start | bytes 626696 | tf_op jit(solution)/shard_map/ppermute | solution.py:426
  53.1 1.4 %collective-permute-start.8 = (bf16[272,384]{1,0:T(8,128)(2,1)S(1)}, bf16[272,384]{1,0:T(8,128)(2,1)S(1)}, u32[]{:S(2)}, u32[]{:S(2)}) collective-permute-start(bf16[272,384]{1,0:T(8,128)(2,1)S(1)} %copy-done.3), channel_id=1, source_target_pairs={{0,3},{1,0},{2,1},{3,2},{4,7},{5,4},{6,5},{7,6},{8,11},{9,8},{10,9... | collective-permute-start | bytes 626696 | tf_op jit(solution)/shard_map/ppermute | solution.py:426
  54.5 5.5 %all-to-all-done.refs_0_ = bf16[8,192,256]{2,1,0:T(8,128)(2,1)S(1)} async-done(((bf16[8,192,256]{2,1,0:T(8,128)(2,1)}), bf16[8,192,256]{2,1,0:T(8,128)(2,1)S(1)}, u32[]{:S(2)}, u32[]{:S(2)}) %all-to-all-start) | async-done | bytes 786464 | tf_op jit(solution)/shard_map/all_to_all | solution.py:477
  60.0 4.3 %weight_share.1.refs_12_ = bf16[4,192,1152]{2,1,0:T(8,128)(2,1)} custom-call(bf16[8,192,256]{2,1,0:T(8,128)(2,1)S(1)} %all-to-all-done.refs_0_, bf16[4,256,1152]{2,1,0:T(8,128)(2,1)} %gate.2.refs_1_, bf16[4,256,1152]{2,1,0:T(8,128)(2,1)} %collective-permute-done.9.refs_2_), custom_call_target="tpu_custom_call" | custom-call | tf_op jit(solution)/shard_map/weight_share/pallas_call | solution.py:88
  64.3 4.5 %all-to-all-start.2 = ((bf16[4,192,1152]{2,1,0:T(8,128)(2,1)}), bf16[4,192,1152]{2,1,0:T(8,128)(2,1)S(1)}, u32[]{:S(2)}, u32[]{:S(2)}) async-start(bf16[4,192,1152]{2,1,0:T(8,128)(2,1)} %weight_share.1.refs_12_), calls=%async_computation.2 | async-start | bytes 3538944 | tf_op jit(solution)/shard_map/all_to_all | solution.py:484
  69.0 3.1 %collective-permute-done.8.refs_3_ = bf16[272,384]{1,0:T(8,128)(2,1)S(1)} collective-permute-done((bf16[272,384]{1,0:T(8,128)(2,1)S(1)}, bf16[272,384]{1,0:T(8,128)(2,1)S(1)}, u32[]{:S(2)}, u32[]{:S(2)}) %collective-permute-start.8) | collective-permute-done | bytes 208928 | tf_op jit(solution)/shard_map/ppermute | solution.py:426
  72.1 5.6 %conv_backward.1 = (bf16[4,240,384]{2,1,0:T(8,128)(2,1)}, f32[4,240,384]{2,1,0:T(8,128)}, bf16[64,1792]{1,0:T(8,128)(2,1)}, bf16[64,1792]{1,0:T(8,128)(2,1)}, bf...) custom-call(bf16[272,384]{1,0:T(8,128)(2,1)} %get-tuple-element.61.refs_0_, ...), custom_call_target="tpu_custom_call" | custom-call | flops 40000000000 | tf_op jit(solution)/shard_map/conv_backward/pallas_call | solution.py:88
  79.3 1.5 %collective-permute-start.12 = (bf16[64,1792]{1,0:T(8,128)(2,1)}, bf16[64,1792]{1,0:T(8,128)(2,1)S(1)}, u32[]{:S(2)}, u32[]{:S(2)}) collective-permute-start(bf16[64,1792]{1,0:T(8,128)(2,1)} %get-tuple-element.74), channel_id=1, source_target_pairs={{0,3},{1,0},{2,1},{3,2},{4,7},{5,4},{6,5},{7,6},{8,11},{9,8},{10,9... | collective-permute-start | bytes 688136 | tf_op jit(solution)/shard_map/ppermute | solution.py:426
  80.7 1.6 %core_sum.1 = (bf16[240,384]{1,0:T(8,128)(2,1)S(1)}, bf16[240,384]{1,0:T(8,128)(2,1)S(1)}, bf16[240,384]{1,0:T(8,128)(2,1)S(1)}, f32[240,384]{1,0:T(8,128)S(1)}) custom-call(f32[4,240,384]{2,1,0:T(8,128)} %get-tuple-element.76.refs_0_, bf16[4,240,384]{2,1,0:T(8,128)(2,1)S(1)} %collective-permute-done.13.refs_1_), custom_call_target="tpu_custom_call" | custom-call | tf_op jit(solution)/shard_map/core_sum/pallas_call | solution.py:88
  82.3 1.8 %collective-permute-start.14 = (bf16[240,384]{1,0:T(8,128)(2,1)S(1)}, bf16[240,384]{1,0:T(8,128)(2,1)S(1)}, u32[]{:S(2)}, u32[]{:S(2)}) collective-permute-start(bf16[240,384]{1,0:T(8,128)(2,1)S(1)} %get-tuple-element.79), channel_id=1, source_target_pairs={{0,8},{4,12},{8,0},{12,4},{16,24},{20,28},{24,16},{28,20},{1,9},{5... | collective-permute-start | bytes 552968 | tf_op jit(solution)/shard_map/ppermute | solution.py:428
  85.7 2.3 %collective-permute-start.16 = (bf16[240,384]{1,0:T(8,128)(2,1)S(1)}, bf16[240,384]{1,0:T(8,128)(2,1)S(1)}, u32[]{:S(2)}, u32[]{:S(2)}) collective-permute-start(bf16[240,384]{1,0:T(8,128)(2,1)S(1)} %get-tuple-element.81), channel_id=1, source_target_pairs={{0,24},{4,28},{8,16},{12,20},{16,8},{20,12},{24,0},{28,4},{1,25},{... | collective-permute-start | bytes 552968 | tf_op jit(solution)/shard_map/ppermute | solution.py:428
  88.0 10.6 %collective-permute-done.11.refs_2_ = bf16[64,1792]{1,0:T(8,128)(2,1)S(1)} collective-permute-done((bf16[64,1792]{1,0:T(8,128)(2,1)}, bf16[64,1792]{1,0:T(8,128)(2,1)S(1)}, u32[]{:S(2)}, u32[]{:S(2)}) %collective-permute-start.11) | collective-permute-done | bytes 229408 | tf_op jit(solution)/shard_map/ppermute | solution.py:426
  98.5 1.8 %collective-permute-done.12.refs_3_ = bf16[64,1792]{1,0:T(8,128)(2,1)S(1)} collective-permute-done((bf16[64,1792]{1,0:T(8,128)(2,1)}, bf16[64,1792]{1,0:T(8,128)(2,1)S(1)}, u32[]{:S(2)}, u32[]{:S(2)}) %collective-permute-start.12) | collective-permute-done | bytes 229408 | tf_op jit(solution)/shard_map/ppermute | solution.py:426
  101.5 1.7 %collective-permute-start.17 = (bf16[256,384]{1,0:T(8,128)(2,1)S(1)}, bf16[256,384]{1,0:T(8,128)(2,1)S(1)}, u32[]{:S(2)}, u32[]{:S(2)}) collective-permute-start(bf16[256,384]{1,0:T(8,128)(2,1)S(1)} %chip_sum.1.__1_.refs_0_), channel_id=1, source_target_pairs={{0,8},{4,12},{8,0},{12,4},{16,24},{20,28},{24,16},{28,20},{1,9},{5... | collective-permute-start | bytes 589832 | tf_op jit(solution)/shard_map/ppermute | solution.py:428
  104.8 1.8 %weight_grad.1.refs_4_ = bf16[4,2,192,1152]{3,2,1,0:T(8,128)(2,1)} custom-call(bf16[4,192,1152]{2,1,0:T(8,128)(2,1)S(1)} %gate.3.mine, bf16[4,192,1152]{2,1,0:T(8,128)(2,1)S(1)} %collective-permute-done.20.other), custom_call_target="tpu_custom_call" | custom-call | tf_op jit(solution)/shard_map/weight_grad/pallas_call | solution.py:535
  106.6 1.7 %collective-permute-done.17.refs_1_ = bf16[256,384]{1,0:T(8,128)(2,1)S(1)} collective-permute-done((bf16[256,384]{1,0:T(8,128)(2,1)S(1)}, bf16[256,384]{1,0:T(8,128)(2,1)S(1)}, u32[]{:S(2)}, u32[]{:S(2)}) %collective-permute-start.17) | collective-permute-done | bytes 196640 | tf_op jit(solution)/shard_map/ppermute | solution.py:428
  108.3 4.1 %collective-permute-done.18.refs_2_ = bf16[256,384]{1,0:T(8,128)(2,1)S(1)} collective-permute-done((bf16[256,384]{1,0:T(8,128)(2,1)S(1)}, bf16[256,384]{1,0:T(8,128)(2,1)S(1)}, u32[]{:S(2)}, u32[]{:S(2)}) %collective-permute-start.18) | collective-permute-done | bytes 196640 | tf_op jit(solution)/shard_map/ppermute | solution.py:428
  112.4 1.2 %collective-permute-done.19.refs_3_ = bf16[256,384]{1,0:T(8,128)(2,1)S(1)} collective-permute-done((bf16[256,384]{1,0:T(8,128)(2,1)S(1)}, bf16[256,384]{1,0:T(8,128)(2,1)S(1)}, u32[]{:S(2)}, u32[]{:S(2)}) %collective-permute-start.19) | collective-permute-done | bytes 196640 | tf_op jit(solution)/shard_map/ppermute | solution.py:428
  116.8 1.3 %kernel_grad.1 = (bf16[960,768]{1,0:T(8,128)(2,1)}, f32[2,384]{1,0:T(2,128)S(1)}, f32[4,384]{1,0:T(4,128)S(1)}) custom-call(bf16[976,384]{1,0:T(8,128)(2,1)S(1)} %kernel_grad_half.1.refs_0_, bf16[976,384]{1,0:T(8,128)(2,1)S(1)} %collective-permute-done.21.refs_1_), custom_call_target="tpu_custom_call" | custom-call | tf_op jit(solution)/shard_map/kernel_grad/pallas_call | solution.py:88
  (54 shorter events, 15.8 us)
Async XLA Ops:
  1.6 16.7 %collective-permute-start = (bf16[64,1536]{1,0:T(8,128)(2,1)S(1)}, bf16[64,1536]{1,0:T(8,128)(2,1)S(1)}, u32[]{:S(2)}, u32[]{:S(2)}) collective-permute-start(bf16[64,1536]{1,0:T(8,128)(2,1)S(1)} %reshape_squeeze.3.refs_0_.refs_4_), channel_id=1, source_target_pairs={{0,1},{1,2},{2,3},{3,0},{4,5},{5,6},{6,7},{7,4},{8,9},{9,10},{10,1... | collective-permute-start | bytes 589832 | tf_op jit(solution)/shard_map/ppermute | solution.py:426
  3.0 16.2 %collective-permute-start.1 = (bf16[64,1536]{1,0:T(8,128)(2,1)S(1)}, bf16[64,1536]{1,0:T(8,128)(2,1)S(1)}, u32[]{:S(2)}, u32[]{:S(2)}) collective-permute-start(bf16[64,1536]{1,0:T(8,128)(2,1)S(1)} %reshape_squeeze.3.refs_0_.refs_4_), channel_id=1, source_target_pairs={{0,2},{1,3},{2,0},{3,1},{4,6},{5,7},{6,4},{7,5},{8,10},{9,11},{10,... | collective-permute-start | bytes 589832 | tf_op jit(solution)/shard_map/ppermute | solution.py:426
  4.1 18.1 %collective-permute-start.2 = (bf16[64,1536]{1,0:T(8,128)(2,1)S(1)}, bf16[64,1536]{1,0:T(8,128)(2,1)S(1)}, u32[]{:S(2)}, u32[]{:S(2)}) collective-permute-start(bf16[64,1536]{1,0:T(8,128)(2,1)S(1)} %reshape_squeeze.3.refs_0_.refs_4_), channel_id=1, source_target_pairs={{0,3},{1,0},{2,1},{3,2},{4,7},{5,4},{6,5},{7,6},{8,11},{9,8},{10,9... | collective-permute-start | bytes 589832 | tf_op jit(solution)/shard_map/ppermute | solution.py:426
  8.1 4.7 %copy-start.1 = (f32[1536]{0:T(1024)S(1)}, f32[1536]{0:T(1024)}, u32[]{:S(2)}) copy-start(f32[1536]{0:T(1024)} %param.10) | copy-start | bytes 18436
  8.1 5.4 %copy-start.2 = (f32[768]{0:T(1024)S(1)}, f32[768]{0:T(1024)}, u32[]{:S(2)}) copy-start(f32[768]{0:T(1024)} %param.9) | copy-start | bytes 9220
  8.1 38.3 %all-to-all-start.1 = ((bf16[4,256,1152]{2,1,0:T(8,128)(2,1)}), bf16[4,256,1152]{2,1,0:T(8,128)(2,1)}, u32[]{:S(2)}, u32[]{:S(2)}) async-start(bf16[4,256,1152]{2,1,0:T(8,128)(2,1)} %broadcast_in_dim.9), calls=%async_computation.1 | async-start | bytes 4718592 | tf_op jit(solution)/shard_map/all_to_all | solution.py:439
  24.0 6.3 %collective-permute-start.3 = (bf16[256,384]{1,0:T(8,128)(2,1)S(1)}, bf16[256,384]{1,0:T(8,128)(2,1)S(1)}, u32[]{:S(2)}, u32[]{:S(2)}) collective-permute-start(bf16[256,384]{1,0:T(8,128)(2,1)S(1)} %get-tuple-element.48.refs_0_), channel_id=1, source_target_pairs={{0,1},{1,2},{2,3},{3,0},{4,5},{5,6},{6,7},{7,4},{8,9},{9,10},{10,1... | collective-permute-start | bytes 589832 | tf_op jit(solution)/shard_map/ppermute | solution.py:426
  24.1 16.8 %collective-permute-start.4 = (bf16[256,384]{1,0:T(8,128)(2,1)S(1)}, bf16[256,384]{1,0:T(8,128)(2,1)S(1)}, u32[]{:S(2)}, u32[]{:S(2)}) collective-permute-start(bf16[256,384]{1,0:T(8,128)(2,1)S(1)} %get-tuple-element.48.refs_0_), channel_id=1, source_target_pairs={{0,2},{1,3},{2,0},{3,1},{4,6},{5,7},{6,4},{7,5},{8,10},{9,11},{10,... | collective-permute-start | bytes 589832 | tf_op jit(solution)/shard_map/ppermute | solution.py:426
  24.4 17.9 %collective-permute-start.5 = (bf16[256,384]{1,0:T(8,128)(2,1)S(1)}, bf16[256,384]{1,0:T(8,128)(2,1)S(1)}, u32[]{:S(2)}, u32[]{:S(2)}) collective-permute-start(bf16[256,384]{1,0:T(8,128)(2,1)S(1)} %get-tuple-element.48.refs_0_), channel_id=1, source_target_pairs={{0,3},{1,0},{2,1},{3,2},{4,7},{5,4},{6,5},{7,6},{8,11},{9,8},{10,9... | collective-permute-start | bytes 589832 | tf_op jit(solution)/shard_map/ppermute | solution.py:426
  46.5 4.4 %copy-start.5 = (bf16[272,384]{1,0:T(8,128)(2,1)S(1)}, bf16[272,384]{1,0:T(8,128)(2,1)}, u32[]{:S(2)}) copy-start(bf16[272,384]{1,0:T(8,128)(2,1)} %get-tuple-element.62) | copy-start | bytes 626692
  46.5 4.4 %copy-start.4 = (bf16[272,384]{1,0:T(8,128)(2,1)S(1)}, bf16[272,384]{1,0:T(8,128)(2,1)}, u32[]{:S(2)}) copy-start(bf16[272,384]{1,0:T(8,128)(2,1)} %get-tuple-element.63) | copy-start | bytes 626692
  46.5 6.6 %copy-start.3 = (bf16[272,384]{1,0:T(8,128)(2,1)S(1)}, bf16[272,384]{1,0:T(8,128)(2,1)}, u32[]{:S(2)}) copy-start(bf16[272,384]{1,0:T(8,128)(2,1)} %get-tuple-element.64) | copy-start | bytes 626692
  46.5 13.5 %collective-permute-start.9 = (bf16[4,256,1152]{2,1,0:T(8,128)(2,1)}, bf16[4,256,1152]{2,1,0:T(8,128)(2,1)}, u32[]{:S(2)}, u32[]{:S(2)}) collective-permute-start(bf16[4,256,1152]{2,1,0:T(8,128)(2,1)} %gate.2.refs_1_), channel_id=1, source_target_pairs={{0,4},{4,0},{8,12},{12,8},{16,20},{20,16},{24,28},{28,24},{1,5},{5... | collective-permute-start | bytes 7077896 | tf_op jit(solution)/shard_map/ppermute | solution.py:428
  47.1 12.9 %all-to-all-start = ((bf16[8,192,256]{2,1,0:T(8,128)(2,1)}), bf16[8,192,256]{2,1,0:T(8,128)(2,1)S(1)}, u32[]{:S(2)}, u32[]{:S(2)}) async-start(bf16[8,192,256]{2,1,0:T(8,128)(2,1)} %bitcast.6), calls=%async_computation | async-start | bytes 1572864 | tf_op jit(solution)/shard_map/all_to_all | solution.py:477
  50.8 18.0 %collective-permute-start.6 = (bf16[272,384]{1,0:T(8,128)(2,1)S(1)}, bf16[272,384]{1,0:T(8,128)(2,1)S(1)}, u32[]{:S(2)}, u32[]{:S(2)}) collective-permute-start(bf16[272,384]{1,0:T(8,128)(2,1)S(1)} %copy-done.5), channel_id=1, source_target_pairs={{0,1},{1,2},{2,3},{3,0},{4,5},{5,6},{6,7},{7,4},{8,9},{9,10},{10,1... | collective-permute-start | bytes 626696 | tf_op jit(solution)/shard_map/ppermute | solution.py:426
  50.8 18.2 %collective-permute-start.7 = (bf16[272,384]{1,0:T(8,128)(2,1)S(1)}, bf16[272,384]{1,0:T(8,128)(2,1)S(1)}, u32[]{:S(2)}, u32[]{:S(2)}) collective-permute-start(bf16[272,384]{1,0:T(8,128)(2,1)S(1)} %copy-done.4), channel_id=1, source_target_pairs={{0,2},{1,3},{2,0},{3,1},{4,6},{5,7},{6,4},{7,5},{8,10},{9,11},{10,... | collective-permute-start | bytes 626696 | tf_op jit(solution)/shard_map/ppermute | solution.py:426
  53.1 19.0 %collective-permute-start.8 = (bf16[272,384]{1,0:T(8,128)(2,1)S(1)}, bf16[272,384]{1,0:T(8,128)(2,1)S(1)}, u32[]{:S(2)}, u32[]{:S(2)}) collective-permute-start(bf16[272,384]{1,0:T(8,128)(2,1)S(1)} %copy-done.3), channel_id=1, source_target_pairs={{0,3},{1,0},{2,1},{3,2},{4,7},{5,4},{6,5},{7,6},{8,11},{9,8},{10,9... | collective-permute-start | bytes 626696 | tf_op jit(solution)/shard_map/ppermute | solution.py:426
  64.3 36.6 %all-to-all-start.2 = ((bf16[4,192,1152]{2,1,0:T(8,128)(2,1)}), bf16[4,192,1152]{2,1,0:T(8,128)(2,1)S(1)}, u32[]{:S(2)}, u32[]{:S(2)}) async-start(bf16[4,192,1152]{2,1,0:T(8,128)(2,1)} %weight_share.1.refs_12_), calls=%async_computation.2 | async-start | bytes 3538944 | tf_op jit(solution)/shard_map/all_to_all | solution.py:484
  77.7 22.6 %copy-start = (bf16[64,1792]{1,0:T(8,128)(2,1)S(1)}, bf16[64,1792]{1,0:T(8,128)(2,1)}, u32[]{:S(2)}) copy-start(bf16[64,1792]{1,0:T(8,128)(2,1)} %get-tuple-element.71.refs_0_) | copy-start | bytes 688132
  77.7 3.0 %collective-permute-start.13 = (bf16[4,240,384]{2,1,0:T(8,128)(2,1)}, bf16[4,240,384]{2,1,0:T(8,128)(2,1)S(1)}, u32[]{:S(2)}, u32[]{:S(2)}) collective-permute-start(bf16[4,240,384]{2,1,0:T(8,128)(2,1)} %get-tuple-element.77), channel_id=1, source_target_pairs={{0,4},{4,0},{8,12},{12,8},{16,20},{20,16},{24,28},{28,24},{1,5},{5... | collective-permute-start | bytes 2211848 | tf_op jit(solution)/shard_map/ppermute | solution.py:428
  78.3 7.4 %collective-permute-start.10 = (bf16[64,1792]{1,0:T(8,128)(2,1)}, bf16[64,1792]{1,0:T(8,128)(2,1)S(1)}, u32[]{:S(2)}, u32[]{:S(2)}) collective-permute-start(bf16[64,1792]{1,0:T(8,128)(2,1)} %get-tuple-element.72), channel_id=1, source_target_pairs={{0,1},{1,2},{2,3},{3,0},{4,5},{5,6},{6,7},{7,4},{8,9},{9,10},{10,1... | collective-permute-start | bytes 688136 | tf_op jit(solution)/shard_map/ppermute | solution.py:426
  78.3 20.2 %collective-permute-start.11 = (bf16[64,1792]{1,0:T(8,128)(2,1)}, bf16[64,1792]{1,0:T(8,128)(2,1)S(1)}, u32[]{:S(2)}, u32[]{:S(2)}) collective-permute-start(bf16[64,1792]{1,0:T(8,128)(2,1)} %get-tuple-element.73), channel_id=1, source_target_pairs={{0,2},{1,3},{2,0},{3,1},{4,6},{5,7},{6,4},{7,5},{8,10},{9,11},{10,... | collective-permute-start | bytes 688136 | tf_op jit(solution)/shard_map/ppermute | solution.py:426
  79.3 21.1 %collective-permute-start.12 = (bf16[64,1792]{1,0:T(8,128)(2,1)}, bf16[64,1792]{1,0:T(8,128)(2,1)S(1)}, u32[]{:S(2)}, u32[]{:S(2)}) collective-permute-start(bf16[64,1792]{1,0:T(8,128)(2,1)} %get-tuple-element.74), channel_id=1, source_target_pairs={{0,3},{1,0},{2,1},{3,2},{4,7},{5,4},{6,5},{7,6},{8,11},{9,8},{10,9... | collective-permute-start | bytes 688136 | tf_op jit(solution)/shard_map/ppermute | solution.py:426
  82.3 18.4 %collective-permute-start.14 = (bf16[240,384]{1,0:T(8,128)(2,1)S(1)}, bf16[240,384]{1,0:T(8,128)(2,1)S(1)}, u32[]{:S(2)}, u32[]{:S(2)}) collective-permute-start(bf16[240,384]{1,0:T(8,128)(2,1)S(1)} %get-tuple-element.79), channel_id=1, source_target_pairs={{0,8},{4,12},{8,0},{12,4},{16,24},{20,28},{24,16},{28,20},{1,9},{5... | collective-permute-start | bytes 552968 | tf_op jit(solution)/shard_map/ppermute | solution.py:428
  84.0 16.7 %collective-permute-start.15 = (bf16[240,384]{1,0:T(8,128)(2,1)S(1)}, bf16[240,384]{1,0:T(8,128)(2,1)S(1)}, u32[]{:S(2)}, u32[]{:S(2)}) collective-permute-start(bf16[240,384]{1,0:T(8,128)(2,1)S(1)} %get-tuple-element.80), channel_id=1, source_target_pairs={{0,16},{4,20},{8,24},{12,28},{16,0},{20,4},{24,8},{28,12},{1,17},{... | collective-permute-start | bytes 552968 | tf_op jit(solution)/shard_map/ppermute | solution.py:428
  85.7 15.1 %collective-permute-start.16 = (bf16[240,384]{1,0:T(8,128)(2,1)S(1)}, bf16[240,384]{1,0:T(8,128)(2,1)S(1)}, u32[]{:S(2)}, u32[]{:S(2)}) collective-permute-start(bf16[240,384]{1,0:T(8,128)(2,1)S(1)} %get-tuple-element.81), channel_id=1, source_target_pairs={{0,24},{4,28},{8,16},{12,20},{16,8},{20,12},{24,0},{28,4},{1,25},{... | collective-permute-start | bytes 552968 | tf_op jit(solution)/shard_map/ppermute | solution.py:428
  100.9 3.9 %collective-permute-start.20 = (bf16[4,192,1152]{2,1,0:T(8,128)(2,1)S(1)}, bf16[4,192,1152]{2,1,0:T(8,128)(2,1)S(1)}, u32[]{:S(2)}, u32[]{:S(2)}) collective-permute-start(bf16[4,192,1152]{2,1,0:T(8,128)(2,1)S(1)} %gate.3.mine), channel_id=1, source_target_pairs={{0,4},{4,0},{8,12},{12,8},{16,20},{20,16},{24,28},{28,24},{1,5},{5... | collective-permute-start | bytes 5308424 | tf_op jit(solution)/shard_map/ppermute | solution.py:428
  101.5 6.8 %collective-permute-start.17 = (bf16[256,384]{1,0:T(8,128)(2,1)S(1)}, bf16[256,384]{1,0:T(8,128)(2,1)S(1)}, u32[]{:S(2)}, u32[]{:S(2)}) collective-permute-start(bf16[256,384]{1,0:T(8,128)(2,1)S(1)} %chip_sum.1.__1_.refs_0_), channel_id=1, source_target_pairs={{0,8},{4,12},{8,0},{12,4},{16,24},{20,28},{24,16},{28,20},{1,9},{5... | collective-permute-start | bytes 589832 | tf_op jit(solution)/shard_map/ppermute | solution.py:428
  103.2 9.2 %collective-permute-start.18 = (bf16[256,384]{1,0:T(8,128)(2,1)S(1)}, bf16[256,384]{1,0:T(8,128)(2,1)S(1)}, u32[]{:S(2)}, u32[]{:S(2)}) collective-permute-start(bf16[256,384]{1,0:T(8,128)(2,1)S(1)} %chip_sum.1.__1_.refs_0_), channel_id=1, source_target_pairs={{0,16},{4,20},{8,24},{12,28},{16,0},{20,4},{24,8},{28,12},{1,17},{... | collective-permute-start | bytes 589832 | tf_op jit(solution)/shard_map/ppermute | solution.py:428
  104.4 9.3 %collective-permute-start.19 = (bf16[256,384]{1,0:T(8,128)(2,1)S(1)}, bf16[256,384]{1,0:T(8,128)(2,1)S(1)}, u32[]{:S(2)}, u32[]{:S(2)}) collective-permute-start(bf16[256,384]{1,0:T(8,128)(2,1)S(1)} %chip_sum.1.__1_.refs_0_), channel_id=1, source_target_pairs={{0,24},{4,28},{8,16},{12,20},{16,8},{20,12},{24,0},{28,4},{1,25},{... | collective-permute-start | bytes 589832 | tf_op jit(solution)/shard_map/ppermute | solution.py:428
  113.7 3.0 %collective-permute-start.21 = (bf16[976,384]{1,0:T(8,128)(2,1)S(1)}, bf16[976,384]{1,0:T(8,128)(2,1)S(1)}, u32[]{:S(2)}, u32[]{:S(2)}) collective-permute-start(bf16[976,384]{1,0:T(8,128)(2,1)S(1)} %kernel_grad_half.1.refs_0_), channel_id=1, source_target_pairs={{0,4},{4,0},{8,12},{12,8},{16,20},{20,16},{24,28},{28,24},{1,5},{5... | collective-permute-start | bytes 2248712 | tf_op jit(solution)/shard_map/ppermute | solution.py:428

commit v5 on v4

--- a/solution.py
+++ b/solution.py
@@ -63,6 +63,8 @@
             operands[i] = In(landed[k], pltpu.make_async_copy(ins[i], landed[k], in_sems.at[k]))
         pairs = [*zip(made, targets), *zip(saved, places), *zip(fetched, nears)]
         copies = [pltpu.make_async_copy(v, t, out_sems.at[k]) for k, (v, t) in enumerate(pairs)]
+        operands += [In(t, copy) for t, copy in zip(nears, copies[len(pairs) - len(nears) :])]
+        copies = copies[: len(pairs) - len(nears)]
         gone = [False] * len(made)
 
         def go(ref):
@@ -166,14 +168,11 @@
 def mid_kernel(n, c, chans, ins, outs, go):
     me = lax.axis_index("seq")
     cot, w = ins[:2]
-    stays = outs[n:]
     g, w = cot()[...], w()
     for k in range(n):
         at = pl.multiple_of(lax.rem(me + k, n) * c, c & -c)
         rows = jnp.concatenate([w[pl.ds(at, c), :], w[pl.ds(chans + at, c), :]], axis=0)
         outs[k][...] = dot_nt(g, rows).astype(BF16)
-    for v, stay in zip(ins, stays):
-        stay[...] = v()[...]
 
 
 def conv_kernel_fwd(n, c, chans, ins, outs, go, xs):
@@ -210,7 +209,7 @@
     me = lax.axis_index("seq")
     blocks, mids = ins[:n], ins[n : 2 * n]
     gains, cot, w = ins[2 * n :]
-    nmt, rtwo, *msgs, qkv, part = outs
+    nmt, rtwo, qkv, part, *msgs = outs
     squares = 0.0
     for v in blocks:
         v = v()[...].astype(F32)
@@ -228,6 +227,8 @@
     go(nmt)
     half, wide = mids[0].ref.shape
     q = dot_tn(nmt[...], w()[...])
+    qkv[...] = q.astype(BF16)
+    go(qkv)
     row = jnp.sum(q * cot()[...].astype(F32), axis=1, keepdims=True)
     row = jnp.broadcast_to(row, (row.shape[0], 128)).T[:8, :]
     part[...] = row
@@ -238,10 +239,9 @@
             msgs[k][:half, :] = mids[k]()[...]
             msgs[k][half:, :] = in_two(row)
             go(msgs[k])
-    qkv[...] = q.astype(BF16)
-
-
-def back_kernel(n, c, chans, m, ins, outs, go, evens, odds, whole):
+
+
+def back_kernel(n, c, chans, m, ins, outs, go, evens, odds, whole, spare):
     seq_at = lax.axis_index("seq")
     core = lax.rem(lax.axis_index("dp"), 2)
     mids, parts = ins[:n], ins[n:-8]
@@ -297,7 +297,7 @@
         means = jnp.where(lane == h, jnp.mean(placed * aone, axis=1, keepdims=True), means)
         total = (placed + rone[:, h : h + 1] * gin * ng).astype(BF16)
         whole[:, h * chans : (h + 1) * chans] = total
-    whole[:, width : width + 128] = means.astype(BF16)
+    spare[...] = means
     mid = jnp.sum(mid * atwo, axis=0, keepdims=True)
     short = -2 * c % 128
     if short:
@@ -310,9 +310,11 @@
     gains = in_two(gains)
     for k in range(n):
         at = pl.multiple_of(lax.rem(seq_at + k, n) * block, block)
-        msgs[k][:, : width + 128] = whole[pl.ds(at, block), :]
-        msgs[k][:, width + 128 :] = jnp.zeros((block, 128), BF16)
-        msgs[k][:32, width + 128 :] = gains
+        msgs[k][:, :width] = whole[pl.ds(at, block), :]
+        msgs[k][:, width:] = jnp.zeros((block, 128), BF16)
+        msgs[k][:32, width:] = gains
+        mean = spare[pl.ds(at, block), :].T[:16, :]
+        msgs[k][32:48, width : width + block] = mean.astype(BF16)
         go(msgs[k])
 
 
@@ -379,8 +381,9 @@
         side = pl.multiple_of(which * wide, wide & -wide)
         taps[:, pl.ds(side, wide)] = v()[:rows, :]
         total = total + joined(v()[rows:, :])
-    gain_in[...] = total[:2, :]
-    gain_mid[...] = total[2 : 2 + n, : 2 * c]
+    gain_in[...] = jnp.concatenate([total[0:1, :], total[1:2, :]], axis=1).reshape(gain_in.shape)
+    pieces = [total[2 + b : 3 + b, h * c : (h + 1) * c] for h in range(2) for b in range(n)]
+    gain_mid[...] = jnp.concatenate(pieces, axis=1).reshape(gain_mid.shape)
 
 
 def weave_kernel(mine, other, *refs):
@@ -400,16 +403,18 @@
     me = lax.axis_index("seq")
     got, own = ins[:n], ins[n]
     out, gains = outs
-    total = got[0]()[:, : 2 * chans + 128].astype(F32)
+    total = got[0]()[...].astype(F32)
     for v in got[1:]:
-        total = total + v()[:, : 2 * chans + 128].astype(F32)
+        total = total + v()[...].astype(F32)
     for k in range(n):
-        gains[lax.rem(me - k + n, n)] = joined(got[k]()[:32, 2 * chans + 128 :])
+        gains[lax.rem(me - k + n, n)] = joined(got[k]()[:32, 2 * chans :])
+    rows = total.shape[0]
+    means = jnp.concatenate([total[32:48, 2 * chans :]] * 8, axis=0).T
     for h in range(2):
         x = own()[:, h * chans : (h + 1) * chans].astype(F32)
         a = x * inv_rms(x)
         t = total[:, h * chans : (h + 1) * chans]
-        mean = total[:, 2 * chans + h : 2 * chans + h + 1]
+        mean = means[:rows, h : h + 1]
         v = t - a * (jnp.mean(t * a, axis=-1, keepdims=True) - mean)
         out[:, h * chans : (h + 1) * chans] = v.astype(BF16)
 
@@ -424,7 +429,7 @@
     half = length // 2 * n
     scale = 1.0 / math.sqrt(m * half)
     shift = lambda v, k: lax.ppermute(v, "seq", [(i, (i + k) % n) for i in range(n)])
-    from_ring = lambda v: [v] + [shift(v, k) for k in range(1, n)]
+    from_all = lambda v: [v] + [shift(v, k) for k in range(1, n)]
     across = lambda v, k: lax.ppermute(v, "dp", [(i, i ^ k) for i in range(m)])
     same_core = [[i for i in range(m) if i % 2 == core] for core in range(2)]
     chips = m // 2
@@ -432,7 +437,7 @@
 
     taps_rows = conv_kernel.transpose(0, 2, 1).reshape(5 * c, chans)
     own = x.reshape(length // 2, width)
-    xs = from_ring(own)
+    xs = from_all(own)
     gin = gain_in.reshape(1, chans)
     gmid = gain_mid.reshape(2, n, c).transpose(1, 0, 2).reshape(n, 2 * c)
     cots = jnp.broadcast_to(cot[None], (chips, *cot.shape))
@@ -440,8 +445,9 @@
     used = [cot, qkv_weight, taps_rows, gin, gmid]
     held = call(
         functools.partial(mid_kernel, n, c, chans),
-        [*map(Far, used)],
-        kept=[shaped((half, 2 * c), BF16)] * n + [shaped(v.shape, v.dtype) for v in used],
+        [],
+        kept=[shaped((half, 2 * c), BF16)] * n,
+        fetch=used,
         flops=WAIT,
         name="mid_parts",
     )
@@ -460,20 +466,25 @@
         scratch=[pltpu.VMEM((half, width), BF16)],
         name="conv_forward",
     )
-    blocks = from_ring(pooled_msg)
+    blocks = from_all(pooled_msg)
     rides = half <= 2 * c
-    nmt, rtwo, *tailed, qkv, part, pooled, conv_out, nin, rone = call(
+    nmt, rtwo, qkv, part, *tailed, pooled, conv_out, nin, rone = call(
         functools.partial(qkv_kernel, n, c, chans),
         [*blocks, *mid_msgs, gmid, cot, weight],
-        outs=[shaped((width, half), BF16), shaped((half, 1), F32)] + [shaped((half + 16, 2 * c), BF16)] * (n * rides),
-        free=[shaped((half, cols), BF16), shaped((8, half), F32)],
+        outs=[
+            shaped((width, half), BF16),
+            shaped((half, 1), F32),
+            shaped((half, cols), BF16),
+            shaped((8, half), F32),
+        ]
+        + [shaped((half + 16, 2 * c), BF16)] * (n * rides),
         spill=states,
         name="qkv",
     )
     cots = gate(cots, nmt, pltpu.HBM)
     mid_msgs = tailed if rides else mid_msgs
     mids = [mid_msgs[0]] + [shift(mid_msgs[k], k) for k in range(1, n)]
-    parts = [] if rides else from_ring(part)
+    parts = [] if rides else from_all(part)
     nms = lax.all_to_all(nmt.reshape(m, width // m, half), "dp", 0, 0, tiled=True)
     (wshare,) = call(
         functools.partial(weight_kernel, m, scale),
@@ -499,11 +510,12 @@
             shaped((chips, rows, wide), BF16),
             shaped((chips, rows, wide), F32),
         ]
-        + [shaped((half // n, width + 256), BF16)] * n,
+        + [shaped((half // n, width + 128), BF16)] * n,
         scratch=[
             pltpu.VMEM((half, 5 * c), BF16),
             pltpu.VMEM((half, 5 * c), BF16),
-            pltpu.VMEM((half, width + 128), BF16),
+            pltpu.VMEM((half, width), BF16),
+            pltpu.VMEM((half, 128), F32),
         ],
         after=[wshare],
         flops=WAIT,
@@ -553,7 +565,7 @@
         taps_grad, gain_in_grad, gain_mid_grad = call(
             functools.partial(place_kernel, n, c),
             [mine, across(mine, 1)],
-            free=[shaped((5 * c, chans), BF16), shaped((2, wide), F32), shaped((n, 2 * c), F32)],
+            free=[shaped((5 * c, chans), BF16), shaped((chans,), F32), shaped((width,), F32)],
             name="kernel_grad",
         )
     else:
@@ -576,12 +588,13 @@
         )(within(whalf), within(across(whalf, 1)))
         gain_in_grad = jnp.sum(gains[:, : chans // 128], axis=0)
         gain_mid_grad = gains[:, chans // 128 :].reshape(n, -1)[:, : 2 * c]
+        gain_mid_grad = gain_mid_grad.reshape(n, 2, c).transpose(1, 0, 2)
     return (
         qkv[None],
         input_grad.reshape(1, length, chans),
         taps_grad.reshape(5, c, chans).transpose(0, 2, 1),
         gain_in_grad.reshape(chans),
-        gain_mid_grad.reshape(n, 2, c).transpose(1, 0, 2).reshape(width),
+        gain_mid_grad.reshape(width),
         weight_grad.reshape(width, cols),
     )
 

time: 120 us -> 116 us (0.967)
  Pallas kernels: 25.3 us -> 23.9 us
  local copies, waits for them, and re-layouts: 7.12 us -> 5.75 us
    pallas_call x10, Pallas kernels: 23.5 us -> 22.1 us  [call(): pl.pallas_call(whole, out_shape=tuple([*memory(pltpu.HBM, outs), *free, *...]
    reshape x4 -> x0, local copies, waits for them, and re-layouts: 1.37 us -> none  [the longest x3 0.77 us: body(): gain_mid_grad.reshape(n, 2, c).transpose(1, 0, 2).reshape(width)]
  transfers between devices with their start and end apart: 25 -> 25, of which waited for: 16 -> 16; matrix products, arithmetic and copies ran while one was open for 4% -> 4% of each run, Pallas kernels for 20% -> 19%
where the time goes in v5:
time: 116 us
  waiting for transfers between devices  49.5 us (43%)
  starting transfers between devices  35.6 us (31%)
  Pallas kernels  23.9 us (21%)
  local copies, waits for them, and re-layouts  5.75 us (5%)
    ppermute x12, waiting for transfers between devices, body(): lax.ppermute(v, 'seq', [(i, (i + k) % n) for i in range(n)])  35.5 us
    pallas_call x10, Pallas kernels, call(): pl.pallas_call(whole, out_shape=tuple([*memory(pltpu.HBM, outs), *free, *...  22.1 us
    ppermute x12, starting transfers between devices, body(): lax.ppermute(v, 'seq', [(i, (i + k) % n) for i in range(n)])  11.7 us
    ppermute x10, starting transfers between devices, body(): across = lambda v, k: lax.ppermute(v, 'dp', [(i, i ^ k) for i in range(m)])  10.9 us
    ppermute x10, waiting for transfers between devices, body(): across = lambda v, k: lax.ppermute(v, 'dp', [(i, i ^ k) for i in range(m)])  8.52 us
    all_to_all x1, waiting for transfers between devices, body(): lax.all_to_all(nmt.reshape(m, width // m, half), 'dp', 0, 0, tiled=True)  5.48 us
    all_to_all x1, starting transfers between devices, body(): lax.all_to_all(cots, 'dp', 0, 0, axis_index_groups=same_core, tiled=True)  4.65 us
    all_to_all x1, starting transfers between devices, body(): lax.all_to_all(wshare, 'dp', 0, 0, axis_index_groups=same_core, tiled=True)  4.54 us
  transfers between devices with their start and end apart: 25, of which 16 were waited for; matrix products, arithmetic and copies ran while one was open for 4% of the time, Pallas kernels for 19%

profile of v5, /device:TPU:9, one launch (start us, length us, event | category | flops | bytes accessed | tf_op | source)
XLA Modules:
  0.0 115.6 jit_solution(4175435641582834683)
XLA Ops:
  1.6 1.3 %collective-permute-start = (bf16[64,1536]{1,0:T(8,128)(2,1)S(1)}, bf16[64,1536]{1,0:T(8,128)(2,1)S(1)}, u32[]{:S(2)}, u32[]{:S(2)}) collective-permute-start(bf16[64,1536]{1,0:T(8,128)(2,1)S(1)} %reshape_squeeze.3.refs_0_.refs_4_), channel_id=1, source_target_pairs={{0,1},{1,2},{2,3},{3,0},{4,5},{5,6},{6,7},{7,4},{8,9},{9,10},{10,1... | collective-permute-start | bytes 589832 | tf_op jit(solution)/shard_map/ppermute | solution.py:431
  4.1 1.4 %collective-permute-start.2 = (bf16[64,1536]{1,0:T(8,128)(2,1)S(1)}, bf16[64,1536]{1,0:T(8,128)(2,1)S(1)}, u32[]{:S(2)}, u32[]{:S(2)}) collective-permute-start(bf16[64,1536]{1,0:T(8,128)(2,1)S(1)} %reshape_squeeze.3.refs_0_.refs_4_), channel_id=1, source_target_pairs={{0,3},{1,0},{2,1},{3,2},{4,7},{5,4},{6,5},{7,6},{8,11},{9,8},{10,9... | collective-permute-start | bytes 589832 | tf_op jit(solution)/shard_map/ppermute | solution.py:431
  5.5 2.6 %broadcast_in_dim.9 = bf16[4,256,1152]{2,1,0:T(8,128)(2,1)} broadcast(bf16[256,1152]{1,0:T(8,128)(2,1)} %bitcast.12), dimensions={1,2} | broadcast | bytes 2949120 | tf_op jit(solution)/shard_map/broadcast_in_dim | solution.py:443
  8.1 4.6 %all-to-all-start.1 = ((bf16[4,256,1152]{2,1,0:T(8,128)(2,1)}), bf16[4,256,1152]{2,1,0:T(8,128)(2,1)}, u32[]{:S(2)}, u32[]{:S(2)}) async-start(bf16[4,256,1152]{2,1,0:T(8,128)(2,1)} %broadcast_in_dim.9), calls=%async_computation.1 | async-start | bytes 4718592 | tf_op jit(solution)/shard_map/all_to_all | solution.py:444
  14.1 3.8 %mid_parts.1 = (bf16[256,384]{1,0:T(8,128)(2,1)S(1)}, bf16[256,384]{1,0:T(8,128)(2,1)S(1)}, bf16[256,384]{1,0:T(8,128)(2,1)S(1)}, bf16[256,384]{1,0:T(8,128)(2,1...) custom-call(bf16[256,1152]{1,0:T(8,128)(2,1)} %bitcast.13, ...), custom_call_target="tpu_custom_call" | custom-call | flops 40000000000 | tf_op jit(solution)/shard_map/mid_parts/pallas_call | solution.py:90
  17.9 1.3 %collective-permute-done.1.refs_2_ = bf16[64,1536]{1,0:T(8,128)(2,1)S(1)} collective-permute-done((bf16[64,1536]{1,0:T(8,128)(2,1)S(1)}, bf16[64,1536]{1,0:T(8,128)(2,1)S(1)}, u32[]{:S(2)}, u32[]{:S(2)}) %collective-permute-start.1) | collective-permute-done | bytes 196640 | tf_op jit(solution)/shard_map/ppermute | solution.py:431
  19.2 2.9 %collective-permute-done.2.refs_3_ = bf16[64,1536]{1,0:T(8,128)(2,1)S(1)} collective-permute-done((bf16[64,1536]{1,0:T(8,128)(2,1)S(1)}, bf16[64,1536]{1,0:T(8,128)(2,1)S(1)}, u32[]{:S(2)}, u32[]{:S(2)}) %collective-permute-start.2) | collective-permute-done | bytes 196640 | tf_op jit(solution)/shard_map/ppermute | solution.py:431
  22.1 1.9 %conv_forward.1 = (bf16[256,384]{1,0:T(8,128)(2,1)S(1)}, f32[256,384]{1,0:T(8,128)S(1)}, f32[256,384]{1,0:T(8,128)S(1)}, bf16[256,1536]{1,0:T(8,128)(2,1)S(1)}, f32[256,2]{1,0:T(8,128)S(1)}) custom-call(bf16[64,1536]{1,0:T(8,128)(2,1)S(1)} %reshape_squeeze.3.refs_0_.refs_4_, bf16[64,1536]{1,0:T(8,128)(2,1)S(1)} %collective-permute-done.refs_1_, ...), custom_call_target="tpu_custom_call" | custom-call | tf_op jit(solution)/shard_map/conv_forward/pallas_call | solution.py:90
  24.4 1.4 %collective-permute-start.5 = (bf16[256,384]{1,0:T(8,128)(2,1)S(1)}, bf16[256,384]{1,0:T(8,128)(2,1)S(1)}, u32[]{:S(2)}, u32[]{:S(2)}) collective-permute-start(bf16[256,384]{1,0:T(8,128)(2,1)S(1)} %get-tuple-element.48.refs_0_), channel_id=1, source_target_pairs={{0,3},{1,0},{2,1},{3,2},{4,7},{5,4},{6,5},{7,6},{8,11},{9,8},{10,9... | collective-permute-start | bytes 589832 | tf_op jit(solution)/shard_map/ppermute | solution.py:431
  25.8 4.5 %collective-permute-done.3.refs_1_ = bf16[256,384]{1,0:T(8,128)(2,1)S(1)} collective-permute-done((bf16[256,384]{1,0:T(8,128)(2,1)S(1)}, bf16[256,384]{1,0:T(8,128)(2,1)S(1)}, u32[]{:S(2)}, u32[]{:S(2)}) %collective-permute-start.3) | collective-permute-done | bytes 196640 | tf_op jit(solution)/shard_map/ppermute | solution.py:431
  30.3 10.7 %collective-permute-done.4.refs_2_ = bf16[256,384]{1,0:T(8,128)(2,1)S(1)} collective-permute-done((bf16[256,384]{1,0:T(8,128)(2,1)S(1)}, bf16[256,384]{1,0:T(8,128)(2,1)S(1)}, u32[]{:S(2)}, u32[]{:S(2)}) %collective-permute-start.4) | collective-permute-done | bytes 196640 | tf_op jit(solution)/shard_map/ppermute | solution.py:431
  40.9 1.4 %collective-permute-done.5.refs_3_ = bf16[256,384]{1,0:T(8,128)(2,1)S(1)} collective-permute-done((bf16[256,384]{1,0:T(8,128)(2,1)S(1)}, bf16[256,384]{1,0:T(8,128)(2,1)S(1)}, u32[]{:S(2)}, u32[]{:S(2)}) %collective-permute-start.5) | collective-permute-done | bytes 196640 | tf_op jit(solution)/shard_map/ppermute | solution.py:431
  42.3 3.0 %qkv.1 = (bf16[1536,256]{1,0:T(8,128)(2,1)}, f32[256,1]{1,0:T(8,128)}, bf16[256,1152]{1,0:T(8,128)(2,1)}, f32[8,256]{1,0:T(8,128)}, bf16[272,384]{1,0:T(8,128)(2...) custom-call(bf16[256,384]{1,0:T(8,128)(2,1)S(1)} %get-tuple-element., ...), custom_call_target="tpu_custom_call" | custom-call | tf_op jit(solution)/shard_map/qkv/pallas_call | solution.py:90
  46.0 3.8 %all-to-all-start = ((bf16[8,192,256]{2,1,0:T(8,128)(2,1)}), bf16[8,192,256]{2,1,0:T(8,128)(2,1)S(1)}, u32[]{:S(2)}, u32[]{:S(2)}) async-start(bf16[8,192,256]{2,1,0:T(8,128)(2,1)} %bitcast.6), calls=%async_computation | async-start | bytes 1572864 | tf_op jit(solution)/shard_map/all_to_all | solution.py:488
  49.8 2.2 %collective-permute-start.7 = (bf16[272,384]{1,0:T(8,128)(2,1)S(1)}, bf16[272,384]{1,0:T(8,128)(2,1)S(1)}, u32[]{:S(2)}, u32[]{:S(2)}) collective-permute-start(bf16[272,384]{1,0:T(8,128)(2,1)S(1)} %copy-done.4), channel_id=1, source_target_pairs={{0,2},{1,3},{2,0},{3,1},{4,6},{5,7},{6,4},{7,5},{8,10},{9,11},{10,... | collective-permute-start | bytes 626696 | tf_op jit(solution)/shard_map/ppermute | solution.py:431
  52.0 1.4 %collective-permute-start.8 = (bf16[272,384]{1,0:T(8,128)(2,1)S(1)}, bf16[272,384]{1,0:T(8,128)(2,1)S(1)}, u32[]{:S(2)}, u32[]{:S(2)}) collective-permute-start(bf16[272,384]{1,0:T(8,128)(2,1)S(1)} %copy-done.3), channel_id=1, source_target_pairs={{0,3},{1,0},{2,1},{3,2},{4,7},{5,4},{6,5},{7,6},{8,11},{9,8},{10,9... | collective-permute-start | bytes 626696 | tf_op jit(solution)/shard_map/ppermute | solution.py:431
  53.4 5.5 %all-to-all-done.refs_0_ = bf16[8,192,256]{2,1,0:T(8,128)(2,1)S(1)} async-done(((bf16[8,192,256]{2,1,0:T(8,128)(2,1)}), bf16[8,192,256]{2,1,0:T(8,128)(2,1)S(1)}, u32[]{:S(2)}, u32[]{:S(2)}) %all-to-all-start) | async-done | bytes 786464 | tf_op jit(solution)/shard_map/all_to_all | solution.py:488
  58.9 4.3 %weight_share.1.refs_12_ = bf16[4,192,1152]{2,1,0:T(8,128)(2,1)} custom-call(bf16[8,192,256]{2,1,0:T(8,128)(2,1)S(1)} %all-to-all-done.refs_0_, bf16[4,256,1152]{2,1,0:T(8,128)(2,1)} %gate.2.refs_1_, bf16[4,256,1152]{2,1,0:T(8,128)(2,1)} %collective-permute-done.9.refs_2_), custom_call_target="tpu_custom_call" | custom-call | tf_op jit(solution)/shard_map/weight_share/pallas_call | solution.py:90
  63.2 4.5 %all-to-all-start.2 = ((bf16[4,192,1152]{2,1,0:T(8,128)(2,1)}), bf16[4,192,1152]{2,1,0:T(8,128)(2,1)S(1)}, u32[]{:S(2)}, u32[]{:S(2)}) async-start(bf16[4,192,1152]{2,1,0:T(8,128)(2,1)} %weight_share.1.refs_12_), calls=%async_computation.2 | async-start | bytes 3538944 | tf_op jit(solution)/shard_map/all_to_all | solution.py:495
  67.9 3.1 %collective-permute-done.8.refs_3_ = bf16[272,384]{1,0:T(8,128)(2,1)S(1)} collective-permute-done((bf16[272,384]{1,0:T(8,128)(2,1)S(1)}, bf16[272,384]{1,0:T(8,128)(2,1)S(1)}, u32[]{:S(2)}, u32[]{:S(2)}) %collective-permute-start.8) | collective-permute-done | bytes 208928 | tf_op jit(solution)/shard_map/ppermute | solution.py:431
  71.1 5.6 %conv_backward.1 = (bf16[4,240,384]{2,1,0:T(8,128)(2,1)}, f32[4,240,384]{2,1,0:T(8,128)}, bf16[64,1664]{1,0:T(8,128)(2,1)}, bf16[64,1664]{1,0:T(8,128)(2,1)}, bf...) custom-call(bf16[272,384]{1,0:T(8,128)(2,1)} %get-tuple-element.61.refs_0_, ...), custom_call_target="tpu_custom_call" | custom-call | flops 40000000000 | tf_op jit(solution)/shard_map/conv_backward/pallas_call | solution.py:90
  78.2 1.5 %collective-permute-start.12 = (bf16[64,1664]{1,0:T(8,128)(2,1)}, bf16[64,1664]{1,0:T(8,128)(2,1)S(1)}, u32[]{:S(2)}, u32[]{:S(2)}) collective-permute-start(bf16[64,1664]{1,0:T(8,128)(2,1)} %get-tuple-element.74), channel_id=1, source_target_pairs={{0,3},{1,0},{2,1},{3,2},{4,7},{5,4},{6,5},{7,6},{8,11},{9,8},{10,9... | collective-permute-start | bytes 638984 | tf_op jit(solution)/shard_map/ppermute | solution.py:431
  79.7 1.6 %core_sum.1 = (bf16[240,384]{1,0:T(8,128)(2,1)S(1)}, bf16[240,384]{1,0:T(8,128)(2,1)S(1)}, bf16[240,384]{1,0:T(8,128)(2,1)S(1)}, f32[240,384]{1,0:T(8,128)S(1)}) custom-call(f32[4,240,384]{2,1,0:T(8,128)} %get-tuple-element.76.refs_0_, bf16[4,240,384]{2,1,0:T(8,128)(2,1)S(1)} %collective-permute-done.13.refs_1_), custom_call_target="tpu_custom_call" | custom-call | tf_op jit(solution)/shard_map/core_sum/pallas_call | solution.py:90
  81.3 1.7 %collective-permute-start.14 = (bf16[240,384]{1,0:T(8,128)(2,1)S(1)}, bf16[240,384]{1,0:T(8,128)(2,1)S(1)}, u32[]{:S(2)}, u32[]{:S(2)}) collective-permute-start(bf16[240,384]{1,0:T(8,128)(2,1)S(1)} %get-tuple-element.79), channel_id=1, source_target_pairs={{0,8},{4,12},{8,0},{12,4},{16,24},{20,28},{24,16},{28,20},{1,9},{5... | collective-permute-start | bytes 552968 | tf_op jit(solution)/shard_map/ppermute | solution.py:433
  84.3 2.3 %collective-permute-start.16 = (bf16[240,384]{1,0:T(8,128)(2,1)S(1)}, bf16[240,384]{1,0:T(8,128)(2,1)S(1)}, u32[]{:S(2)}, u32[]{:S(2)}) collective-permute-start(bf16[240,384]{1,0:T(8,128)(2,1)S(1)} %get-tuple-element.81), channel_id=1, source_target_pairs={{0,24},{4,28},{8,16},{12,20},{16,8},{20,12},{24,0},{28,4},{1,25},{... | collective-permute-start | bytes 552968 | tf_op jit(solution)/shard_map/ppermute | solution.py:433
  86.6 9.5 %collective-permute-done.11.refs_2_ = bf16[64,1664]{1,0:T(8,128)(2,1)S(1)} collective-permute-done((bf16[64,1664]{1,0:T(8,128)(2,1)}, bf16[64,1664]{1,0:T(8,128)(2,1)S(1)}, u32[]{:S(2)}, u32[]{:S(2)}) %collective-permute-start.11) | collective-permute-done | bytes 213024 | tf_op jit(solution)/shard_map/ppermute | solution.py:431
  96.1 1.8 %collective-permute-done.12.refs_3_ = bf16[64,1664]{1,0:T(8,128)(2,1)S(1)} collective-permute-done((bf16[64,1664]{1,0:T(8,128)(2,1)}, bf16[64,1664]{1,0:T(8,128)(2,1)S(1)}, u32[]{:S(2)}, u32[]{:S(2)}) %collective-permute-start.12) | collective-permute-done | bytes 213024 | tf_op jit(solution)/shard_map/ppermute | solution.py:431
  99.1 1.6 %collective-permute-start.17 = (bf16[256,384]{1,0:T(8,128)(2,1)S(1)}, bf16[256,384]{1,0:T(8,128)(2,1)S(1)}, u32[]{:S(2)}, u32[]{:S(2)}) collective-permute-start(bf16[256,384]{1,0:T(8,128)(2,1)S(1)} %chip_sum.1.__1_.refs_0_), channel_id=1, source_target_pairs={{0,8},{4,12},{8,0},{12,4},{16,24},{20,28},{24,16},{28,20},{1,9},{5... | collective-permute-start | bytes 589832 | tf_op jit(solution)/shard_map/ppermute | solution.py:433
  102.4 1.8 %weight_grad.1.refs_4_ = bf16[4,2,192,1152]{3,2,1,0:T(8,128)(2,1)} custom-call(bf16[4,192,1152]{2,1,0:T(8,128)(2,1)S(1)} %gate.3.mine, bf16[4,192,1152]{2,1,0:T(8,128)(2,1)S(1)} %collective-permute-done.20.other), custom_call_target="tpu_custom_call" | custom-call | tf_op jit(solution)/shard_map/weight_grad/pallas_call | solution.py:547
  104.3 1.6 %collective-permute-done.17.refs_1_ = bf16[256,384]{1,0:T(8,128)(2,1)S(1)} collective-permute-done((bf16[256,384]{1,0:T(8,128)(2,1)S(1)}, bf16[256,384]{1,0:T(8,128)(2,1)S(1)}, u32[]{:S(2)}, u32[]{:S(2)}) %collective-permute-start.17) | collective-permute-done | bytes 196640 | tf_op jit(solution)/shard_map/ppermute | solution.py:433
  105.9 4.1 %collective-permute-done.18.refs_2_ = bf16[256,384]{1,0:T(8,128)(2,1)S(1)} collective-permute-done((bf16[256,384]{1,0:T(8,128)(2,1)S(1)}, bf16[256,384]{1,0:T(8,128)(2,1)S(1)}, u32[]{:S(2)}, u32[]{:S(2)}) %collective-permute-start.18) | collective-permute-done | bytes 196640 | tf_op jit(solution)/shard_map/ppermute | solution.py:433
  114.3 1.3 %kernel_grad.1 = (bf16[960,768]{1,0:T(8,128)(2,1)}, f32[768]{0:T(1024)}, f32[1536]{0:T(1024)}) custom-call(bf16[976,384]{1,0:T(8,128)(2,1)S(1)} %kernel_grad_half.1.refs_0_, bf16[976,384]{1,0:T(8,128)(2,1)S(1)} %collective-permute-done.21.refs_1_), custom_call_target="tpu_custom_call" | custom-call | tf_op jit(solution)/shard_map/kernel_grad/pallas_call | solution.py:90
  (50 shorter events, 14.6 us)
Async XLA Ops:
  1.6 16.3 %collective-permute-start = (bf16[64,1536]{1,0:T(8,128)(2,1)S(1)}, bf16[64,1536]{1,0:T(8,128)(2,1)S(1)}, u32[]{:S(2)}, u32[]{:S(2)}) collective-permute-start(bf16[64,1536]{1,0:T(8,128)(2,1)S(1)} %reshape_squeeze.3.refs_0_.refs_4_), channel_id=1, source_target_pairs={{0,1},{1,2},{2,3},{3,0},{4,5},{5,6},{6,7},{7,4},{8,9},{9,10},{10,1... | collective-permute-start | bytes 589832 | tf_op jit(solution)/shard_map/ppermute | solution.py:431
  3.0 16.2 %collective-permute-start.1 = (bf16[64,1536]{1,0:T(8,128)(2,1)S(1)}, bf16[64,1536]{1,0:T(8,128)(2,1)S(1)}, u32[]{:S(2)}, u32[]{:S(2)}) collective-permute-start(bf16[64,1536]{1,0:T(8,128)(2,1)S(1)} %reshape_squeeze.3.refs_0_.refs_4_), channel_id=1, source_target_pairs={{0,2},{1,3},{2,0},{3,1},{4,6},{5,7},{6,4},{7,5},{8,10},{9,11},{10,... | collective-permute-start | bytes 589832 | tf_op jit(solution)/shard_map/ppermute | solution.py:431
  4.1 18.1 %collective-permute-start.2 = (bf16[64,1536]{1,0:T(8,128)(2,1)S(1)}, bf16[64,1536]{1,0:T(8,128)(2,1)S(1)}, u32[]{:S(2)}, u32[]{:S(2)}) collective-permute-start(bf16[64,1536]{1,0:T(8,128)(2,1)S(1)} %reshape_squeeze.3.refs_0_.refs_4_), channel_id=1, source_target_pairs={{0,3},{1,0},{2,1},{3,2},{4,7},{5,4},{6,5},{7,6},{8,11},{9,8},{10,9... | collective-permute-start | bytes 589832 | tf_op jit(solution)/shard_map/ppermute | solution.py:431
  8.1 4.7 %copy-start.1 = (f32[1536]{0:T(1024)S(1)}, f32[1536]{0:T(1024)}, u32[]{:S(2)}) copy-start(f32[1536]{0:T(1024)} %param.10) | copy-start | bytes 18436
  8.1 5.4 %copy-start.2 = (f32[768]{0:T(1024)S(1)}, f32[768]{0:T(1024)}, u32[]{:S(2)}) copy-start(f32[768]{0:T(1024)} %param.9) | copy-start | bytes 9220
  8.1 37.3 %all-to-all-start.1 = ((bf16[4,256,1152]{2,1,0:T(8,128)(2,1)}), bf16[4,256,1152]{2,1,0:T(8,128)(2,1)}, u32[]{:S(2)}, u32[]{:S(2)}) async-start(bf16[4,256,1152]{2,1,0:T(8,128)(2,1)} %broadcast_in_dim.9), calls=%async_computation.1 | async-start | bytes 4718592 | tf_op jit(solution)/shard_map/all_to_all | solution.py:444
  24.0 6.3 %collective-permute-start.3 = (bf16[256,384]{1,0:T(8,128)(2,1)S(1)}, bf16[256,384]{1,0:T(8,128)(2,1)S(1)}, u32[]{:S(2)}, u32[]{:S(2)}) collective-permute-start(bf16[256,384]{1,0:T(8,128)(2,1)S(1)} %get-tuple-element.48.refs_0_), channel_id=1, source_target_pairs={{0,1},{1,2},{2,3},{3,0},{4,5},{5,6},{6,7},{7,4},{8,9},{9,10},{10,1... | collective-permute-start | bytes 589832 | tf_op jit(solution)/shard_map/ppermute | solution.py:431
  24.1 16.8 %collective-permute-start.4 = (bf16[256,384]{1,0:T(8,128)(2,1)S(1)}, bf16[256,384]{1,0:T(8,128)(2,1)S(1)}, u32[]{:S(2)}, u32[]{:S(2)}) collective-permute-start(bf16[256,384]{1,0:T(8,128)(2,1)S(1)} %get-tuple-element.48.refs_0_), channel_id=1, source_target_pairs={{0,2},{1,3},{2,0},{3,1},{4,6},{5,7},{6,4},{7,5},{8,10},{9,11},{10,... | collective-permute-start | bytes 589832 | tf_op jit(solution)/shard_map/ppermute | solution.py:431
  24.4 17.9 %collective-permute-start.5 = (bf16[256,384]{1,0:T(8,128)(2,1)S(1)}, bf16[256,384]{1,0:T(8,128)(2,1)S(1)}, u32[]{:S(2)}, u32[]{:S(2)}) collective-permute-start(bf16[256,384]{1,0:T(8,128)(2,1)S(1)} %get-tuple-element.48.refs_0_), channel_id=1, source_target_pairs={{0,3},{1,0},{2,1},{3,2},{4,7},{5,4},{6,5},{7,6},{8,11},{9,8},{10,9... | collective-permute-start | bytes 589832 | tf_op jit(solution)/shard_map/ppermute | solution.py:431
  45.4 4.4 %copy-start.5 = (bf16[272,384]{1,0:T(8,128)(2,1)S(1)}, bf16[272,384]{1,0:T(8,128)(2,1)}, u32[]{:S(2)}) copy-start(bf16[272,384]{1,0:T(8,128)(2,1)} %get-tuple-element.62) | copy-start | bytes 626692
  45.4 4.4 %copy-start.4 = (bf16[272,384]{1,0:T(8,128)(2,1)S(1)}, bf16[272,384]{1,0:T(8,128)(2,1)}, u32[]{:S(2)}) copy-start(bf16[272,384]{1,0:T(8,128)(2,1)} %get-tuple-element.63) | copy-start | bytes 626692
  45.4 6.6 %copy-start.3 = (bf16[272,384]{1,0:T(8,128)(2,1)S(1)}, bf16[272,384]{1,0:T(8,128)(2,1)}, u32[]{:S(2)}) copy-start(bf16[272,384]{1,0:T(8,128)(2,1)} %get-tuple-element.64) | copy-start | bytes 626692
  45.4 13.5 %collective-permute-start.9 = (bf16[4,256,1152]{2,1,0:T(8,128)(2,1)}, bf16[4,256,1152]{2,1,0:T(8,128)(2,1)}, u32[]{:S(2)}, u32[]{:S(2)}) collective-permute-start(bf16[4,256,1152]{2,1,0:T(8,128)(2,1)} %gate.2.refs_1_), channel_id=1, source_target_pairs={{0,4},{4,0},{8,12},{12,8},{16,20},{20,16},{24,28},{28,24},{1,5},{5... | collective-permute-start | bytes 7077896 | tf_op jit(solution)/shard_map/ppermute | solution.py:433
  46.0 12.9 %all-to-all-start = ((bf16[8,192,256]{2,1,0:T(8,128)(2,1)}), bf16[8,192,256]{2,1,0:T(8,128)(2,1)S(1)}, u32[]{:S(2)}, u32[]{:S(2)}) async-start(bf16[8,192,256]{2,1,0:T(8,128)(2,1)} %bitcast.6), calls=%async_computation | async-start | bytes 1572864 | tf_op jit(solution)/shard_map/all_to_all | solution.py:488
  49.8 18.0 %collective-permute-start.6 = (bf16[272,384]{1,0:T(8,128)(2,1)S(1)}, bf16[272,384]{1,0:T(8,128)(2,1)S(1)}, u32[]{:S(2)}, u32[]{:S(2)}) collective-permute-start(bf16[272,384]{1,0:T(8,128)(2,1)S(1)} %copy-done.5), channel_id=1, source_target_pairs={{0,1},{1,2},{2,3},{3,0},{4,5},{5,6},{6,7},{7,4},{8,9},{9,10},{10,1... | collective-permute-start | bytes 626696 | tf_op jit(solution)/shard_map/ppermute | solution.py:431
  49.8 18.2 %collective-permute-start.7 = (bf16[272,384]{1,0:T(8,128)(2,1)S(1)}, bf16[272,384]{1,0:T(8,128)(2,1)S(1)}, u32[]{:S(2)}, u32[]{:S(2)}) collective-permute-start(bf16[272,384]{1,0:T(8,128)(2,1)S(1)} %copy-done.4), channel_id=1, source_target_pairs={{0,2},{1,3},{2,0},{3,1},{4,6},{5,7},{6,4},{7,5},{8,10},{9,11},{10,... | collective-permute-start | bytes 626696 | tf_op jit(solution)/shard_map/ppermute | solution.py:431
  52.0 19.0 %collective-permute-start.8 = (bf16[272,384]{1,0:T(8,128)(2,1)S(1)}, bf16[272,384]{1,0:T(8,128)(2,1)S(1)}, u32[]{:S(2)}, u32[]{:S(2)}) collective-permute-start(bf16[272,384]{1,0:T(8,128)(2,1)S(1)} %copy-done.3), channel_id=1, source_target_pairs={{0,3},{1,0},{2,1},{3,2},{4,7},{5,4},{6,5},{7,6},{8,11},{9,8},{10,9... | collective-permute-start | bytes 626696 | tf_op jit(solution)/shard_map/ppermute | solution.py:431
  63.2 35.3 %all-to-all-start.2 = ((bf16[4,192,1152]{2,1,0:T(8,128)(2,1)}), bf16[4,192,1152]{2,1,0:T(8,128)(2,1)S(1)}, u32[]{:S(2)}, u32[]{:S(2)}) async-start(bf16[4,192,1152]{2,1,0:T(8,128)(2,1)} %weight_share.1.refs_12_), calls=%async_computation.2 | async-start | bytes 3538944 | tf_op jit(solution)/shard_map/all_to_all | solution.py:495
  76.7 21.2 %copy-start = (bf16[64,1664]{1,0:T(8,128)(2,1)S(1)}, bf16[64,1664]{1,0:T(8,128)(2,1)}, u32[]{:S(2)}) copy-start(bf16[64,1664]{1,0:T(8,128)(2,1)} %get-tuple-element.71.refs_0_) | copy-start | bytes 638980
  76.7 3.0 %collective-permute-start.13 = (bf16[4,240,384]{2,1,0:T(8,128)(2,1)}, bf16[4,240,384]{2,1,0:T(8,128)(2,1)S(1)}, u32[]{:S(2)}, u32[]{:S(2)}) collective-permute-start(bf16[4,240,384]{2,1,0:T(8,128)(2,1)} %get-tuple-element.77), channel_id=1, source_target_pairs={{0,4},{4,0},{8,12},{12,8},{16,20},{20,16},{24,28},{28,24},{1,5},{5... | collective-permute-start | bytes 2211848 | tf_op jit(solution)/shard_map/ppermute | solution.py:433
  77.3 7.0 %collective-permute-start.10 = (bf16[64,1664]{1,0:T(8,128)(2,1)}, bf16[64,1664]{1,0:T(8,128)(2,1)S(1)}, u32[]{:S(2)}, u32[]{:S(2)}) collective-permute-start(bf16[64,1664]{1,0:T(8,128)(2,1)} %get-tuple-element.72), channel_id=1, source_target_pairs={{0,1},{1,2},{2,3},{3,0},{4,5},{5,6},{6,7},{7,4},{8,9},{9,10},{10,1... | collective-permute-start | bytes 638984 | tf_op jit(solution)/shard_map/ppermute | solution.py:431
  77.3 18.8 %collective-permute-start.11 = (bf16[64,1664]{1,0:T(8,128)(2,1)}, bf16[64,1664]{1,0:T(8,128)(2,1)S(1)}, u32[]{:S(2)}, u32[]{:S(2)}) collective-permute-start(bf16[64,1664]{1,0:T(8,128)(2,1)} %get-tuple-element.73), channel_id=1, source_target_pairs={{0,2},{1,3},{2,0},{3,1},{4,6},{5,7},{6,4},{7,5},{8,10},{9,11},{10,... | collective-permute-start | bytes 638984 | tf_op jit(solution)/shard_map/ppermute | solution.py:431
  78.2 19.7 %collective-permute-start.12 = (bf16[64,1664]{1,0:T(8,128)(2,1)}, bf16[64,1664]{1,0:T(8,128)(2,1)S(1)}, u32[]{:S(2)}, u32[]{:S(2)}) collective-permute-start(bf16[64,1664]{1,0:T(8,128)(2,1)} %get-tuple-element.74), channel_id=1, source_target_pairs={{0,3},{1,0},{2,1},{3,2},{4,7},{5,4},{6,5},{7,6},{8,11},{9,8},{10,9... | collective-permute-start | bytes 638984 | tf_op jit(solution)/shard_map/ppermute | solution.py:431
  81.3 17.0 %collective-permute-start.14 = (bf16[240,384]{1,0:T(8,128)(2,1)S(1)}, bf16[240,384]{1,0:T(8,128)(2,1)S(1)}, u32[]{:S(2)}, u32[]{:S(2)}) collective-permute-start(bf16[240,384]{1,0:T(8,128)(2,1)S(1)} %get-tuple-element.79), channel_id=1, source_target_pairs={{0,8},{4,12},{8,0},{12,4},{16,24},{20,28},{24,16},{28,20},{1,9},{5... | collective-permute-start | bytes 552968 | tf_op jit(solution)/shard_map/ppermute | solution.py:433
  83.0 15.3 %collective-permute-start.15 = (bf16[240,384]{1,0:T(8,128)(2,1)S(1)}, bf16[240,384]{1,0:T(8,128)(2,1)S(1)}, u32[]{:S(2)}, u32[]{:S(2)}) collective-permute-start(bf16[240,384]{1,0:T(8,128)(2,1)S(1)} %get-tuple-element.80), channel_id=1, source_target_pairs={{0,16},{4,20},{8,24},{12,28},{16,0},{20,4},{24,8},{28,12},{1,17},{... | collective-permute-start | bytes 552968 | tf_op jit(solution)/shard_map/ppermute | solution.py:433
  84.3 14.0 %collective-permute-start.16 = (bf16[240,384]{1,0:T(8,128)(2,1)S(1)}, bf16[240,384]{1,0:T(8,128)(2,1)S(1)}, u32[]{:S(2)}, u32[]{:S(2)}) collective-permute-start(bf16[240,384]{1,0:T(8,128)(2,1)S(1)} %get-tuple-element.81), channel_id=1, source_target_pairs={{0,24},{4,28},{8,16},{12,20},{16,8},{20,12},{24,0},{28,4},{1,25},{... | collective-permute-start | bytes 552968 | tf_op jit(solution)/shard_map/ppermute | solution.py:433
  98.5 3.9 %collective-permute-start.20 = (bf16[4,192,1152]{2,1,0:T(8,128)(2,1)S(1)}, bf16[4,192,1152]{2,1,0:T(8,128)(2,1)S(1)}, u32[]{:S(2)}, u32[]{:S(2)}) collective-permute-start(bf16[4,192,1152]{2,1,0:T(8,128)(2,1)S(1)} %gate.3.mine), channel_id=1, source_target_pairs={{0,4},{4,0},{8,12},{12,8},{16,20},{20,16},{24,28},{28,24},{1,5},{5... | collective-permute-start | bytes 5308424 | tf_op jit(solution)/shard_map/ppermute | solution.py:433
  99.1 6.8 %collective-permute-start.17 = (bf16[256,384]{1,0:T(8,128)(2,1)S(1)}, bf16[256,384]{1,0:T(8,128)(2,1)S(1)}, u32[]{:S(2)}, u32[]{:S(2)}) collective-permute-start(bf16[256,384]{1,0:T(8,128)(2,1)S(1)} %chip_sum.1.__1_.refs_0_), channel_id=1, source_target_pairs={{0,8},{4,12},{8,0},{12,4},{16,24},{20,28},{24,16},{28,20},{1,9},{5... | collective-permute-start | bytes 589832 | tf_op jit(solution)/shard_map/ppermute | solution.py:433
  100.7 9.2 %collective-permute-start.18 = (bf16[256,384]{1,0:T(8,128)(2,1)S(1)}, bf16[256,384]{1,0:T(8,128)(2,1)S(1)}, u32[]{:S(2)}, u32[]{:S(2)}) collective-permute-start(bf16[256,384]{1,0:T(8,128)(2,1)S(1)} %chip_sum.1.__1_.refs_0_), channel_id=1, source_target_pairs={{0,16},{4,20},{8,24},{12,28},{16,0},{20,4},{24,8},{28,12},{1,17},{... | collective-permute-start | bytes 589832 | tf_op jit(solution)/shard_map/ppermute | solution.py:433
  101.9 9.3 %collective-permute-start.19 = (bf16[256,384]{1,0:T(8,128)(2,1)S(1)}, bf16[256,384]{1,0:T(8,128)(2,1)S(1)}, u32[]{:S(2)}, u32[]{:S(2)}) collective-permute-start(bf16[256,384]{1,0:T(8,128)(2,1)S(1)} %chip_sum.1.__1_.refs_0_), channel_id=1, source_target_pairs={{0,24},{4,28},{8,16},{12,20},{16,8},{20,12},{24,0},{28,4},{1,25},{... | collective-permute-start | bytes 589832 | tf_op jit(solution)/shard_map/ppermute | solution.py:433
  111.3 3.0 %collective-permute-start.21 = (bf16[976,384]{1,0:T(8,128)(2,1)S(1)}, bf16[976,384]{1,0:T(8,128)(2,1)S(1)}, u32[]{:S(2)}, u32[]{:S(2)}) collective-permute-start(bf16[976,384]{1,0:T(8,128)(2,1)S(1)} %kernel_grad_half.1.refs_0_), channel_id=1, source_target_pairs={{0,4},{4,0},{8,12},{12,8},{16,20},{20,16},{24,28},{28,24},{1,5},{5... | collective-permute-start | bytes 2248712 | tf_op jit(solution)/shard_map/ppermute | solution.py:433

commit v6 on v5

--- a/solution.py
+++ b/solution.py
@@ -155,8 +155,8 @@
 
 
 def joined(tail):
-    rows = tail.shape[0] // 2
-    return tail[:rows].astype(F32) + tail[rows:].astype(F32)
+    rows, tail = tail.shape[0] // 2, tail.astype(F32)
+    return tail[:rows] + tail[rows:]
 
 
 def picker(shape, me, c):
@@ -167,7 +167,13 @@
 
 def mid_kernel(n, c, chans, ins, outs, go):
     me = lax.axis_index("seq")
-    cot, w = ins[:2]
+    gain_in, gain_mid, cot, w = ins[:4]
+    gin, gmid = outs[n:]
+    gin[...] = gain_in()[...].reshape(1, chans)
+    gains = gain_mid()[...].reshape(1, 2 * chans)
+    for b in range(n):
+        pair = [gains[:, h * chans + b * c : h * chans + (b + 1) * c] for h in range(2)]
+        gmid[b : b + 1, :] = jnp.concatenate(pair, axis=1)
     g, w = cot()[...], w()
     for k in range(n):
         at = pl.multiple_of(lax.rem(me + k, n) * c, c & -c)
@@ -438,21 +444,19 @@
     taps_rows = conv_kernel.transpose(0, 2, 1).reshape(5 * c, chans)
     own = x.reshape(length // 2, width)
     xs = from_all(own)
-    gin = gain_in.reshape(1, chans)
-    gmid = gain_mid.reshape(2, n, c).transpose(1, 0, 2).reshape(n, 2 * c)
     cots = jnp.broadcast_to(cot[None], (chips, *cot.shape))
     cots = lax.all_to_all(cots, "dp", 0, 0, axis_index_groups=same_core, tiled=True)
-    used = [cot, qkv_weight, taps_rows, gin, gmid]
+    used = [cot, qkv_weight, taps_rows]
     held = call(
         functools.partial(mid_kernel, n, c, chans),
-        [],
-        kept=[shaped((half, 2 * c), BF16)] * n,
+        [gain_in, gain_mid],
+        kept=[shaped((half, 2 * c), BF16)] * n + [shaped((1, chans), F32), shaped((n, 2 * c), F32)],
         fetch=used,
         flops=WAIT,
         name="mid_parts",
     )
     mid_msgs = held[:n]
-    cot, weight, taps, gin, gmid = held[n:]
+    gin, gmid, cot, weight, taps = held[n:]
     pooled_msg, *states = call(
         functools.partial(conv_kernel_fwd, n, c, chans),
         [*xs, taps, gin],

time: 116 us -> 116 us (level)
  local copies, waits for them, and re-layouts: 5.75 us -> 4.4 us
  waiting for transfers between devices: 49.5 us -> 50.8 us
    ppermute x12, waiting for transfers between devices: 35.5 us -> 36.8 us  [body(): lax.ppermute(v, 'seq', [(i, (i + k) % n) for i in range(n)])]
    reshape x3 -> x0, local copies, waits for them, and re-layouts: 1.34 us -> none  [the longest x2 0.76 us: body(): gmid = gain_mid.reshape(2, n, c).transpose(1, 0, 2).reshape(n, 2 * c)]
  transfers between devices with their start and end apart: 25 -> 25, of which waited for: 16 -> 16; matrix products, arithmetic and copies ran while one was open for 4% -> 3% of each run, Pallas kernels for 19% -> 20%
where the time goes in v6:
time: 116 us
  waiting for transfers between devices  50.8 us (44%)
  starting transfers between devices  35.5 us (31%)
  Pallas kernels  24 us (21%)
  local copies, waits for them, and re-layouts  4.4 us (4%)
    ppermute x12, waiting for transfers between devices, body(): lax.ppermute(v, 'seq', [(i, (i + k) % n) for i in range(n)])  36.8 us
    pallas_call x10, Pallas kernels, call(): pl.pallas_call(whole, out_shape=tuple([*memory(pltpu.HBM, outs), *free, *...  22.2 us
    ppermute x12, starting transfers between devices, body(): lax.ppermute(v, 'seq', [(i, (i + k) % n) for i in range(n)])  11.7 us
    ppermute x10, starting transfers between devices, body(): across = lambda v, k: lax.ppermute(v, 'dp', [(i, i ^ k) for i in range(m)])  10.9 us
    ppermute x10, waiting for transfers between devices, body(): across = lambda v, k: lax.ppermute(v, 'dp', [(i, i ^ k) for i in range(m)])  8.52 us
    all_to_all x1, waiting for transfers between devices, body(): lax.all_to_all(nmt.reshape(m, width // m, half), 'dp', 0, 0, tiled=True)  5.49 us
    all_to_all x1, starting transfers between devices, body(): lax.all_to_all(cots, 'dp', 0, 0, axis_index_groups=same_core, tiled=True)  4.65 us
    all_to_all x1, starting transfers between devices, body(): lax.all_to_all(wshare, 'dp', 0, 0, axis_index_groups=same_core, tiled=True)  4.55 us
  transfers between devices with their start and end apart: 25, of which 16 were waited for; matrix products, arithmetic and copies ran while one was open for 3% of the time, Pallas kernels for 20%

profile of v6, /device:TPU:9, one launch (start us, length us, event | category | flops | bytes accessed | tf_op | source)
XLA Modules:
  0.0 115.7 jit_solution(10162124527924944440)
XLA Ops:
  1.6 1.3 %collective-permute-start = (bf16[64,1536]{1,0:T(8,128)(2,1)S(1)}, bf16[64,1536]{1,0:T(8,128)(2,1)S(1)}, u32[]{:S(2)}, u32[]{:S(2)}) collective-permute-start(bf16[64,1536]{1,0:T(8,128)(2,1)S(1)} %reshape_squeeze.3.refs_0_.refs_4_), channel_id=1, source_target_pairs={{0,1},{1,2},{2,3},{3,0},{4,5},{5,6},{6,7},{7,4},{8,9},{9,10},{10,1... | collective-permute-start | bytes 589832 | tf_op jit(solution)/shard_map/ppermute | solution.py:437
  4.1 1.4 %collective-permute-start.2 = (bf16[64,1536]{1,0:T(8,128)(2,1)S(1)}, bf16[64,1536]{1,0:T(8,128)(2,1)S(1)}, u32[]{:S(2)}, u32[]{:S(2)}) collective-permute-start(bf16[64,1536]{1,0:T(8,128)(2,1)S(1)} %reshape_squeeze.3.refs_0_.refs_4_), channel_id=1, source_target_pairs={{0,3},{1,0},{2,1},{3,2},{4,7},{5,4},{6,5},{7,6},{8,11},{9,8},{10,9... | collective-permute-start | bytes 589832 | tf_op jit(solution)/shard_map/ppermute | solution.py:437
  5.5 2.6 %broadcast_in_dim.9 = bf16[4,256,1152]{2,1,0:T(8,128)(2,1)} broadcast(bf16[256,1152]{1,0:T(8,128)(2,1)} %bitcast.11), dimensions={1,2} | broadcast | bytes 2949120 | tf_op jit(solution)/shard_map/broadcast_in_dim | solution.py:447
  8.1 4.6 %all-to-all-start.1 = ((bf16[4,256,1152]{2,1,0:T(8,128)(2,1)}), bf16[4,256,1152]{2,1,0:T(8,128)(2,1)}, u32[]{:S(2)}, u32[]{:S(2)}) async-start(bf16[4,256,1152]{2,1,0:T(8,128)(2,1)} %broadcast_in_dim.9), calls=%async_computation.1 | async-start | bytes 4718592 | tf_op jit(solution)/shard_map/all_to_all | solution.py:448
  12.8 3.8 %mid_parts.1 = (bf16[256,384]{1,0:T(8,128)(2,1)S(1)}, bf16[256,384]{1,0:T(8,128)(2,1)S(1)}, bf16[256,384]{1,0:T(8,128)(2,1)S(1)}, bf16[256,384]{1,0:T(8,128)(2,1...) custom-call(f32[768]{0:T(1024)S(1)} %copy-done.2, ...), custom_call_target="tpu_custom_call" | custom-call | flops 40000000000 | tf_op jit(solution)/shard_map/mid_parts/pallas_call | solution.py:90
  16.6 2.6 %collective-permute-done.1.refs_2_ = bf16[64,1536]{1,0:T(8,128)(2,1)S(1)} collective-permute-done((bf16[64,1536]{1,0:T(8,128)(2,1)S(1)}, bf16[64,1536]{1,0:T(8,128)(2,1)S(1)}, u32[]{:S(2)}, u32[]{:S(2)}) %collective-permute-start.1) | collective-permute-done | bytes 196640 | tf_op jit(solution)/shard_map/ppermute | solution.py:437
  19.2 2.9 %collective-permute-done.2.refs_3_ = bf16[64,1536]{1,0:T(8,128)(2,1)S(1)} collective-permute-done((bf16[64,1536]{1,0:T(8,128)(2,1)S(1)}, bf16[64,1536]{1,0:T(8,128)(2,1)S(1)}, u32[]{:S(2)}, u32[]{:S(2)}) %collective-permute-start.2) | collective-permute-done | bytes 196640 | tf_op jit(solution)/shard_map/ppermute | solution.py:437
  22.1 1.9 %conv_forward.1 = (bf16[256,384]{1,0:T(8,128)(2,1)S(1)}, f32[256,384]{1,0:T(8,128)S(1)}, f32[256,384]{1,0:T(8,128)S(1)}, bf16[256,1536]{1,0:T(8,128)(2,1)S(1)}, f32[256,2]{1,0:T(8,128)S(1)}) custom-call(bf16[64,1536]{1,0:T(8,128)(2,1)S(1)} %reshape_squeeze.3.refs_0_.refs_4_, bf16[64,1536]{1,0:T(8,128)(2,1)S(1)} %collective-permute-done.refs_1_, ...), custom_call_target="tpu_custom_call" | custom-call | tf_op jit(solution)/shard_map/conv_forward/pallas_call | solution.py:90
  24.4 1.4 %collective-permute-start.5 = (bf16[256,384]{1,0:T(8,128)(2,1)S(1)}, bf16[256,384]{1,0:T(8,128)(2,1)S(1)}, u32[]{:S(2)}, u32[]{:S(2)}) collective-permute-start(bf16[256,384]{1,0:T(8,128)(2,1)S(1)} %get-tuple-element.48.refs_0_), channel_id=1, source_target_pairs={{0,3},{1,0},{2,1},{3,2},{4,7},{5,4},{6,5},{7,6},{8,11},{9,8},{10,9... | collective-permute-start | bytes 589832 | tf_op jit(solution)/shard_map/ppermute | solution.py:437
  25.8 4.5 %collective-permute-done.3.refs_1_ = bf16[256,384]{1,0:T(8,128)(2,1)S(1)} collective-permute-done((bf16[256,384]{1,0:T(8,128)(2,1)S(1)}, bf16[256,384]{1,0:T(8,128)(2,1)S(1)}, u32[]{:S(2)}, u32[]{:S(2)}) %collective-permute-start.3) | collective-permute-done | bytes 196640 | tf_op jit(solution)/shard_map/ppermute | solution.py:437
  30.3 10.7 %collective-permute-done.4.refs_2_ = bf16[256,384]{1,0:T(8,128)(2,1)S(1)} collective-permute-done((bf16[256,384]{1,0:T(8,128)(2,1)S(1)}, bf16[256,384]{1,0:T(8,128)(2,1)S(1)}, u32[]{:S(2)}, u32[]{:S(2)}) %collective-permute-start.4) | collective-permute-done | bytes 196640 | tf_op jit(solution)/shard_map/ppermute | solution.py:437
  41.0 1.4 %collective-permute-done.5.refs_3_ = bf16[256,384]{1,0:T(8,128)(2,1)S(1)} collective-permute-done((bf16[256,384]{1,0:T(8,128)(2,1)S(1)}, bf16[256,384]{1,0:T(8,128)(2,1)S(1)}, u32[]{:S(2)}, u32[]{:S(2)}) %collective-permute-start.5) | collective-permute-done | bytes 196640 | tf_op jit(solution)/shard_map/ppermute | solution.py:437
  42.4 3.1 %qkv.1 = (bf16[1536,256]{1,0:T(8,128)(2,1)}, f32[256,1]{1,0:T(8,128)}, bf16[256,1152]{1,0:T(8,128)(2,1)}, f32[8,256]{1,0:T(8,128)}, bf16[272,384]{1,0:T(8,128)(2...) custom-call(bf16[256,384]{1,0:T(8,128)(2,1)S(1)} %get-tuple-element., ...), custom_call_target="tpu_custom_call" | custom-call | tf_op jit(solution)/shard_map/qkv/pallas_call | solution.py:90
  46.1 3.8 %all-to-all-start = ((bf16[8,192,256]{2,1,0:T(8,128)(2,1)}), bf16[8,192,256]{2,1,0:T(8,128)(2,1)S(1)}, u32[]{:S(2)}, u32[]{:S(2)}) async-start(bf16[8,192,256]{2,1,0:T(8,128)(2,1)} %bitcast.5), calls=%async_computation | async-start | bytes 1572864 | tf_op jit(solution)/shard_map/all_to_all | solution.py:492
  49.9 2.2 %collective-permute-start.7 = (bf16[272,384]{1,0:T(8,128)(2,1)S(1)}, bf16[272,384]{1,0:T(8,128)(2,1)S(1)}, u32[]{:S(2)}, u32[]{:S(2)}) collective-permute-start(bf16[272,384]{1,0:T(8,128)(2,1)S(1)} %copy-done.4), channel_id=1, source_target_pairs={{0,2},{1,3},{2,0},{3,1},{4,6},{5,7},{6,4},{7,5},{8,10},{9,11},{10,... | collective-permute-start | bytes 626696 | tf_op jit(solution)/shard_map/ppermute | solution.py:437
  52.1 1.4 %collective-permute-start.8 = (bf16[272,384]{1,0:T(8,128)(2,1)S(1)}, bf16[272,384]{1,0:T(8,128)(2,1)S(1)}, u32[]{:S(2)}, u32[]{:S(2)}) collective-permute-start(bf16[272,384]{1,0:T(8,128)(2,1)S(1)} %copy-done.3), channel_id=1, source_target_pairs={{0,3},{1,0},{2,1},{3,2},{4,7},{5,4},{6,5},{7,6},{8,11},{9,8},{10,9... | collective-permute-start | bytes 626696 | tf_op jit(solution)/shard_map/ppermute | solution.py:437
  53.5 5.5 %all-to-all-done.refs_0_ = bf16[8,192,256]{2,1,0:T(8,128)(2,1)S(1)} async-done(((bf16[8,192,256]{2,1,0:T(8,128)(2,1)}), bf16[8,192,256]{2,1,0:T(8,128)(2,1)S(1)}, u32[]{:S(2)}, u32[]{:S(2)}) %all-to-all-start) | async-done | bytes 786464 | tf_op jit(solution)/shard_map/all_to_all | solution.py:492
  59.0 4.3 %weight_share.1.refs_12_ = bf16[4,192,1152]{2,1,0:T(8,128)(2,1)} custom-call(bf16[8,192,256]{2,1,0:T(8,128)(2,1)S(1)} %all-to-all-done.refs_0_, bf16[4,256,1152]{2,1,0:T(8,128)(2,1)} %gate.2.refs_1_, bf16[4,256,1152]{2,1,0:T(8,128)(2,1)} %collective-permute-done.9.refs_2_), custom_call_target="tpu_custom_call" | custom-call | tf_op jit(solution)/shard_map/weight_share/pallas_call | solution.py:90
  63.3 4.5 %all-to-all-start.2 = ((bf16[4,192,1152]{2,1,0:T(8,128)(2,1)}), bf16[4,192,1152]{2,1,0:T(8,128)(2,1)S(1)}, u32[]{:S(2)}, u32[]{:S(2)}) async-start(bf16[4,192,1152]{2,1,0:T(8,128)(2,1)} %weight_share.1.refs_12_), calls=%async_computation.2 | async-start | bytes 3538944 | tf_op jit(solution)/shard_map/all_to_all | solution.py:499
  68.0 3.1 %collective-permute-done.8.refs_3_ = bf16[272,384]{1,0:T(8,128)(2,1)S(1)} collective-permute-done((bf16[272,384]{1,0:T(8,128)(2,1)S(1)}, bf16[272,384]{1,0:T(8,128)(2,1)S(1)}, u32[]{:S(2)}, u32[]{:S(2)}) %collective-permute-start.8) | collective-permute-done | bytes 208928 | tf_op jit(solution)/shard_map/ppermute | solution.py:437
  71.1 5.7 %conv_backward.1 = (bf16[4,240,384]{2,1,0:T(8,128)(2,1)}, f32[4,240,384]{2,1,0:T(8,128)}, bf16[64,1664]{1,0:T(8,128)(2,1)}, bf16[64,1664]{1,0:T(8,128)(2,1)}, bf...) custom-call(bf16[272,384]{1,0:T(8,128)(2,1)} %get-tuple-element.61.refs_0_, ...), custom_call_target="tpu_custom_call" | custom-call | flops 40000000000 | tf_op jit(solution)/shard_map/conv_backward/pallas_call | solution.py:90
  78.3 1.5 %collective-permute-start.12 = (bf16[64,1664]{1,0:T(8,128)(2,1)}, bf16[64,1664]{1,0:T(8,128)(2,1)S(1)}, u32[]{:S(2)}, u32[]{:S(2)}) collective-permute-start(bf16[64,1664]{1,0:T(8,128)(2,1)} %get-tuple-element.74), channel_id=1, source_target_pairs={{0,3},{1,0},{2,1},{3,2},{4,7},{5,4},{6,5},{7,6},{8,11},{9,8},{10,9... | collective-permute-start | bytes 638984 | tf_op jit(solution)/shard_map/ppermute | solution.py:437
  79.8 1.6 %core_sum.1 = (bf16[240,384]{1,0:T(8,128)(2,1)S(1)}, bf16[240,384]{1,0:T(8,128)(2,1)S(1)}, bf16[240,384]{1,0:T(8,128)(2,1)S(1)}, f32[240,384]{1,0:T(8,128)S(1)}) custom-call(f32[4,240,384]{2,1,0:T(8,128)} %get-tuple-element.76.refs_0_, bf16[4,240,384]{2,1,0:T(8,128)(2,1)S(1)} %collective-permute-done.13.refs_1_), custom_call_target="tpu_custom_call" | custom-call | tf_op jit(solution)/shard_map/core_sum/pallas_call | solution.py:90
  81.3 1.7 %collective-permute-start.14 = (bf16[240,384]{1,0:T(8,128)(2,1)S(1)}, bf16[240,384]{1,0:T(8,128)(2,1)S(1)}, u32[]{:S(2)}, u32[]{:S(2)}) collective-permute-start(bf16[240,384]{1,0:T(8,128)(2,1)S(1)} %get-tuple-element.79), channel_id=1, source_target_pairs={{0,8},{4,12},{8,0},{12,4},{16,24},{20,28},{24,16},{28,20},{1,9},{5... | collective-permute-start | bytes 552968 | tf_op jit(solution)/shard_map/ppermute | solution.py:439
  84.4 2.3 %collective-permute-start.16 = (bf16[240,384]{1,0:T(8,128)(2,1)S(1)}, bf16[240,384]{1,0:T(8,128)(2,1)S(1)}, u32[]{:S(2)}, u32[]{:S(2)}) collective-permute-start(bf16[240,384]{1,0:T(8,128)(2,1)S(1)} %get-tuple-element.81), channel_id=1, source_target_pairs={{0,24},{4,28},{8,16},{12,20},{16,8},{20,12},{24,0},{28,4},{1,25},{... | collective-permute-start | bytes 552968 | tf_op jit(solution)/shard_map/ppermute | solution.py:439
  86.7 9.5 %collective-permute-done.11.refs_2_ = bf16[64,1664]{1,0:T(8,128)(2,1)S(1)} collective-permute-done((bf16[64,1664]{1,0:T(8,128)(2,1)}, bf16[64,1664]{1,0:T(8,128)(2,1)S(1)}, u32[]{:S(2)}, u32[]{:S(2)}) %collective-permute-start.11) | collective-permute-done | bytes 213024 | tf_op jit(solution)/shard_map/ppermute | solution.py:437
  96.2 1.8 %collective-permute-done.12.refs_3_ = bf16[64,1664]{1,0:T(8,128)(2,1)S(1)} collective-permute-done((bf16[64,1664]{1,0:T(8,128)(2,1)}, bf16[64,1664]{1,0:T(8,128)(2,1)S(1)}, u32[]{:S(2)}, u32[]{:S(2)}) %collective-permute-start.12) | collective-permute-done | bytes 213024 | tf_op jit(solution)/shard_map/ppermute | solution.py:437
  99.2 1.6 %collective-permute-start.17 = (bf16[256,384]{1,0:T(8,128)(2,1)S(1)}, bf16[256,384]{1,0:T(8,128)(2,1)S(1)}, u32[]{:S(2)}, u32[]{:S(2)}) collective-permute-start(bf16[256,384]{1,0:T(8,128)(2,1)S(1)} %chip_sum.1.__1_.refs_0_), channel_id=1, source_target_pairs={{0,8},{4,12},{8,0},{12,4},{16,24},{20,28},{24,16},{28,20},{1,9},{5... | collective-permute-start | bytes 589832 | tf_op jit(solution)/shard_map/ppermute | solution.py:439
  102.5 1.8 %weight_grad.1.refs_4_ = bf16[4,2,192,1152]{3,2,1,0:T(8,128)(2,1)} custom-call(bf16[4,192,1152]{2,1,0:T(8,128)(2,1)S(1)} %gate.3.mine, bf16[4,192,1152]{2,1,0:T(8,128)(2,1)S(1)} %collective-permute-done.20.other), custom_call_target="tpu_custom_call" | custom-call | tf_op jit(solution)/shard_map/weight_grad/pallas_call | solution.py:551
  104.3 1.6 %collective-permute-done.17.refs_1_ = bf16[256,384]{1,0:T(8,128)(2,1)S(1)} collective-permute-done((bf16[256,384]{1,0:T(8,128)(2,1)S(1)}, bf16[256,384]{1,0:T(8,128)(2,1)S(1)}, u32[]{:S(2)}, u32[]{:S(2)}) %collective-permute-start.17) | collective-permute-done | bytes 196640 | tf_op jit(solution)/shard_map/ppermute | solution.py:439
  106.0 4.0 %collective-permute-done.18.refs_2_ = bf16[256,384]{1,0:T(8,128)(2,1)S(1)} collective-permute-done((bf16[256,384]{1,0:T(8,128)(2,1)S(1)}, bf16[256,384]{1,0:T(8,128)(2,1)S(1)}, u32[]{:S(2)}, u32[]{:S(2)}) %collective-permute-start.18) | collective-permute-done | bytes 196640 | tf_op jit(solution)/shard_map/ppermute | solution.py:439
  114.4 1.3 %kernel_grad.1 = (bf16[960,768]{1,0:T(8,128)(2,1)}, f32[768]{0:T(1024)}, f32[1536]{0:T(1024)}) custom-call(bf16[976,384]{1,0:T(8,128)(2,1)S(1)} %kernel_grad_half.1.refs_0_, bf16[976,384]{1,0:T(8,128)(2,1)S(1)} %collective-permute-done.21.refs_1_), custom_call_target="tpu_custom_call" | custom-call | tf_op jit(solution)/shard_map/kernel_grad/pallas_call | solution.py:90
  (46 shorter events, 13.2 us)
Async XLA Ops:
  1.6 14.9 %collective-permute-start = (bf16[64,1536]{1,0:T(8,128)(2,1)S(1)}, bf16[64,1536]{1,0:T(8,128)(2,1)S(1)}, u32[]{:S(2)}, u32[]{:S(2)}) collective-permute-start(bf16[64,1536]{1,0:T(8,128)(2,1)S(1)} %reshape_squeeze.3.refs_0_.refs_4_), channel_id=1, source_target_pairs={{0,1},{1,2},{2,3},{3,0},{4,5},{5,6},{6,7},{7,4},{8,9},{9,10},{10,1... | collective-permute-start | bytes 589832 | tf_op jit(solution)/shard_map/ppermute | solution.py:437
  3.0 16.2 %collective-permute-start.1 = (bf16[64,1536]{1,0:T(8,128)(2,1)S(1)}, bf16[64,1536]{1,0:T(8,128)(2,1)S(1)}, u32[]{:S(2)}, u32[]{:S(2)}) collective-permute-start(bf16[64,1536]{1,0:T(8,128)(2,1)S(1)} %reshape_squeeze.3.refs_0_.refs_4_), channel_id=1, source_target_pairs={{0,2},{1,3},{2,0},{3,1},{4,6},{5,7},{6,4},{7,5},{8,10},{9,11},{10,... | collective-permute-start | bytes 589832 | tf_op jit(solution)/shard_map/ppermute | solution.py:437
  4.1 18.1 %collective-permute-start.2 = (bf16[64,1536]{1,0:T(8,128)(2,1)S(1)}, bf16[64,1536]{1,0:T(8,128)(2,1)S(1)}, u32[]{:S(2)}, u32[]{:S(2)}) collective-permute-start(bf16[64,1536]{1,0:T(8,128)(2,1)S(1)} %reshape_squeeze.3.refs_0_.refs_4_), channel_id=1, source_target_pairs={{0,3},{1,0},{2,1},{3,2},{4,7},{5,4},{6,5},{7,6},{8,11},{9,8},{10,9... | collective-permute-start | bytes 589832 | tf_op jit(solution)/shard_map/ppermute | solution.py:437
  8.1 4.7 %copy-start.1 = (f32[1536]{0:T(1024)S(1)}, f32[1536]{0:T(1024)}, u32[]{:S(2)}) copy-start(f32[1536]{0:T(1024)} %refs_1_.1) | copy-start | bytes 18436
  8.1 4.7 %copy-start.2 = (f32[768]{0:T(1024)S(1)}, f32[768]{0:T(1024)}, u32[]{:S(2)}) copy-start(f32[768]{0:T(1024)} %refs_0_.1) | copy-start | bytes 9220
  8.1 37.4 %all-to-all-start.1 = ((bf16[4,256,1152]{2,1,0:T(8,128)(2,1)}), bf16[4,256,1152]{2,1,0:T(8,128)(2,1)}, u32[]{:S(2)}, u32[]{:S(2)}) async-start(bf16[4,256,1152]{2,1,0:T(8,128)(2,1)} %broadcast_in_dim.9), calls=%async_computation.1 | async-start | bytes 4718592 | tf_op jit(solution)/shard_map/all_to_all | solution.py:448
  24.0 6.3 %collective-permute-start.3 = (bf16[256,384]{1,0:T(8,128)(2,1)S(1)}, bf16[256,384]{1,0:T(8,128)(2,1)S(1)}, u32[]{:S(2)}, u32[]{:S(2)}) collective-permute-start(bf16[256,384]{1,0:T(8,128)(2,1)S(1)} %get-tuple-element.48.refs_0_), channel_id=1, source_target_pairs={{0,1},{1,2},{2,3},{3,0},{4,5},{5,6},{6,7},{7,4},{8,9},{9,10},{10,1... | collective-permute-start | bytes 589832 | tf_op jit(solution)/shard_map/ppermute | solution.py:437
  24.1 16.9 %collective-permute-start.4 = (bf16[256,384]{1,0:T(8,128)(2,1)S(1)}, bf16[256,384]{1,0:T(8,128)(2,1)S(1)}, u32[]{:S(2)}, u32[]{:S(2)}) collective-permute-start(bf16[256,384]{1,0:T(8,128)(2,1)S(1)} %get-tuple-element.48.refs_0_), channel_id=1, source_target_pairs={{0,2},{1,3},{2,0},{3,1},{4,6},{5,7},{6,4},{7,5},{8,10},{9,11},{10,... | collective-permute-start | bytes 589832 | tf_op jit(solution)/shard_map/ppermute | solution.py:437
  24.4 17.9 %collective-permute-start.5 = (bf16[256,384]{1,0:T(8,128)(2,1)S(1)}, bf16[256,384]{1,0:T(8,128)(2,1)S(1)}, u32[]{:S(2)}, u32[]{:S(2)}) collective-permute-start(bf16[256,384]{1,0:T(8,128)(2,1)S(1)} %get-tuple-element.48.refs_0_), channel_id=1, source_target_pairs={{0,3},{1,0},{2,1},{3,2},{4,7},{5,4},{6,5},{7,6},{8,11},{9,8},{10,9... | collective-permute-start | bytes 589832 | tf_op jit(solution)/shard_map/ppermute | solution.py:437
  45.5 4.4 %copy-start.5 = (bf16[272,384]{1,0:T(8,128)(2,1)S(1)}, bf16[272,384]{1,0:T(8,128)(2,1)}, u32[]{:S(2)}) copy-start(bf16[272,384]{1,0:T(8,128)(2,1)} %get-tuple-element.62) | copy-start | bytes 626692
  45.5 4.4 %copy-start.4 = (bf16[272,384]{1,0:T(8,128)(2,1)S(1)}, bf16[272,384]{1,0:T(8,128)(2,1)}, u32[]{:S(2)}) copy-start(bf16[272,384]{1,0:T(8,128)(2,1)} %get-tuple-element.63) | copy-start | bytes 626692
  45.5 6.6 %copy-start.3 = (bf16[272,384]{1,0:T(8,128)(2,1)S(1)}, bf16[272,384]{1,0:T(8,128)(2,1)}, u32[]{:S(2)}) copy-start(bf16[272,384]{1,0:T(8,128)(2,1)} %get-tuple-element.64) | copy-start | bytes 626692
  45.5 13.5 %collective-permute-start.9 = (bf16[4,256,1152]{2,1,0:T(8,128)(2,1)}, bf16[4,256,1152]{2,1,0:T(8,128)(2,1)}, u32[]{:S(2)}, u32[]{:S(2)}) collective-permute-start(bf16[4,256,1152]{2,1,0:T(8,128)(2,1)} %gate.2.refs_1_), channel_id=1, source_target_pairs={{0,4},{4,0},{8,12},{12,8},{16,20},{20,16},{24,28},{28,24},{1,5},{5... | collective-permute-start | bytes 7077896 | tf_op jit(solution)/shard_map/ppermute | solution.py:439
  46.1 12.9 %all-to-all-start = ((bf16[8,192,256]{2,1,0:T(8,128)(2,1)}), bf16[8,192,256]{2,1,0:T(8,128)(2,1)S(1)}, u32[]{:S(2)}, u32[]{:S(2)}) async-start(bf16[8,192,256]{2,1,0:T(8,128)(2,1)} %bitcast.5), calls=%async_computation | async-start | bytes 1572864 | tf_op jit(solution)/shard_map/all_to_all | solution.py:492
  49.8 18.0 %collective-permute-start.6 = (bf16[272,384]{1,0:T(8,128)(2,1)S(1)}, bf16[272,384]{1,0:T(8,128)(2,1)S(1)}, u32[]{:S(2)}, u32[]{:S(2)}) collective-permute-start(bf16[272,384]{1,0:T(8,128)(2,1)S(1)} %copy-done.5), channel_id=1, source_target_pairs={{0,1},{1,2},{2,3},{3,0},{4,5},{5,6},{6,7},{7,4},{8,9},{9,10},{10,1... | collective-permute-start | bytes 626696 | tf_op jit(solution)/shard_map/ppermute | solution.py:437
  49.9 18.2 %collective-permute-start.7 = (bf16[272,384]{1,0:T(8,128)(2,1)S(1)}, bf16[272,384]{1,0:T(8,128)(2,1)S(1)}, u32[]{:S(2)}, u32[]{:S(2)}) collective-permute-start(bf16[272,384]{1,0:T(8,128)(2,1)S(1)} %copy-done.4), channel_id=1, source_target_pairs={{0,2},{1,3},{2,0},{3,1},{4,6},{5,7},{6,4},{7,5},{8,10},{9,11},{10,... | collective-permute-start | bytes 626696 | tf_op jit(solution)/shard_map/ppermute | solution.py:437
  52.1 19.0 %collective-permute-start.8 = (bf16[272,384]{1,0:T(8,128)(2,1)S(1)}, bf16[272,384]{1,0:T(8,128)(2,1)S(1)}, u32[]{:S(2)}, u32[]{:S(2)}) collective-permute-start(bf16[272,384]{1,0:T(8,128)(2,1)S(1)} %copy-done.3), channel_id=1, source_target_pairs={{0,3},{1,0},{2,1},{3,2},{4,7},{5,4},{6,5},{7,6},{8,11},{9,8},{10,9... | collective-permute-start | bytes 626696 | tf_op jit(solution)/shard_map/ppermute | solution.py:437
  63.3 35.3 %all-to-all-start.2 = ((bf16[4,192,1152]{2,1,0:T(8,128)(2,1)}), bf16[4,192,1152]{2,1,0:T(8,128)(2,1)S(1)}, u32[]{:S(2)}, u32[]{:S(2)}) async-start(bf16[4,192,1152]{2,1,0:T(8,128)(2,1)} %weight_share.1.refs_12_), calls=%async_computation.2 | async-start | bytes 3538944 | tf_op jit(solution)/shard_map/all_to_all | solution.py:499
  76.8 21.2 %copy-start = (bf16[64,1664]{1,0:T(8,128)(2,1)S(1)}, bf16[64,1664]{1,0:T(8,128)(2,1)}, u32[]{:S(2)}) copy-start(bf16[64,1664]{1,0:T(8,128)(2,1)} %get-tuple-element.71.refs_0_) | copy-start | bytes 638980
  76.8 3.0 %collective-permute-start.13 = (bf16[4,240,384]{2,1,0:T(8,128)(2,1)}, bf16[4,240,384]{2,1,0:T(8,128)(2,1)S(1)}, u32[]{:S(2)}, u32[]{:S(2)}) collective-permute-start(bf16[4,240,384]{2,1,0:T(8,128)(2,1)} %get-tuple-element.77), channel_id=1, source_target_pairs={{0,4},{4,0},{8,12},{12,8},{16,20},{20,16},{24,28},{28,24},{1,5},{5... | collective-permute-start | bytes 2211848 | tf_op jit(solution)/shard_map/ppermute | solution.py:439
  77.3 7.0 %collective-permute-start.10 = (bf16[64,1664]{1,0:T(8,128)(2,1)}, bf16[64,1664]{1,0:T(8,128)(2,1)S(1)}, u32[]{:S(2)}, u32[]{:S(2)}) collective-permute-start(bf16[64,1664]{1,0:T(8,128)(2,1)} %get-tuple-element.72), channel_id=1, source_target_pairs={{0,1},{1,2},{2,3},{3,0},{4,5},{5,6},{6,7},{7,4},{8,9},{9,10},{10,1... | collective-permute-start | bytes 638984 | tf_op jit(solution)/shard_map/ppermute | solution.py:437
  77.3 18.8 %collective-permute-start.11 = (bf16[64,1664]{1,0:T(8,128)(2,1)}, bf16[64,1664]{1,0:T(8,128)(2,1)S(1)}, u32[]{:S(2)}, u32[]{:S(2)}) collective-permute-start(bf16[64,1664]{1,0:T(8,128)(2,1)} %get-tuple-element.73), channel_id=1, source_target_pairs={{0,2},{1,3},{2,0},{3,1},{4,6},{5,7},{6,4},{7,5},{8,10},{9,11},{10,... | collective-permute-start | bytes 638984 | tf_op jit(solution)/shard_map/ppermute | solution.py:437
  78.3 19.7 %collective-permute-start.12 = (bf16[64,1664]{1,0:T(8,128)(2,1)}, bf16[64,1664]{1,0:T(8,128)(2,1)S(1)}, u32[]{:S(2)}, u32[]{:S(2)}) collective-permute-start(bf16[64,1664]{1,0:T(8,128)(2,1)} %get-tuple-element.74), channel_id=1, source_target_pairs={{0,3},{1,0},{2,1},{3,2},{4,7},{5,4},{6,5},{7,6},{8,11},{9,8},{10,9... | collective-permute-start | bytes 638984 | tf_op jit(solution)/shard_map/ppermute | solution.py:437
  81.3 17.0 %collective-permute-start.14 = (bf16[240,384]{1,0:T(8,128)(2,1)S(1)}, bf16[240,384]{1,0:T(8,128)(2,1)S(1)}, u32[]{:S(2)}, u32[]{:S(2)}) collective-permute-start(bf16[240,384]{1,0:T(8,128)(2,1)S(1)} %get-tuple-element.79), channel_id=1, source_target_pairs={{0,8},{4,12},{8,0},{12,4},{16,24},{20,28},{24,16},{28,20},{1,9},{5... | collective-permute-start | bytes 552968 | tf_op jit(solution)/shard_map/ppermute | solution.py:439
  83.1 15.3 %collective-permute-start.15 = (bf16[240,384]{1,0:T(8,128)(2,1)S(1)}, bf16[240,384]{1,0:T(8,128)(2,1)S(1)}, u32[]{:S(2)}, u32[]{:S(2)}) collective-permute-start(bf16[240,384]{1,0:T(8,128)(2,1)S(1)} %get-tuple-element.80), channel_id=1, source_target_pairs={{0,16},{4,20},{8,24},{12,28},{16,0},{20,4},{24,8},{28,12},{1,17},{... | collective-permute-start | bytes 552968 | tf_op jit(solution)/shard_map/ppermute | solution.py:439
  84.4 14.0 %collective-permute-start.16 = (bf16[240,384]{1,0:T(8,128)(2,1)S(1)}, bf16[240,384]{1,0:T(8,128)(2,1)S(1)}, u32[]{:S(2)}, u32[]{:S(2)}) collective-permute-start(bf16[240,384]{1,0:T(8,128)(2,1)S(1)} %get-tuple-element.81), channel_id=1, source_target_pairs={{0,24},{4,28},{8,16},{12,20},{16,8},{20,12},{24,0},{28,4},{1,25},{... | collective-permute-start | bytes 552968 | tf_op jit(solution)/shard_map/ppermute | solution.py:439
  98.6 3.9 %collective-permute-start.20 = (bf16[4,192,1152]{2,1,0:T(8,128)(2,1)S(1)}, bf16[4,192,1152]{2,1,0:T(8,128)(2,1)S(1)}, u32[]{:S(2)}, u32[]{:S(2)}) collective-permute-start(bf16[4,192,1152]{2,1,0:T(8,128)(2,1)S(1)} %gate.3.mine), channel_id=1, source_target_pairs={{0,4},{4,0},{8,12},{12,8},{16,20},{20,16},{24,28},{28,24},{1,5},{5... | collective-permute-start | bytes 5308424 | tf_op jit(solution)/shard_map/ppermute | solution.py:439
  99.2 6.8 %collective-permute-start.17 = (bf16[256,384]{1,0:T(8,128)(2,1)S(1)}, bf16[256,384]{1,0:T(8,128)(2,1)S(1)}, u32[]{:S(2)}, u32[]{:S(2)}) collective-permute-start(bf16[256,384]{1,0:T(8,128)(2,1)S(1)} %chip_sum.1.__1_.refs_0_), channel_id=1, source_target_pairs={{0,8},{4,12},{8,0},{12,4},{16,24},{20,28},{24,16},{28,20},{1,9},{5... | collective-permute-start | bytes 589832 | tf_op jit(solution)/shard_map/ppermute | solution.py:439
  100.8 9.2 %collective-permute-start.18 = (bf16[256,384]{1,0:T(8,128)(2,1)S(1)}, bf16[256,384]{1,0:T(8,128)(2,1)S(1)}, u32[]{:S(2)}, u32[]{:S(2)}) collective-permute-start(bf16[256,384]{1,0:T(8,128)(2,1)S(1)} %chip_sum.1.__1_.refs_0_), channel_id=1, source_target_pairs={{0,16},{4,20},{8,24},{12,28},{16,0},{20,4},{24,8},{28,12},{1,17},{... | collective-permute-start | bytes 589832 | tf_op jit(solution)/shard_map/ppermute | solution.py:439
  102.0 9.2 %collective-permute-start.19 = (bf16[256,384]{1,0:T(8,128)(2,1)S(1)}, bf16[256,384]{1,0:T(8,128)(2,1)S(1)}, u32[]{:S(2)}, u32[]{:S(2)}) collective-permute-start(bf16[256,384]{1,0:T(8,128)(2,1)S(1)} %chip_sum.1.__1_.refs_0_), channel_id=1, source_target_pairs={{0,24},{4,28},{8,16},{12,20},{16,8},{20,12},{24,0},{28,4},{1,25},{... | collective-permute-start | bytes 589832 | tf_op jit(solution)/shard_map/ppermute | solution.py:439
  111.4 3.0 %collective-permute-start.21 = (bf16[976,384]{1,0:T(8,128)(2,1)S(1)}, bf16[976,384]{1,0:T(8,128)(2,1)S(1)}, u32[]{:S(2)}, u32[]{:S(2)}) collective-permute-start(bf16[976,384]{1,0:T(8,128)(2,1)S(1)} %kernel_grad_half.1.refs_0_), channel_id=1, source_target_pairs={{0,4},{4,0},{8,12},{12,8},{16,20},{20,16},{24,28},{28,24},{1,5},{5... | collective-permute-start | bytes 2248712 | tf_op jit(solution)/shard_map/ppermute | solution.py:439

commit v7 on v6

--- a/solution.py
+++ b/solution.py
@@ -534,7 +534,7 @@
     )
     *split, keep_sum = call(
         functools.partial(split_kernel, chips),
-        [Far(keep), across(send, 1)],
+        [keep, across(send, 1)],
         free=[shaped((rows, wide), BF16)] * (chips - 1),
         kept=[shaped((rows, wide), F32)],
         name="core_sum",

time: 116 us -> 116 us (level)
  Pallas kernels: 24 us -> 22.6 us
  local copies, waits for them, and re-layouts: 4.4 us -> 5.78 us
    pallas_call x10, Pallas kernels: 22.2 us -> 20.8 us  [call(): pl.pallas_call(whole, out_shape=tuple([*memory(pltpu.HBM, outs), *free, *...]
    unnamed x12 -> x14, local copies, waits for them, and re-layouts: 0.02 us -> 1.4 us
  transfers between devices with their start and end apart: 25 -> 25, of which waited for: 16 -> 16; matrix products, arithmetic and copies ran while one was open for 3% -> 3% of each run, Pallas kernels for 20% -> 18%
where the time goes in v7:
time: 116 us
  waiting for transfers between devices  50.9 us (44%)
  starting transfers between devices  35.5 us (31%)
  Pallas kernels  22.6 us (19%)
  local copies, waits for them, and re-layouts  5.78 us (5%)
    ppermute x12, waiting for transfers between devices, body(): lax.ppermute(v, 'seq', [(i, (i + k) % n) for i in range(n)])  36.9 us
    pallas_call x10, Pallas kernels, call(): pl.pallas_call(whole, out_shape=tuple([*memory(pltpu.HBM, outs), *free, *...  20.8 us
    ppermute x12, starting transfers between devices, body(): lax.ppermute(v, 'seq', [(i, (i + k) % n) for i in range(n)])  11.7 us
    ppermute x10, starting transfers between devices, body(): across = lambda v, k: lax.ppermute(v, 'dp', [(i, i ^ k) for i in range(m)])  10.9 us
    ppermute x10, waiting for transfers between devices, body(): across = lambda v, k: lax.ppermute(v, 'dp', [(i, i ^ k) for i in range(m)])  8.52 us
    all_to_all x1, waiting for transfers between devices, body(): lax.all_to_all(nmt.reshape(m, width // m, half), 'dp', 0, 0, tiled=True)  5.49 us
    all_to_all x1, starting transfers between devices, body(): lax.all_to_all(cots, 'dp', 0, 0, axis_index_groups=same_core, tiled=True)  4.63 us
    all_to_all x1, starting transfers between devices, body(): lax.all_to_all(wshare, 'dp', 0, 0, axis_index_groups=same_core, tiled=True)  4.55 us
  transfers between devices with their start and end apart: 25, of which 16 were waited for; matrix products, arithmetic and copies ran while one was open for 3% of the time, Pallas kernels for 18%

profile of v7, /device:TPU:9, one launch (start us, length us, event | category | flops | bytes accessed | tf_op | source)
XLA Modules:
  0.0 115.7 jit_solution(12873595391167727246)
XLA Ops:
  1.6 1.3 %collective-permute-start = (bf16[64,1536]{1,0:T(8,128)(2,1)S(1)}, bf16[64,1536]{1,0:T(8,128)(2,1)S(1)}, u32[]{:S(2)}, u32[]{:S(2)}) collective-permute-start(bf16[64,1536]{1,0:T(8,128)(2,1)S(1)} %reshape_squeeze.3.refs_0_.refs_4_), channel_id=1, source_target_pairs={{0,1},{1,2},{2,3},{3,0},{4,5},{5,6},{6,7},{7,4},{8,9},{9,10},{10,1... | collective-permute-start | bytes 589832 | tf_op jit(solution)/shard_map/ppermute | solution.py:437
  4.1 1.4 %collective-permute-start.2 = (bf16[64,1536]{1,0:T(8,128)(2,1)S(1)}, bf16[64,1536]{1,0:T(8,128)(2,1)S(1)}, u32[]{:S(2)}, u32[]{:S(2)}) collective-permute-start(bf16[64,1536]{1,0:T(8,128)(2,1)S(1)} %reshape_squeeze.3.refs_0_.refs_4_), channel_id=1, source_target_pairs={{0,3},{1,0},{2,1},{3,2},{4,7},{5,4},{6,5},{7,6},{8,11},{9,8},{10,9... | collective-permute-start | bytes 589832 | tf_op jit(solution)/shard_map/ppermute | solution.py:437
  5.5 2.6 %broadcast_in_dim.9 = bf16[4,256,1152]{2,1,0:T(8,128)(2,1)} broadcast(bf16[256,1152]{1,0:T(8,128)(2,1)} %bitcast.11), dimensions={1,2} | broadcast | bytes 2949120 | tf_op jit(solution)/shard_map/broadcast_in_dim | solution.py:447
  8.1 4.6 %all-to-all-start.1 = ((bf16[4,256,1152]{2,1,0:T(8,128)(2,1)}), bf16[4,256,1152]{2,1,0:T(8,128)(2,1)}, u32[]{:S(2)}, u32[]{:S(2)}) async-start(bf16[4,256,1152]{2,1,0:T(8,128)(2,1)} %broadcast_in_dim.9), calls=%async_computation.1 | async-start | bytes 4718592 | tf_op jit(solution)/shard_map/all_to_all | solution.py:448
  12.8 3.8 %mid_parts.1 = (bf16[256,384]{1,0:T(8,128)(2,1)S(1)}, bf16[256,384]{1,0:T(8,128)(2,1)S(1)}, bf16[256,384]{1,0:T(8,128)(2,1)S(1)}, bf16[256,384]{1,0:T(8,128)(2,1...) custom-call(f32[768]{0:T(1024)S(1)} %copy-done.3, ...), custom_call_target="tpu_custom_call" | custom-call | flops 40000000000 | tf_op jit(solution)/shard_map/mid_parts/pallas_call | solution.py:90
  16.5 2.7 %collective-permute-done.1.refs_2_ = bf16[64,1536]{1,0:T(8,128)(2,1)S(1)} collective-permute-done((bf16[64,1536]{1,0:T(8,128)(2,1)S(1)}, bf16[64,1536]{1,0:T(8,128)(2,1)S(1)}, u32[]{:S(2)}, u32[]{:S(2)}) %collective-permute-start.1) | collective-permute-done | bytes 196640 | tf_op jit(solution)/shard_map/ppermute | solution.py:437
  19.2 2.9 %collective-permute-done.2.refs_3_ = bf16[64,1536]{1,0:T(8,128)(2,1)S(1)} collective-permute-done((bf16[64,1536]{1,0:T(8,128)(2,1)S(1)}, bf16[64,1536]{1,0:T(8,128)(2,1)S(1)}, u32[]{:S(2)}, u32[]{:S(2)}) %collective-permute-start.2) | collective-permute-done | bytes 196640 | tf_op jit(solution)/shard_map/ppermute | solution.py:437
  22.1 1.9 %conv_forward.1 = (bf16[256,384]{1,0:T(8,128)(2,1)S(1)}, f32[256,384]{1,0:T(8,128)S(1)}, f32[256,384]{1,0:T(8,128)S(1)}, bf16[256,1536]{1,0:T(8,128)(2,1)S(1)}, f32[256,2]{1,0:T(8,128)S(1)}) custom-call(bf16[64,1536]{1,0:T(8,128)(2,1)S(1)} %reshape_squeeze.3.refs_0_.refs_4_, bf16[64,1536]{1,0:T(8,128)(2,1)S(1)} %collective-permute-done.refs_1_, ...), custom_call_target="tpu_custom_call" | custom-call | tf_op jit(solution)/shard_map/conv_forward/pallas_call | solution.py:90
  24.4 1.4 %collective-permute-start.5 = (bf16[256,384]{1,0:T(8,128)(2,1)S(1)}, bf16[256,384]{1,0:T(8,128)(2,1)S(1)}, u32[]{:S(2)}, u32[]{:S(2)}) collective-permute-start(bf16[256,384]{1,0:T(8,128)(2,1)S(1)} %get-tuple-element.48.refs_0_), channel_id=1, source_target_pairs={{0,3},{1,0},{2,1},{3,2},{4,7},{5,4},{6,5},{7,6},{8,11},{9,8},{10,9... | collective-permute-start | bytes 589832 | tf_op jit(solution)/shard_map/ppermute | solution.py:437
  25.8 4.5 %collective-permute-done.3.refs_1_ = bf16[256,384]{1,0:T(8,128)(2,1)S(1)} collective-permute-done((bf16[256,384]{1,0:T(8,128)(2,1)S(1)}, bf16[256,384]{1,0:T(8,128)(2,1)S(1)}, u32[]{:S(2)}, u32[]{:S(2)}) %collective-permute-start.3) | collective-permute-done | bytes 196640 | tf_op jit(solution)/shard_map/ppermute | solution.py:437
  30.3 10.7 %collective-permute-done.4.refs_2_ = bf16[256,384]{1,0:T(8,128)(2,1)S(1)} collective-permute-done((bf16[256,384]{1,0:T(8,128)(2,1)S(1)}, bf16[256,384]{1,0:T(8,128)(2,1)S(1)}, u32[]{:S(2)}, u32[]{:S(2)}) %collective-permute-start.4) | collective-permute-done | bytes 196640 | tf_op jit(solution)/shard_map/ppermute | solution.py:437
  41.0 1.4 %collective-permute-done.5.refs_3_ = bf16[256,384]{1,0:T(8,128)(2,1)S(1)} collective-permute-done((bf16[256,384]{1,0:T(8,128)(2,1)S(1)}, bf16[256,384]{1,0:T(8,128)(2,1)S(1)}, u32[]{:S(2)}, u32[]{:S(2)}) %collective-permute-start.5) | collective-permute-done | bytes 196640 | tf_op jit(solution)/shard_map/ppermute | solution.py:437
  42.4 3.1 %qkv.1 = (bf16[1536,256]{1,0:T(8,128)(2,1)}, f32[256,1]{1,0:T(8,128)}, bf16[256,1152]{1,0:T(8,128)(2,1)}, f32[8,256]{1,0:T(8,128)}, bf16[272,384]{1,0:T(8,128)(2...) custom-call(bf16[256,384]{1,0:T(8,128)(2,1)S(1)} %get-tuple-element., ...), custom_call_target="tpu_custom_call" | custom-call | tf_op jit(solution)/shard_map/qkv/pallas_call | solution.py:90
  46.1 3.8 %all-to-all-start = ((bf16[8,192,256]{2,1,0:T(8,128)(2,1)}), bf16[8,192,256]{2,1,0:T(8,128)(2,1)S(1)}, u32[]{:S(2)}, u32[]{:S(2)}) async-start(bf16[8,192,256]{2,1,0:T(8,128)(2,1)} %bitcast.5), calls=%async_computation | async-start | bytes 1572864 | tf_op jit(solution)/shard_map/all_to_all | solution.py:492
  49.9 2.2 %collective-permute-start.7 = (bf16[272,384]{1,0:T(8,128)(2,1)S(1)}, bf16[272,384]{1,0:T(8,128)(2,1)S(1)}, u32[]{:S(2)}, u32[]{:S(2)}) collective-permute-start(bf16[272,384]{1,0:T(8,128)(2,1)S(1)} %copy-done.5), channel_id=1, source_target_pairs={{0,2},{1,3},{2,0},{3,1},{4,6},{5,7},{6,4},{7,5},{8,10},{9,11},{10,... | collective-permute-start | bytes 626696 | tf_op jit(solution)/shard_map/ppermute | solution.py:437
  52.1 1.4 %collective-permute-start.8 = (bf16[272,384]{1,0:T(8,128)(2,1)S(1)}, bf16[272,384]{1,0:T(8,128)(2,1)S(1)}, u32[]{:S(2)}, u32[]{:S(2)}) collective-permute-start(bf16[272,384]{1,0:T(8,128)(2,1)S(1)} %copy-done.4), channel_id=1, source_target_pairs={{0,3},{1,0},{2,1},{3,2},{4,7},{5,4},{6,5},{7,6},{8,11},{9,8},{10,9... | collective-permute-start | bytes 626696 | tf_op jit(solution)/shard_map/ppermute | solution.py:437
  53.5 5.5 %all-to-all-done.refs_0_ = bf16[8,192,256]{2,1,0:T(8,128)(2,1)S(1)} async-done(((bf16[8,192,256]{2,1,0:T(8,128)(2,1)}), bf16[8,192,256]{2,1,0:T(8,128)(2,1)S(1)}, u32[]{:S(2)}, u32[]{:S(2)}) %all-to-all-start) | async-done | bytes 786464 | tf_op jit(solution)/shard_map/all_to_all | solution.py:492
  59.0 4.3 %weight_share.1.refs_12_ = bf16[4,192,1152]{2,1,0:T(8,128)(2,1)} custom-call(bf16[8,192,256]{2,1,0:T(8,128)(2,1)S(1)} %all-to-all-done.refs_0_, bf16[4,256,1152]{2,1,0:T(8,128)(2,1)} %gate.2.refs_1_, bf16[4,256,1152]{2,1,0:T(8,128)(2,1)} %collective-permute-done.9.refs_2_), custom_call_target="tpu_custom_call" | custom-call | tf_op jit(solution)/shard_map/weight_share/pallas_call | solution.py:90
  63.3 4.5 %all-to-all-start.2 = ((bf16[4,192,1152]{2,1,0:T(8,128)(2,1)}), bf16[4,192,1152]{2,1,0:T(8,128)(2,1)S(1)}, u32[]{:S(2)}, u32[]{:S(2)}) async-start(bf16[4,192,1152]{2,1,0:T(8,128)(2,1)} %weight_share.1.refs_12_), calls=%async_computation.2 | async-start | bytes 3538944 | tf_op jit(solution)/shard_map/all_to_all | solution.py:499
  68.0 3.1 %collective-permute-done.8.refs_3_ = bf16[272,384]{1,0:T(8,128)(2,1)S(1)} collective-permute-done((bf16[272,384]{1,0:T(8,128)(2,1)S(1)}, bf16[272,384]{1,0:T(8,128)(2,1)S(1)}, u32[]{:S(2)}, u32[]{:S(2)}) %collective-permute-start.8) | collective-permute-done | bytes 208928 | tf_op jit(solution)/shard_map/ppermute | solution.py:437
  71.1 5.7 %conv_backward.1 = (bf16[4,240,384]{2,1,0:T(8,128)(2,1)}, f32[4,240,384]{2,1,0:T(8,128)}, bf16[64,1664]{1,0:T(8,128)(2,1)}, bf16[64,1664]{1,0:T(8,128)(2,1)}, bf...) custom-call(bf16[272,384]{1,0:T(8,128)(2,1)} %get-tuple-element.61.refs_0_, ...), custom_call_target="tpu_custom_call" | custom-call | flops 40000000000 | tf_op jit(solution)/shard_map/conv_backward/pallas_call | solution.py:90
  78.3 1.5 %collective-permute-start.12 = (bf16[64,1664]{1,0:T(8,128)(2,1)}, bf16[64,1664]{1,0:T(8,128)(2,1)S(1)}, u32[]{:S(2)}, u32[]{:S(2)}) collective-permute-start(bf16[64,1664]{1,0:T(8,128)(2,1)} %get-tuple-element.74), channel_id=1, source_target_pairs={{0,3},{1,0},{2,1},{3,2},{4,7},{5,4},{6,5},{7,6},{8,11},{9,8},{10,9... | collective-permute-start | bytes 638984 | tf_op jit(solution)/shard_map/ppermute | solution.py:437
  79.8 1.4 %copy-done = f32[4,240,384]{2,1,0:T(8,128)S(1)} copy-done((f32[4,240,384]{2,1,0:T(8,128)S(1)}, f32[4,240,384]{2,1,0:T(8,128)}, u32[]{:S(2)}) %copy-start) | copy-done | bytes 1474584
  81.3 1.8 %collective-permute-start.14 = (bf16[240,384]{1,0:T(8,128)(2,1)S(1)}, bf16[240,384]{1,0:T(8,128)(2,1)S(1)}, u32[]{:S(2)}, u32[]{:S(2)}) collective-permute-start(bf16[240,384]{1,0:T(8,128)(2,1)S(1)} %get-tuple-element.79), channel_id=1, source_target_pairs={{0,8},{4,12},{8,0},{12,4},{16,24},{20,28},{24,16},{28,20},{1,9},{5... | collective-permute-start | bytes 552968 | tf_op jit(solution)/shard_map/ppermute | solution.py:439
  84.4 2.3 %collective-permute-start.16 = (bf16[240,384]{1,0:T(8,128)(2,1)S(1)}, bf16[240,384]{1,0:T(8,128)(2,1)S(1)}, u32[]{:S(2)}, u32[]{:S(2)}) collective-permute-start(bf16[240,384]{1,0:T(8,128)(2,1)S(1)} %get-tuple-element.81), channel_id=1, source_target_pairs={{0,24},{4,28},{8,16},{12,20},{16,8},{20,12},{24,0},{28,4},{1,25},{... | collective-permute-start | bytes 552968 | tf_op jit(solution)/shard_map/ppermute | solution.py:439
  86.6 9.5 %collective-permute-done.11.refs_2_ = bf16[64,1664]{1,0:T(8,128)(2,1)S(1)} collective-permute-done((bf16[64,1664]{1,0:T(8,128)(2,1)}, bf16[64,1664]{1,0:T(8,128)(2,1)S(1)}, u32[]{:S(2)}, u32[]{:S(2)}) %collective-permute-start.11) | collective-permute-done | bytes 213024 | tf_op jit(solution)/shard_map/ppermute | solution.py:437
  96.2 1.8 %collective-permute-done.12.refs_3_ = bf16[64,1664]{1,0:T(8,128)(2,1)S(1)} collective-permute-done((bf16[64,1664]{1,0:T(8,128)(2,1)}, bf16[64,1664]{1,0:T(8,128)(2,1)S(1)}, u32[]{:S(2)}, u32[]{:S(2)}) %collective-permute-start.12) | collective-permute-done | bytes 213024 | tf_op jit(solution)/shard_map/ppermute | solution.py:437
  99.2 1.6 %collective-permute-start.17 = (bf16[256,384]{1,0:T(8,128)(2,1)S(1)}, bf16[256,384]{1,0:T(8,128)(2,1)S(1)}, u32[]{:S(2)}, u32[]{:S(2)}) collective-permute-start(bf16[256,384]{1,0:T(8,128)(2,1)S(1)} %chip_sum.1.__1_.refs_0_), channel_id=1, source_target_pairs={{0,8},{4,12},{8,0},{12,4},{16,24},{20,28},{24,16},{28,20},{1,9},{5... | collective-permute-start | bytes 589832 | tf_op jit(solution)/shard_map/ppermute | solution.py:439
  102.5 1.8 %weight_grad.1.refs_4_ = bf16[4,2,192,1152]{3,2,1,0:T(8,128)(2,1)} custom-call(bf16[4,192,1152]{2,1,0:T(8,128)(2,1)S(1)} %gate.3.mine, bf16[4,192,1152]{2,1,0:T(8,128)(2,1)S(1)} %collective-permute-done.20.other), custom_call_target="tpu_custom_call" | custom-call | tf_op jit(solution)/shard_map/weight_grad/pallas_call | solution.py:551
  104.3 1.6 %collective-permute-done.17.refs_1_ = bf16[256,384]{1,0:T(8,128)(2,1)S(1)} collective-permute-done((bf16[256,384]{1,0:T(8,128)(2,1)S(1)}, bf16[256,384]{1,0:T(8,128)(2,1)S(1)}, u32[]{:S(2)}, u32[]{:S(2)}) %collective-permute-start.17) | collective-permute-done | bytes 196640 | tf_op jit(solution)/shard_map/ppermute | solution.py:439
  105.9 4.1 %collective-permute-done.18.refs_2_ = bf16[256,384]{1,0:T(8,128)(2,1)S(1)} collective-permute-done((bf16[256,384]{1,0:T(8,128)(2,1)S(1)}, bf16[256,384]{1,0:T(8,128)(2,1)S(1)}, u32[]{:S(2)}, u32[]{:S(2)}) %collective-permute-start.18) | collective-permute-done | bytes 196640 | tf_op jit(solution)/shard_map/ppermute | solution.py:439
  114.4 1.3 %kernel_grad.1 = (bf16[960,768]{1,0:T(8,128)(2,1)}, f32[768]{0:T(1024)}, f32[1536]{0:T(1024)}) custom-call(bf16[976,384]{1,0:T(8,128)(2,1)S(1)} %kernel_grad_half.1.refs_0_, bf16[976,384]{1,0:T(8,128)(2,1)S(1)} %collective-permute-done.21.refs_1_), custom_call_target="tpu_custom_call" | custom-call | tf_op jit(solution)/shard_map/kernel_grad/pallas_call | solution.py:90
  (48 shorter events, 13.4 us)
Async XLA Ops:
  1.6 14.9 %collective-permute-start = (bf16[64,1536]{1,0:T(8,128)(2,1)S(1)}, bf16[64,1536]{1,0:T(8,128)(2,1)S(1)}, u32[]{:S(2)}, u32[]{:S(2)}) collective-permute-start(bf16[64,1536]{1,0:T(8,128)(2,1)S(1)} %reshape_squeeze.3.refs_0_.refs_4_), channel_id=1, source_target_pairs={{0,1},{1,2},{2,3},{3,0},{4,5},{5,6},{6,7},{7,4},{8,9},{9,10},{10,1... | collective-permute-start | bytes 589832 | tf_op jit(solution)/shard_map/ppermute | solution.py:437
  3.0 16.2 %collective-permute-start.1 = (bf16[64,1536]{1,0:T(8,128)(2,1)S(1)}, bf16[64,1536]{1,0:T(8,128)(2,1)S(1)}, u32[]{:S(2)}, u32[]{:S(2)}) collective-permute-start(bf16[64,1536]{1,0:T(8,128)(2,1)S(1)} %reshape_squeeze.3.refs_0_.refs_4_), channel_id=1, source_target_pairs={{0,2},{1,3},{2,0},{3,1},{4,6},{5,7},{6,4},{7,5},{8,10},{9,11},{10,... | collective-permute-start | bytes 589832 | tf_op jit(solution)/shard_map/ppermute | solution.py:437
  4.1 18.1 %collective-permute-start.2 = (bf16[64,1536]{1,0:T(8,128)(2,1)S(1)}, bf16[64,1536]{1,0:T(8,128)(2,1)S(1)}, u32[]{:S(2)}, u32[]{:S(2)}) collective-permute-start(bf16[64,1536]{1,0:T(8,128)(2,1)S(1)} %reshape_squeeze.3.refs_0_.refs_4_), channel_id=1, source_target_pairs={{0,3},{1,0},{2,1},{3,2},{4,7},{5,4},{6,5},{7,6},{8,11},{9,8},{10,9... | collective-permute-start | bytes 589832 | tf_op jit(solution)/shard_map/ppermute | solution.py:437
  8.1 4.6 %copy-start.2 = (f32[1536]{0:T(1024)S(1)}, f32[1536]{0:T(1024)}, u32[]{:S(2)}) copy-start(f32[1536]{0:T(1024)} %refs_1_.1) | copy-start | bytes 18436
  8.1 4.6 %copy-start.3 = (f32[768]{0:T(1024)S(1)}, f32[768]{0:T(1024)}, u32[]{:S(2)}) copy-start(f32[768]{0:T(1024)} %refs_0_.1) | copy-start | bytes 9220
  8.1 37.4 %all-to-all-start.1 = ((bf16[4,256,1152]{2,1,0:T(8,128)(2,1)}), bf16[4,256,1152]{2,1,0:T(8,128)(2,1)}, u32[]{:S(2)}, u32[]{:S(2)}) async-start(bf16[4,256,1152]{2,1,0:T(8,128)(2,1)} %broadcast_in_dim.9), calls=%async_computation.1 | async-start | bytes 4718592 | tf_op jit(solution)/shard_map/all_to_all | solution.py:448
  24.0 6.3 %collective-permute-start.3 = (bf16[256,384]{1,0:T(8,128)(2,1)S(1)}, bf16[256,384]{1,0:T(8,128)(2,1)S(1)}, u32[]{:S(2)}, u32[]{:S(2)}) collective-permute-start(bf16[256,384]{1,0:T(8,128)(2,1)S(1)} %get-tuple-element.48.refs_0_), channel_id=1, source_target_pairs={{0,1},{1,2},{2,3},{3,0},{4,5},{5,6},{6,7},{7,4},{8,9},{9,10},{10,1... | collective-permute-start | bytes 589832 | tf_op jit(solution)/shard_map/ppermute | solution.py:437
  24.1 16.9 %collective-permute-start.4 = (bf16[256,384]{1,0:T(8,128)(2,1)S(1)}, bf16[256,384]{1,0:T(8,128)(2,1)S(1)}, u32[]{:S(2)}, u32[]{:S(2)}) collective-permute-start(bf16[256,384]{1,0:T(8,128)(2,1)S(1)} %get-tuple-element.48.refs_0_), channel_id=1, source_target_pairs={{0,2},{1,3},{2,0},{3,1},{4,6},{5,7},{6,4},{7,5},{8,10},{9,11},{10,... | collective-permute-start | bytes 589832 | tf_op jit(solution)/shard_map/ppermute | solution.py:437
  24.4 17.9 %collective-permute-start.5 = (bf16[256,384]{1,0:T(8,128)(2,1)S(1)}, bf16[256,384]{1,0:T(8,128)(2,1)S(1)}, u32[]{:S(2)}, u32[]{:S(2)}) collective-permute-start(bf16[256,384]{1,0:T(8,128)(2,1)S(1)} %get-tuple-element.48.refs_0_), channel_id=1, source_target_pairs={{0,3},{1,0},{2,1},{3,2},{4,7},{5,4},{6,5},{7,6},{8,11},{9,8},{10,9... | collective-permute-start | bytes 589832 | tf_op jit(solution)/shard_map/ppermute | solution.py:437
  45.5 4.4 %copy-start.6 = (bf16[272,384]{1,0:T(8,128)(2,1)S(1)}, bf16[272,384]{1,0:T(8,128)(2,1)}, u32[]{:S(2)}) copy-start(bf16[272,384]{1,0:T(8,128)(2,1)} %get-tuple-element.62) | copy-start | bytes 626692
  45.5 4.4 %copy-start.5 = (bf16[272,384]{1,0:T(8,128)(2,1)S(1)}, bf16[272,384]{1,0:T(8,128)(2,1)}, u32[]{:S(2)}) copy-start(bf16[272,384]{1,0:T(8,128)(2,1)} %get-tuple-element.63) | copy-start | bytes 626692
  45.5 6.6 %copy-start.4 = (bf16[272,384]{1,0:T(8,128)(2,1)S(1)}, bf16[272,384]{1,0:T(8,128)(2,1)}, u32[]{:S(2)}) copy-start(bf16[272,384]{1,0:T(8,128)(2,1)} %get-tuple-element.64) | copy-start | bytes 626692
  45.5 13.5 %collective-permute-start.9 = (bf16[4,256,1152]{2,1,0:T(8,128)(2,1)}, bf16[4,256,1152]{2,1,0:T(8,128)(2,1)}, u32[]{:S(2)}, u32[]{:S(2)}) collective-permute-start(bf16[4,256,1152]{2,1,0:T(8,128)(2,1)} %gate.2.refs_1_), channel_id=1, source_target_pairs={{0,4},{4,0},{8,12},{12,8},{16,20},{20,16},{24,28},{28,24},{1,5},{5... | collective-permute-start | bytes 7077896 | tf_op jit(solution)/shard_map/ppermute | solution.py:439
  46.1 12.9 %all-to-all-start = ((bf16[8,192,256]{2,1,0:T(8,128)(2,1)}), bf16[8,192,256]{2,1,0:T(8,128)(2,1)S(1)}, u32[]{:S(2)}, u32[]{:S(2)}) async-start(bf16[8,192,256]{2,1,0:T(8,128)(2,1)} %bitcast.5), calls=%async_computation | async-start | bytes 1572864 | tf_op jit(solution)/shard_map/all_to_all | solution.py:492
  49.8 18.0 %collective-permute-start.6 = (bf16[272,384]{1,0:T(8,128)(2,1)S(1)}, bf16[272,384]{1,0:T(8,128)(2,1)S(1)}, u32[]{:S(2)}, u32[]{:S(2)}) collective-permute-start(bf16[272,384]{1,0:T(8,128)(2,1)S(1)} %copy-done.6), channel_id=1, source_target_pairs={{0,1},{1,2},{2,3},{3,0},{4,5},{5,6},{6,7},{7,4},{8,9},{9,10},{10,1... | collective-permute-start | bytes 626696 | tf_op jit(solution)/shard_map/ppermute | solution.py:437
  49.9 18.2 %collective-permute-start.7 = (bf16[272,384]{1,0:T(8,128)(2,1)S(1)}, bf16[272,384]{1,0:T(8,128)(2,1)S(1)}, u32[]{:S(2)}, u32[]{:S(2)}) collective-permute-start(bf16[272,384]{1,0:T(8,128)(2,1)S(1)} %copy-done.5), channel_id=1, source_target_pairs={{0,2},{1,3},{2,0},{3,1},{4,6},{5,7},{6,4},{7,5},{8,10},{9,11},{10,... | collective-permute-start | bytes 626696 | tf_op jit(solution)/shard_map/ppermute | solution.py:437
  52.1 19.0 %collective-permute-start.8 = (bf16[272,384]{1,0:T(8,128)(2,1)S(1)}, bf16[272,384]{1,0:T(8,128)(2,1)S(1)}, u32[]{:S(2)}, u32[]{:S(2)}) collective-permute-start(bf16[272,384]{1,0:T(8,128)(2,1)S(1)} %copy-done.4), channel_id=1, source_target_pairs={{0,3},{1,0},{2,1},{3,2},{4,7},{5,4},{6,5},{7,6},{8,11},{9,8},{10,9... | collective-permute-start | bytes 626696 | tf_op jit(solution)/shard_map/ppermute | solution.py:437
  63.3 35.3 %all-to-all-start.2 = ((bf16[4,192,1152]{2,1,0:T(8,128)(2,1)}), bf16[4,192,1152]{2,1,0:T(8,128)(2,1)S(1)}, u32[]{:S(2)}, u32[]{:S(2)}) async-start(bf16[4,192,1152]{2,1,0:T(8,128)(2,1)} %weight_share.1.refs_12_), calls=%async_computation.2 | async-start | bytes 3538944 | tf_op jit(solution)/shard_map/all_to_all | solution.py:499
  76.8 3.0 %collective-permute-start.13 = (bf16[4,240,384]{2,1,0:T(8,128)(2,1)}, bf16[4,240,384]{2,1,0:T(8,128)(2,1)S(1)}, u32[]{:S(2)}, u32[]{:S(2)}) collective-permute-start(bf16[4,240,384]{2,1,0:T(8,128)(2,1)} %get-tuple-element.77), channel_id=1, source_target_pairs={{0,4},{4,0},{8,12},{12,8},{16,20},{20,16},{24,28},{28,24},{1,5},{5... | collective-permute-start | bytes 2211848 | tf_op jit(solution)/shard_map/ppermute | solution.py:439
  77.3 7.0 %collective-permute-start.10 = (bf16[64,1664]{1,0:T(8,128)(2,1)}, bf16[64,1664]{1,0:T(8,128)(2,1)S(1)}, u32[]{:S(2)}, u32[]{:S(2)}) collective-permute-start(bf16[64,1664]{1,0:T(8,128)(2,1)} %get-tuple-element.72), channel_id=1, source_target_pairs={{0,1},{1,2},{2,3},{3,0},{4,5},{5,6},{6,7},{7,4},{8,9},{9,10},{10,1... | collective-permute-start | bytes 638984 | tf_op jit(solution)/shard_map/ppermute | solution.py:437
  77.3 18.8 %collective-permute-start.11 = (bf16[64,1664]{1,0:T(8,128)(2,1)}, bf16[64,1664]{1,0:T(8,128)(2,1)S(1)}, u32[]{:S(2)}, u32[]{:S(2)}) collective-permute-start(bf16[64,1664]{1,0:T(8,128)(2,1)} %get-tuple-element.73), channel_id=1, source_target_pairs={{0,2},{1,3},{2,0},{3,1},{4,6},{5,7},{6,4},{7,5},{8,10},{9,11},{10,... | collective-permute-start | bytes 638984 | tf_op jit(solution)/shard_map/ppermute | solution.py:437
  78.3 19.7 %collective-permute-start.12 = (bf16[64,1664]{1,0:T(8,128)(2,1)}, bf16[64,1664]{1,0:T(8,128)(2,1)S(1)}, u32[]{:S(2)}, u32[]{:S(2)}) collective-permute-start(bf16[64,1664]{1,0:T(8,128)(2,1)} %get-tuple-element.74), channel_id=1, source_target_pairs={{0,3},{1,0},{2,1},{3,2},{4,7},{5,4},{6,5},{7,6},{8,11},{9,8},{10,9... | collective-permute-start | bytes 638984 | tf_op jit(solution)/shard_map/ppermute | solution.py:437
  79.8 1.4 %copy-start = (f32[4,240,384]{2,1,0:T(8,128)S(1)}, f32[4,240,384]{2,1,0:T(8,128)}, u32[]{:S(2)}) copy-start(f32[4,240,384]{2,1,0:T(8,128)} %get-tuple-element.76.refs_0_) | copy-start | bytes 4423684
  81.1 16.8 %copy-start.1 = (bf16[64,1664]{1,0:T(8,128)(2,1)S(1)}, bf16[64,1664]{1,0:T(8,128)(2,1)}, u32[]{:S(2)}) copy-start(bf16[64,1664]{1,0:T(8,128)(2,1)} %get-tuple-element.71.refs_0_) | copy-start | bytes 638980
  81.3 17.0 %collective-permute-start.14 = (bf16[240,384]{1,0:T(8,128)(2,1)S(1)}, bf16[240,384]{1,0:T(8,128)(2,1)S(1)}, u32[]{:S(2)}, u32[]{:S(2)}) collective-permute-start(bf16[240,384]{1,0:T(8,128)(2,1)S(1)} %get-tuple-element.79), channel_id=1, source_target_pairs={{0,8},{4,12},{8,0},{12,4},{16,24},{20,28},{24,16},{28,20},{1,9},{5... | collective-permute-start | bytes 552968 | tf_op jit(solution)/shard_map/ppermute | solution.py:439
  83.1 15.3 %collective-permute-start.15 = (bf16[240,384]{1,0:T(8,128)(2,1)S(1)}, bf16[240,384]{1,0:T(8,128)(2,1)S(1)}, u32[]{:S(2)}, u32[]{:S(2)}) collective-permute-start(bf16[240,384]{1,0:T(8,128)(2,1)S(1)} %get-tuple-element.80), channel_id=1, source_target_pairs={{0,16},{4,20},{8,24},{12,28},{16,0},{20,4},{24,8},{28,12},{1,17},{... | collective-permute-start | bytes 552968 | tf_op jit(solution)/shard_map/ppermute | solution.py:439
  84.4 14.0 %collective-permute-start.16 = (bf16[240,384]{1,0:T(8,128)(2,1)S(1)}, bf16[240,384]{1,0:T(8,128)(2,1)S(1)}, u32[]{:S(2)}, u32[]{:S(2)}) collective-permute-start(bf16[240,384]{1,0:T(8,128)(2,1)S(1)} %get-tuple-element.81), channel_id=1, source_target_pairs={{0,24},{4,28},{8,16},{12,20},{16,8},{20,12},{24,0},{28,4},{1,25},{... | collective-permute-start | bytes 552968 | tf_op jit(solution)/shard_map/ppermute | solution.py:439
  98.6 3.9 %collective-permute-start.20 = (bf16[4,192,1152]{2,1,0:T(8,128)(2,1)S(1)}, bf16[4,192,1152]{2,1,0:T(8,128)(2,1)S(1)}, u32[]{:S(2)}, u32[]{:S(2)}) collective-permute-start(bf16[4,192,1152]{2,1,0:T(8,128)(2,1)S(1)} %gate.3.mine), channel_id=1, source_target_pairs={{0,4},{4,0},{8,12},{12,8},{16,20},{20,16},{24,28},{28,24},{1,5},{5... | collective-permute-start | bytes 5308424 | tf_op jit(solution)/shard_map/ppermute | solution.py:439
  99.2 6.8 %collective-permute-start.17 = (bf16[256,384]{1,0:T(8,128)(2,1)S(1)}, bf16[256,384]{1,0:T(8,128)(2,1)S(1)}, u32[]{:S(2)}, u32[]{:S(2)}) collective-permute-start(bf16[256,384]{1,0:T(8,128)(2,1)S(1)} %chip_sum.1.__1_.refs_0_), channel_id=1, source_target_pairs={{0,8},{4,12},{8,0},{12,4},{16,24},{20,28},{24,16},{28,20},{1,9},{5... | collective-permute-start | bytes 589832 | tf_op jit(solution)/shard_map/ppermute | solution.py:439
  100.8 9.2 %collective-permute-start.18 = (bf16[256,384]{1,0:T(8,128)(2,1)S(1)}, bf16[256,384]{1,0:T(8,128)(2,1)S(1)}, u32[]{:S(2)}, u32[]{:S(2)}) collective-permute-start(bf16[256,384]{1,0:T(8,128)(2,1)S(1)} %chip_sum.1.__1_.refs_0_), channel_id=1, source_target_pairs={{0,16},{4,20},{8,24},{12,28},{16,0},{20,4},{24,8},{28,12},{1,17},{... | collective-permute-start | bytes 589832 | tf_op jit(solution)/shard_map/ppermute | solution.py:439
  102.0 9.2 %collective-permute-start.19 = (bf16[256,384]{1,0:T(8,128)(2,1)S(1)}, bf16[256,384]{1,0:T(8,128)(2,1)S(1)}, u32[]{:S(2)}, u32[]{:S(2)}) collective-permute-start(bf16[256,384]{1,0:T(8,128)(2,1)S(1)} %chip_sum.1.__1_.refs_0_), channel_id=1, source_target_pairs={{0,24},{4,28},{8,16},{12,20},{16,8},{20,12},{24,0},{28,4},{1,25},{... | collective-permute-start | bytes 589832 | tf_op jit(solution)/shard_map/ppermute | solution.py:439
  111.4 3.0 %collective-permute-start.21 = (bf16[976,384]{1,0:T(8,128)(2,1)S(1)}, bf16[976,384]{1,0:T(8,128)(2,1)S(1)}, u32[]{:S(2)}, u32[]{:S(2)}) collective-permute-start(bf16[976,384]{1,0:T(8,128)(2,1)S(1)} %kernel_grad_half.1.refs_0_), channel_id=1, source_target_pairs={{0,4},{4,0},{8,12},{12,8},{16,20},{20,16},{24,28},{28,24},{1,5},{5... | collective-permute-start | bytes 2248712 | tf_op jit(solution)/shard_map/ppermute | solution.py:439
